TPU v7x, 32 devices: a whole 2x2x4 slice. The times are simulated.
32 devices in a mesh: dp: 4 (over z), row: 4 (over y, x), col: 2 (over core).
Axes of the slice: x: 2, y: 2, z: 4, core: 2. Of those that a mesh axis runs over, the one named last changes fastest.
Arguments:
- tokens: bfloat16 [6304, 512], P(('dp', 'row'), 'col'), may hold values from -6 to 6
- norm_gain: float32 [2, 2, 512], P(None, None, 'col'), may hold values from 0.5 to 1.5
- norm_shift: float32 [2, 2, 512], P(None, None, 'col'), may hold values from -3 to 3
- w_qkv: bfloat16 [2, 512, 3, 512], P(None, 'col', None, 'row'), may hold values from -0.25 to 0.25
- w_proj: bfloat16 [2, 512, 512], P(None, 'row', 'col'), may hold values from -0.75 to 0.75
- w_router: bfloat16 [2, 512, 32], P(None, 'col'), may hold values from -0.25 to 0.25
- w_in: bfloat16 [2, 32, 512, 2048], P(None, None, 'col', 'row'), may hold values from -0.25 to 0.25
- w_out: bfloat16 [2, 32, 2048, 512], P(None, None, 'row', 'col'), may hold values from -2 to 2
- expert_ids: int32 [2, 6304, 2], P(None, 'dp'), may hold values from 0 to 31, as said below
- slot_ids: int32 [2, 6304, 2], P(None, 'dp'), may hold values from 0 to 123, as said below
- cotangent: bfloat16 [6304, 512], P(('dp', 'row'), 'col'), may hold values from -6 to 6
Outputs:
- output: bfloat16 [6304, 512], P(('dp', 'row'), 'col')
- grad_input: float32 [6304, 512], P(('dp', 'row'), 'col')
- grad_qkv: float32 [2, 512, 3, 512], P(None, 'col', None, 'row')
- grad_proj: float32 [2, 512, 512], P(None, 'row', 'col')
- grad_router: float32 [2, 512, 32], P(None, 'col')
- grad_in: float32 [2, 32, 512, 2048], P(None, 'dp', 'col', 'row')
- grad_out: float32 [2, 32, 2048, 512], P(None, 'dp', 'row', 'col')
- grad_gain: float32 [2, 2, 512], P(None, None, 'col')
- grad_shift: float32 [2, 2, 512], P(None, None, 'col')
Inputs may be any that keep to these rules, and one draw needn't show every extreme that they name: `expert_ids`: in each layer and each group of 1576 consecutive tokens, a token's two experts differ, no expert is named by more than 124 tokens, and some expert is named by exactly 124 tokens. `slot_ids`: in each layer, group and expert, the tokens that name the expert have different slots.
All inputs are finite; a program needn't handle non-finite values.
Results may differ from a plain program's by a relative error of at most 0.015.
Values may be sent and summed in bfloat16 or wider, within the bound.
No kernel may reach another device: no remote copies, remote signals or barrier semaphores. Data moves between devices by JAX's collectives and lax.ppermute only.
A program may use at most 256 MiB of HBM per device.

v0:
```python
import jax
import jax.numpy as jnp
from jax import lax
from jax.sharding import PartitionSpec as P

HDIM = 64
SEQ = 197


EPSILON = 1e-06


def gather_rows(values):
    return lax.all_gather(values, "row", axis=0, tiled=True)


def sum_rows(values):
    return lax.psum_scatter(values, "row", scatter_dimension=0, tiled=True)


def gather_halves(values):
    return lax.all_gather(values, "col", axis=0, tiled=True)


def sum_halves(values):
    return lax.psum_scatter(values, "col", scatter_dimension=0, tiled=True)


def row_totals(first, second):
    return lax.psum((first, second), "col")


def softmax_rows(values):
    shifted = jnp.exp(values - jnp.max(values, axis=-1, keepdims=True))
    return shifted / jnp.sum(shifted, axis=-1, keepdims=True)


def norm_forward(stream, gain_row, shift_row):
    feature_count = stream.shape[1] * lax.axis_size("col")
    total, squares = row_totals(jnp.sum(stream, axis=1), jnp.sum(stream * stream, axis=1))
    center = total / feature_count
    inverse = lax.rsqrt(squares / feature_count - center * center + EPSILON)
    normal = (stream - center[:, None]) * inverse[:, None]
    return (normal * gain_row + shift_row, normal, inverse)


def norm_backward(upstream, normal, inverse, gain_row):
    feature_count = upstream.shape[1] * lax.axis_size("col")
    scaled = upstream * gain_row
    first, second = row_totals(jnp.sum(scaled, axis=1), jnp.sum(scaled * normal, axis=1))
    result_grad = inverse[:, None] * (
        scaled - first[:, None] / feature_count - normal * (second[:, None] / feature_count)
    )
    return (result_grad, jnp.sum(upstream * normal, axis=0), jnp.sum(upstream, axis=0))


def split_heads(packed):
    row_count = packed.shape[0]
    heads_here = packed.shape[1] // (3 * HDIM)
    parts = packed.reshape(row_count // SEQ, SEQ, 3, heads_here, HDIM)
    return (parts[:, :, 0], parts[:, :, 1], parts[:, :, 2])


def attend_forward(packed):
    query_part, key_part, value_part = split_heads(packed)
    scores = jnp.einsum(
        "bqhd,bkhd->bhqk", query_part, key_part, preferred_element_type=jnp.float32
    ) * HDIM ** (-0.5)
    highest = jnp.max(scores, axis=-1, keepdims=True)
    powers = jnp.exp(scores - highest)
    totals = jnp.sum(powers, axis=-1, keepdims=True)
    weights = (powers / totals).astype(jnp.bfloat16)
    mixed_heads = jnp.einsum(
        "bhqk,bkhd->bqhd", weights, value_part, preferred_element_type=jnp.float32
    )
    return (
        mixed_heads.reshape(packed.shape[0], -1).astype(jnp.bfloat16),
        highest + jnp.log(totals),
    )


def attend_backward(packed, logsum, grad_mixed):
    query_part, key_part, value_part = split_heads(packed)
    scale = HDIM ** (-0.5)
    scores = (
        jnp.einsum("bqhd,bkhd->bhqk", query_part, key_part, preferred_element_type=jnp.float32)
        * scale
    )
    probs_full = jnp.exp(scores - logsum)
    upstream = grad_mixed.reshape(query_part.shape)
    grad_probs = jnp.einsum(
        "bqhd,bkhd->bhqk", upstream, value_part, preferred_element_type=jnp.float32
    )
    grad_values = jnp.einsum(
        "bhqk,bqhd->bkhd",
        probs_full.astype(jnp.bfloat16),
        upstream,
        preferred_element_type=jnp.float32,
    )
    grad_scores = (
        probs_full * (grad_probs - jnp.sum(probs_full * grad_probs, axis=-1, keepdims=True))
    ).astype(jnp.bfloat16)
    grad_query = (
        jnp.einsum("bhqk,bkhd->bqhd", grad_scores, key_part, preferred_element_type=jnp.float32)
        * scale
    )
    grad_keys = (
        jnp.einsum("bhqk,bqhd->bkhd", grad_scores, query_part, preferred_element_type=jnp.float32)
        * scale
    )
    stacked = jnp.stack([grad_query, grad_keys, grad_values], axis=2)
    return stacked.reshape(packed.shape[0], -1).astype(jnp.bfloat16)


def attention_forward(stream, gain_row, shift_row, weight_qkv, weight_proj):
    normed, normal, inverse = norm_forward(stream, gain_row, shift_row)
    normed_all = gather_rows(normed.astype(jnp.bfloat16))
    packed = sum_halves(jnp.dot(normed_all, weight_qkv, preferred_element_type=jnp.float32)).astype(
        jnp.bfloat16
    )
    mixed_heads, logsum = attend_forward(packed)
    mixed_all = gather_halves(mixed_heads)
    branch = sum_rows(jnp.dot(mixed_all, weight_proj, preferred_element_type=jnp.float32))
    saved = {
        "normal": normal,
        "inverse": inverse,
        "normed_all": normed_all,
        "packed": packed,
        "logsum": logsum,
        "mixed_all": mixed_all,
    }
    return (stream + branch, saved)


def attention_backward(upstream, saved, weight_qkv, weight_proj):
    grad_all = gather_rows(upstream.astype(jnp.bfloat16))
    grad_mixed = sum_halves(
        jnp.einsum("te,de->td", grad_all, weight_proj, preferred_element_type=jnp.float32)
    ).astype(jnp.bfloat16)
    grad_w_proj = jnp.einsum(
        "td,te->de", saved["mixed_all"], grad_all, preferred_element_type=jnp.float32
    )
    grad_packed = attend_backward(saved["packed"], saved["logsum"], grad_mixed)
    grad_packed_all = gather_halves(grad_packed)
    grad_part = jnp.einsum(
        "tf,df->td", grad_packed_all, weight_qkv, preferred_element_type=jnp.float32
    )
    grad_w_qkv = jnp.einsum(
        "td,tf->df", saved["normed_all"], grad_packed_all, preferred_element_type=jnp.float32
    )
    return (sum_rows(grad_part), grad_w_qkv, grad_w_proj)


def second_product(active, buffer_shape, weight_out):
    active_all = gather_halves(active).reshape(buffer_shape[0], buffer_shape[1], -1)
    slot_out = jnp.einsum(
        "ecf,efd->ecd", active_all, weight_out, preferred_element_type=jnp.float32
    )
    return (active_all, slot_out.reshape(-1, slot_out.shape[2]))


def expert_forward(
    stream, gain_row, shift_row, choice_ids, slot_rows, weight_router, weight_in, weight_out
):
    normed, normal, inverse = norm_forward(stream, gain_row, shift_row)
    normed_all = gather_rows(normed.astype(jnp.bfloat16))
    row_count = normed_all.shape[0]
    expert_count = weight_in.shape[0]
    capacity = 2 * ((5 * row_count + 4 * expert_count - 1) // (4 * expert_count))
    logits = lax.psum(jnp.dot(normed_all, weight_router, preferred_element_type=jnp.float32), "col")
    router = softmax_rows(logits)
    onehot = (
        choice_ids[:, :, None] == lax.broadcasted_iota(jnp.int32, (1, 1, expert_count), 2)
    ).astype(jnp.float32)
    gate_values = jnp.sum(onehot * router[:, None, :], axis=2)
    flat_slots = choice_ids * capacity + slot_rows
    owners = jnp.broadcast_to(
        lax.broadcasted_iota(jnp.int32, (row_count, 1), 0), flat_slots.shape
    ).reshape(-1)
    slot_owner = (
        jnp.full((expert_count * capacity,), row_count, jnp.int32)
        .at[flat_slots.reshape(-1)]
        .set(owners)
    )
    slot_assign = (
        jnp.full((expert_count * capacity,), 2 * row_count, jnp.int32)
        .at[flat_slots.reshape(-1)]
        .set(lax.iota(jnp.int32, 2 * row_count))
    )
    padded = jnp.concatenate(
        [normed_all, jnp.zeros((1, normed_all.shape[1]), jnp.bfloat16)], axis=0
    )
    buffer = padded[slot_owner].reshape(expert_count, capacity, -1)
    hidden_part = jnp.einsum("ecd,edf->ecf", buffer, weight_in, preferred_element_type=jnp.float32)
    hidden = sum_halves(hidden_part.reshape(buffer.shape[0] * buffer.shape[1], -1))
    active = jax.nn.gelu(hidden).astype(jnp.bfloat16)
    active_all, slot_out = second_product(active, buffer.shape, weight_out)
    branch_part = jnp.sum(gate_values[:, :, None] * slot_out[flat_slots], axis=1)
    saved = {
        "normal": normal,
        "inverse": inverse,
        "normed_all": normed_all,
        "router": router,
        "onehot": onehot,
        "gate_values": gate_values,
        "flat_slots": flat_slots,
        "slot_owner": slot_owner,
        "slot_assign": slot_assign,
        "buffer": buffer,
        "hidden": hidden,
        "active": active,
    }
    saved["active_all"] = active_all
    saved["slot_out"] = slot_out
    return (stream + sum_rows(branch_part), saved)


def expert_backward(upstream, saved, weight_router, weight_in, weight_out):
    buffer = saved["buffer"]
    expert_count = weight_in.shape[0]
    capacity = saved["slot_owner"].shape[0] // expert_count
    active_all = saved["active_all"]
    slot_out = saved["slot_out"]
    flat_slots = saved["flat_slots"]
    grad_all = gather_rows(upstream.astype(jnp.bfloat16))
    gate_part = jnp.sum(grad_all.astype(jnp.float32)[:, None, :] * slot_out[flat_slots], axis=2)
    grad_gates = lax.psum(gate_part, ("row", "col"))
    padded_grad = jnp.concatenate(
        [grad_all, jnp.zeros((1, grad_all.shape[1]), jnp.bfloat16)], axis=0
    )
    slot_gate = jnp.concatenate([saved["gate_values"].reshape(-1), jnp.zeros((1,), jnp.float32)])[
        saved["slot_assign"]
    ]
    grad_slot = (
        (slot_gate[:, None] * padded_grad[saved["slot_owner"]])
        .astype(jnp.bfloat16)
        .reshape(expert_count, capacity, -1)
    )
    grad_active_part = jnp.einsum(
        "ecd,efd->ecf", grad_slot, weight_out, preferred_element_type=jnp.float32
    )
    grad_w_out = jnp.einsum(
        "ecf,ecd->efd", active_all, grad_slot, preferred_element_type=jnp.float32
    )
    grad_active = sum_halves(grad_active_part.reshape(buffer.shape[0] * buffer.shape[1], -1))
    gelu_pull = jax.vjp(jax.nn.gelu, saved["hidden"])[1]
    grad_hidden = gelu_pull(grad_active)[0].astype(jnp.bfloat16)
    grad_hidden_all = gather_halves(grad_hidden).reshape(buffer.shape[0], buffer.shape[1], -1)
    grad_buffer = jnp.einsum(
        "ecf,edf->ecd", grad_hidden_all, weight_in, preferred_element_type=jnp.float32
    )
    grad_w_in = jnp.einsum(
        "ecd,ecf->edf", buffer, grad_hidden_all, preferred_element_type=jnp.float32
    )
    grad_buffer = grad_buffer.reshape(expert_count * capacity, -1)
    router = saved["router"]
    grad_probs = jnp.sum(grad_gates[:, :, None] * saved["onehot"], axis=1)
    grad_logits = (
        router * (grad_probs - jnp.sum(router * grad_probs, axis=1, keepdims=True))
    ).astype(jnp.bfloat16)
    grad_w_router = jnp.einsum(
        "td,te->de", saved["normed_all"], grad_logits, preferred_element_type=jnp.float32
    )
    router_back = jnp.einsum(
        "te,de->td", grad_logits, weight_router, preferred_element_type=jnp.float32
    )
    leading = (lax.axis_index("row") == 0).astype(jnp.float32)
    grad_part = jnp.sum(grad_buffer[flat_slots], axis=1) + leading * router_back
    return (sum_rows(grad_part), grad_w_router, grad_w_in, grad_w_out)


def per_device(
    tokens,
    norm_gain,
    norm_shift,
    w_qkv,
    w_proj,
    w_router,
    w_in,
    w_out,
    expert_ids,
    slot_ids,
    cotangent,
):
    layer_count = w_qkv.shape[0]
    stream = tokens.astype(jnp.float32)
    attention_saved = []
    expert_saved = []
    for layer_index in range(layer_count):
        weight_qkv = w_qkv[layer_index].reshape(w_qkv.shape[1], -1)
        stream, kept_one = attention_forward(
            stream,
            norm_gain[layer_index, 0],
            norm_shift[layer_index, 0],
            weight_qkv,
            w_proj[layer_index],
        )
        stream, kept_two = expert_forward(
            stream,
            norm_gain[layer_index, 1],
            norm_shift[layer_index, 1],
            expert_ids[layer_index],
            slot_ids[layer_index],
            w_router[layer_index],
            w_in[layer_index],
            w_out[layer_index],
        )
        attention_saved.append(kept_one)
        expert_saved.append(kept_two)
    output = stream.astype(jnp.bfloat16)
    grad_stream = cotangent.astype(jnp.float32)
    qkv_grads = [None] * layer_count
    proj_grads = [None] * layer_count
    router_grads = [None] * layer_count
    in_grads = [None] * layer_count
    out_grads = [None] * layer_count
    gain_grads = [None] * layer_count
    shift_grads = [None] * layer_count
    for layer_index in reversed(range(layer_count)):
        weight_qkv = w_qkv[layer_index].reshape(w_qkv.shape[1], -1)
        kept_two = expert_saved[layer_index]
        grad_normed, router_grads[layer_index], grad_w_in, grad_w_out = expert_backward(
            grad_stream, kept_two, w_router[layer_index], w_in[layer_index], w_out[layer_index]
        )
        grad_w_in, grad_w_out = (
            lax.psum_scatter(grad_w_in, "dp", scatter_dimension=0, tiled=True),
            lax.psum_scatter(grad_w_out, "dp", scatter_dimension=0, tiled=True),
        )
        in_grads[layer_index] = grad_w_in
        out_grads[layer_index] = grad_w_out
        grad_inner, gain_two, shift_two = norm_backward(
            grad_normed, kept_two["normal"], kept_two["inverse"], norm_gain[layer_index, 1]
        )
        grad_stream = grad_stream + grad_inner
        kept_one = attention_saved[layer_index]
        grad_normed, grad_w_qkv, proj_grads[layer_index] = attention_backward(
            grad_stream, kept_one, weight_qkv, w_proj[layer_index]
        )
        qkv_grads[layer_index] = grad_w_qkv.reshape(w_qkv.shape[1:])
        grad_inner, gain_one, shift_one = norm_backward(
            grad_normed, kept_one["normal"], kept_one["inverse"], norm_gain[layer_index, 0]
        )
        grad_stream = grad_stream + grad_inner
        gain_grads[layer_index] = jnp.stack([gain_one, gain_two])
        shift_grads[layer_index] = jnp.stack([shift_one, shift_two])
    grad_qkv, grad_proj, grad_router = lax.psum(
        (jnp.stack(qkv_grads), jnp.stack(proj_grads), jnp.stack(router_grads)), "dp"
    )
    grad_gain, grad_shift = lax.psum((jnp.stack(gain_grads), jnp.stack(shift_grads)), ("dp", "row"))
    grad_in = jnp.stack(in_grads)
    grad_out = jnp.stack(out_grads)
    return (
        output,
        grad_stream,
        grad_qkv,
        grad_proj,
        grad_router,
        grad_in,
        grad_out,
        grad_gain,
        grad_shift,
    )


def solution(mesh):
    in_specs = (
        P(("dp", "row"), "col"),
        P(None, None, "col"),
        P(None, None, "col"),
        P(None, "col", None, "row"),
        P(None, "row", "col"),
        P(None, "col", None),
        P(None, None, "col", "row"),
        P(None, None, "row", "col"),
        P(None, "dp", None),
        P(None, "dp", None),
        P(("dp", "row"), "col"),
    )
    out_specs = (
        P(("dp", "row"), "col"),
        P(("dp", "row"), "col"),
        P(None, "col", None, "row"),
        P(None, "row", "col"),
        P(None, "col", None),
        P(None, "dp", "col", "row"),
        P(None, "dp", "row", "col"),
        P(None, None, "col"),
        P(None, None, "col"),
    )
    return jax.shard_map(
        per_device, mesh=mesh, in_specs=in_specs, out_specs=out_specs, check_vma=False
    )
```

profile of v0, /device:TPU:0, one launch (start us, length us, event | category | flops | bytes accessed | tf_op | source)
XLA Modules:
  0.0 2337.2 jit_solution(6488170243038040604)
XLA Ops:
  15.6 13.7 all-gather
  41.3 15.8 scatter_custom_fusion
  70.3 33.1 %fusion.1 = f32[400,256]{1,0:T(8,128)S(1)} fusion(f32[1576,256]{1,0:T(8,128)S(1)} %fusion.116), kind=kCustom, calls=%all-reduce-scatter.1 | all-reduce-scatter fusion | flops 409601 | bytes 2023936
  110.9 14.2 all-gather.2
  125.4 12.3 gather_fusion
  159.3 14.9 reduce-scatter.33.cloned.1.call-done
  181.1 15.4 all-reduce.43.cloned.1.call-done
  201.3 12.0 all-gather.19.cloned.1.call-done
  232.3 10.9 gather_fusion.1
  247.1 11.2 multiply_reduce_fusion.3
  258.4 35.5 %fusion.2 = f32[400,256]{1,0:T(8,128)} fusion(f32[1576,256]{1,0:T(8,128)} %multiply_reduce_fusion.3), kind=kCustom, calls=%all-reduce-scatter.2 | all-reduce-scatter fusion | flops 409601 | bytes 2023936
  297.3 15.8 scatter_custom_fusion.1
  318.9 12.3 all-gather.3
  357.7 33.5 %fusion.4 = f32[400,256]{1,0:T(8,128)S(1)} fusion(f32[1576,256]{1,0:T(8,128)} %fusion.112), kind=kCustom, calls=%all-reduce-scatter.4 | all-reduce-scatter fusion | flops 409601 | bytes 2023936
  401.7 14.7 all-gather.5
  419.3 12.3 gather_fusion.2
  453.4 11.6 all-gather.6
  466.7 12.3 gather_fusion.5
  483.1 16.0 scatter_custom_fusion.2
  502.9 20.9 gather_fusion.4
  523.9 10.9 fusion.12
  543.3 16.7 reduce-scatter.37.cloned.1.call-done
  602.8 10.9 gather_fusion.6
  637.9 10.9 gather_fusion.3
  654.0 19.1 multiply_reduce_fusion.1
  673.0 32.3 %psum.185 = f32[1576,2]{1,0:T(8,128)S(1)} all-reduce(f32[1576,2]{1,0:T(8,128)S(1)} %get-tuple-element.45), channel_id=1, replica_groups=mesh['dp'=4,'row'=4,'col'=2] {'row','col'}, use_global_device_ids=true, to_apply=%region_44.0 | all-reduce | flops 3152 | bytes 25216 | tf_op jit(solution)/shard_map/psum | solution.py:227
  705.7 10.8 reduce_sum.394
  719.7 33.0 %fusion.6 = f32[400,256]{1,0:T(8,128)S(1)} fusion(f32[1576,256]{1,0:T(8,128)} %fusion.50), kind=kCustom, calls=%all-reduce-scatter.6 | all-reduce-scatter fusion | flops 409601 | bytes 2023936
  762.3 14.0 all-gather.7
  795.5 16.4 scatter_custom_fusion.3
  814.5 32.8 %fusion.8 = f32[400,256]{1,0:T(8,128)S(1)} fusion(f32[1576,256]{1,0:T(8,128)S(1)} %fusion.155), kind=kCustom, calls=%all-reduce-scatter.8 | all-reduce-scatter fusion | flops 409601 | bytes 2023936
  849.9 20.9 gather_fusion.7
  876.1 12.3 all-gather.9
  889.6 12.1 gather_fusion.8
  903.8 10.9 fusion.20
  923.1 16.8 reduce-scatter.39.cloned.1.call-done
  957.3 33.2 %psum.190 = f32[1576,2]{1,0:T(8,128)S(1)} all-reduce(f32[1576,2]{1,0:T(8,128)} %multiply_reduce_fusion), channel_id=1, replica_groups=mesh['dp'=4,'row'=4,'col'=2] {'row','col'}, use_global_device_ids=true, to_apply=%region_63.0 | all-reduce | flops 3152 | bytes 25216 | tf_op jit(solution)/shard_map/psum | solution.py:227
  1025.0 15.4 reduce_sum.403
  1042.0 32.9 %fusion.9 = f32[400,256]{1,0:T(8,128)S(1)} fusion(f32[1576,256]{1,0:T(8,128)} %fusion.51), kind=kCustom, calls=%all-reduce-scatter.9 | all-reduce-scatter fusion | flops 409601 | bytes 2023936
  1083.6 14.2 all-gather.10
  1131.3 11.7 fusion.72
  1143.8 11.7 fusion.73
  1182.3 59.5 %fusion.145 = (f32[400,256]{1,0:T(8,128)S(1)}, f32[400,256]{1,0:T(8,128)S(1)}) fusion(f32[1576,256]{1,0:T(8,128)S(1)} %copy-done.31, f32[1576,256]{1,0:T(8,128)} %fusion.156), kind=kCustom, calls=%all-reduce-scatter.12 | all-reduce-scatter fusion | flops 819201 | bytes 4047360
  1253.7 43.6 %all-reduce.28 = (f32[2,2,256]{2,1,0:T(2,128)}, f32[2,2,256]{2,1,0:T(2,128)}) all-reduce(f32[2,2,256]{2,1,0:T(2,128)S(1)} %pad_maximum_fusion.9, f32[2,2,256]{2,1,0:T(2,128)S(1)} %pad_maximum_fusion.10), channel_id=1, replica_groups=mesh['dp'=4,'row'=4,'col'=2] {'dp','row'}, use_global_device_ids=true, to_apply=%region_89.0 | all-reduce | flops 2048 | bytes 16384 | tf_op jit(solution)/shard_map/psum | solution.py:349
  1301.4 169.0 %reduce-scatter.47.cloned.1.call-done = f32[8,512,256]{2,1,0:T(8,128)} async-done(((f32[32,512,256]{2,1,0:T(8,128)}), f32[8,512,256]{2,1,0:T(8,128)}) %reduce-scatter.47.cloned.1.call-update) | async-done | bytes 4194320 | tf_op jit(solution)/shard_map/reduce_scatter | solution.py:327
  1470.4 283.5 %reduce-scatter.45.cloned.1.call-done = f32[8,512,256]{2,1,0:T(8,128)} async-done(((f32[32,512,256]{2,1,0:T(8,128)}), f32[8,512,256]{2,1,0:T(8,128)}) %reduce-scatter.45.cloned.1.call-update) | async-done | bytes 4194320 | tf_op jit(solution)/shard_map/reduce_scatter | solution.py:327
  1761.5 275.8 %reduce-scatter.43.cloned.1.call-done = f32[8,256,512]{2,1,0:T(8,128)} async-done(((f32[32,256,512]{2,1,0:T(8,128)}), f32[8,256,512]{2,1,0:T(8,128)}) %reduce-scatter.43.cloned.1.call-update) | async-done | bytes 4194320 | tf_op jit(solution)/shard_map/reduce_scatter | solution.py:326
  2037.3 283.3 %reduce-scatter.41.cloned.1.call-done = f32[8,256,512]{2,1,0:T(8,128)} async-done(((f32[32,256,512]{2,1,0:T(8,128)}), f32[8,256,512]{2,1,0:T(8,128)}) %reduce-scatter.41.cloned.1.call-update) | async-done | bytes 4194320 | tf_op jit(solution)/shard_map/reduce_scatter | solution.py:326
  (574 shorter events, 465.6 us)
Async XLA Ops:
  7.2 167.0 %reduce-scatter.33.cloned.1.call-start = ((), (), s32[]{:S(2)}) async-start(), calls=%async_computation.9 | async-start | bytes 12189696 | tf_op jit(solution)/shard_map/reduce_scatter | solution.py:26
  8.0 102.7 %copy-start.114 = (f32[1,1,256]{2,1,0:T(1,128)}, f32[1,1,256]{2,1,0:T(1,128)S(1)}, u32[]{:S(2)}) copy-start(f32[1,1,256]{2,1,0:T(1,128)S(1)} %get-tuple-element.124) | copy-start | bytes 3076
  8.0 310.2 %copy-start.116 = (f32[1,1,256]{2,1,0:T(1,128)}, f32[1,1,256]{2,1,0:T(1,128)S(1)}, u32[]{:S(2)}) copy-start(f32[1,1,256]{2,1,0:T(1,128)S(1)} %get-tuple-element.126) | copy-start | bytes 3076
  8.0 393.1 %copy-start.120 = (f32[1,1,256]{2,1,0:T(1,128)}, f32[1,1,256]{2,1,0:T(1,128)S(1)}, u32[]{:S(2)}) copy-start(f32[1,1,256]{2,1,0:T(1,128)S(1)} %get-tuple-element.123) | copy-start | bytes 3076
  37.0 21.3 collective-permute-start
  103.4 4.0 collective-permute-start.1
  157.4 39.1 %all-reduce.43.cloned.1.call-start = ((), (), s32[]{:S(2)}) async-start(), calls=%async_computation.8 | async-start | bytes 425984 | tf_op jit(solution)/shard_map/psum | solution.py:170
  159.2 54.1 %all-gather.19.cloned.1.call-start = ((), (), s32[]{:S(2)}) async-start(), calls=%async_computation.10 | async-start | bytes 6094848 | tf_op jit(solution)/shard_map/all_gather | solution.py:22
  178.9 320.2 %all-reduce.45.cloned.1.call-start = ((), (), s32[]{:S(2)}) async-start(), calls=%async_computation.11 | async-start | bytes 425984 | tf_op jit(solution)/shard_map/psum | solution.py:170
  180.5 51.9 %copy-start = (s32[4096]{0:T(1024)}, s32[4096]{0:T(1024)S(1)}, u32[]{:S(2)}) copy-start(s32[4096]{0:T(1024)S(1)} %pad_clamp_fusion.4) | copy-start | bytes 49156
  247.1 46.8 %copy-start.4 = (f32[1576,2,256]{2,1,0:T(2,128)}, f32[1576,2,256]{2,1,0:T(2,128)S(1)}, u32[]{:S(2)}) copy-start(f32[1576,2,256]{2,1,0:T(2,128)S(1)} %reshape.352) | copy-start | bytes 9682948
  247.1 50.1 %copy-start.64 = (bf16[1,256,3,128]{3,1,2,0:T(8,128)(2,1)S(1)}, bf16[1,256,3,128]{3,1,2,0:T(8,128)(2,1)}, u32[]{:S(2)}) copy-start(bf16[1,256,3,128]{3,1,2,0:T(8,128)(2,1)} %get-tuple-element.117) | copy-start | bytes 589828
  294.6 18.6 collective-permute-start.2
  315.7 81.7 %copy-start.17 = (f32[394,256]{1,0:T(8,128)}, f32[394,256]{1,0:T(8,128)S(1)}, u32[]{:S(2)}) copy-start(f32[394,256]{1,0:T(8,128)S(1)} %get-tuple-element.105) | copy-start | bytes 1210372
  341.0 3.1 collective-permute-start.3
  391.2 4.0 collective-permute-start.4
  418.8 124.4 %reduce-scatter.35.cloned.1.call-start = ((), (), s32[]{:S(2)}) async-start(), calls=%async_computation.12 | async-start | bytes 12189696 | tf_op jit(solution)/shard_map/reduce_scatter | solution.py:26
  452.5 107.5 %reduce-scatter.37.cloned.1.call-start = ((), (), s32[]{:S(2)}) async-start(), calls=%async_computation.14 | async-start | bytes 12189696 | tf_op jit(solution)/shard_map/reduce_scatter | solution.py:26
  543.2 38.1 %all-gather.23.cloned.1.call-start = ((), (), s32[]{:S(2)}) async-start(), calls=%async_computation.15 | async-start | bytes 6094848 | tf_op jit(solution)/shard_map/all_gather | solution.py:22
  566.4 52.6 %all-gather.21.cloned.1.call-start = ((), (), s32[]{:S(2)}) async-start(), calls=%async_computation.13 | async-start | bytes 6094848 | tf_op jit(solution)/shard_map/all_gather | solution.py:22
  567.1 245.3 %all-gather.27.cloned.1.call-start = ((), (), s32[]{:S(2)}) async-start(), calls=%async_computation.22 | async-start | bytes 1824768 | tf_op jit(solution)/shard_map/all_gather | solution.py:22
  716.6 44.6 %copy-start.63 = (bf16[394,256]{1,0:T(8,128)(2,1)S(1)}, bf16[394,256]{1,0:T(8,128)(2,1)}, u32[]{:S(2)}) copy-start(bf16[394,256]{1,0:T(8,128)(2,1)} %param.21) | copy-start | bytes 605188
  752.7 4.0 collective-permute-start.6
  782.8 3.1 collective-permute-start.7
  795.5 144.4 %reduce-scatter.39.cloned.1.call-start = ((), (), s32[]{:S(2)}) async-start(), calls=%async_computation.16 | async-start | bytes 12189696 | tf_op jit(solution)/shard_map/reduce_scatter | solution.py:26
  847.3 23.6 %collective-permute-start.8 = (f32[18,256]{1,0:T(8,128)S(1)}, f32[18,256]{1,0:T(8,128)S(1)}, u32[]{:S(2)}, u32[]{:S(2)}) collective-permute-start(f32[18,256]{1,0:T(8,128)S(1)} %slice.166), channel_id=1, source_target_pairs={{0,2},{2,4},{4,6},{1,3},{3,5},{5,7},{8,10},{10,12},{12,14},{9,11},... | collective-permute-start | bytes 55304
  923.0 68.7 %all-gather.25.cloned.1.call-start = ((), (), s32[]{:S(2)}) async-start(), calls=%async_computation.17 | async-start | bytes 6094848 | tf_op jit(solution)/shard_map/all_gather | solution.py:22
  945.7 182.4 %all-gather.29.cloned.1.call-start = ((), (), s32[]{:S(2)}) async-start(), calls=%async_computation.23 | async-start | bytes 1824768 | tf_op jit(solution)/shard_map/all_gather | solution.py:22
  947.9 43.0 %copy-start.70 = (f32[1576]{0:T(1024)S(1)}, f32[1576]{0:T(1024)}, u32[]{:S(2)}) copy-start(f32[1576]{0:T(1024)} %copy-done.69) | copy-start | bytes 18916
  947.9 43.0 %copy-start.82 = (f32[1576]{0:T(1024)S(1)}, f32[1576]{0:T(1024)}, u32[]{:S(2)}) copy-start(f32[1576]{0:T(1024)} %copy-done.81) | copy-start | bytes 18916
  991.7 48.7 %copy-start.60 = (bf16[1576,32]{0,1:T(8,128)(2,1)}, bf16[1576,32]{0,1:T(8,128)(2,1)S(1)}, u32[]{:S(2)}) copy-start(bf16[1576,32]{0,1:T(8,128)(2,1)S(1)} %multiply_convert_fusion.10) | copy-start | bytes 302596
  1075.0 4.1 collective-permute-start.9
  1103.7 3.1 collective-permute-start.10
  1118.7 180.5 %all-reduce.47.cloned.1.call-start = ((), (), s32[]{:S(2)}) async-start(), calls=%async_computation.24 | async-start | bytes 2228224 | tf_op jit(solution)/shard_map/psum | solution.py:346
  1131.3 339.1 %reduce-scatter.47.cloned.1.call-start = ((), (), s32[]{:S(2)}) async-start(), calls=%async_computation.21 | async-start | bytes 20971520 | tf_op jit(solution)/shard_map/reduce_scatter | solution.py:327
  1143.1 610.9 %reduce-scatter.45.cloned.1.call-start = ((), (), s32[]{:S(2)}) async-start(), calls=%async_computation.20 | async-start | bytes 20971520 | tf_op jit(solution)/shard_map/reduce_scatter | solution.py:327
  1155.5 881.8 %reduce-scatter.43.cloned.1.call-start = ((), (), s32[]{:S(2)}) async-start(), calls=%async_computation.19 | async-start | bytes 20971520 | tf_op jit(solution)/shard_map/reduce_scatter | solution.py:326
  1167.6 1153.0 %reduce-scatter.41.cloned.1.call-start = ((), (), s32[]{:S(2)}) async-start(), calls=%async_computation.18 | async-start | bytes 20971520 | tf_op jit(solution)/shard_map/reduce_scatter | solution.py:326
  1180.6 68.1 %copy-start.122 = (f32[256]{0:T(256)S(1)}, f32[256]{0:T(256)}, u32[]{:S(2)}) copy-start(f32[256]{0:T(256)} %get-tuple-element.62) | copy-start | bytes 3076
  1180.6 68.1 %copy-start.124 = (f32[256]{0:T(256)S(1)}, f32[256]{0:T(256)}, u32[]{:S(2)}) copy-start(f32[256]{0:T(256)} %get-tuple-element.61) | copy-start | bytes 3076
  1182.3 68.5 %copy-start.35 = (bf16[394,256]{1,0:T(8,128)(2,1)S(1)}, bf16[394,256]{1,0:T(8,128)(2,1)}, u32[]{:S(2)}) copy-start(bf16[394,256]{1,0:T(8,128)(2,1)} %param.11) | copy-start | bytes 605188
  1182.3 68.5 %copy-start.94 = (f32[394]{0:T(512)S(1)}, f32[394]{0:T(512)}, u32[]{:S(2)}) copy-start(f32[394]{0:T(512)} %copy-done.93) | copy-start | bytes 4732
  1182.3 68.5 %copy-start.96 = (f32[394]{0:T(512)S(1)}, f32[394]{0:T(512)}, u32[]{:S(2)}) copy-start(f32[394]{0:T(512)} %copy-done.95) | copy-start | bytes 4732
  1182.3 68.5 %copy-start.113 = (f32[1,1,256]{2,1,0:T(1,128)S(1)}, f32[1,1,256]{2,1,0:T(1,128)}, u32[]{:S(2)}) copy-start(f32[1,1,256]{2,1,0:T(1,128)} %copy-done.112) | copy-start | bytes 3076
  1182.3 115.0 %copy-start.21 = (f32[394,256]{1,0:T(8,128)S(1)}, f32[394,256]{1,0:T(8,128)}, u32[]{:S(2)}) copy-start(f32[394,256]{1,0:T(8,128)} %copy-done.19) | copy-start | bytes 1210372
  1182.3 115.7 %copy-start.51 = (f32[394,256]{1,0:T(8,128)S(1)}, f32[394,256]{1,0:T(8,128)}, u32[]{:S(2)}) copy-start(f32[394,256]{1,0:T(8,128)} %get-tuple-element.97) | copy-start | bytes 1210372
  1241.9 6.8 collective-permute-start.11
  1245.3 4.9 collective-permute-start.5
  (109 other events, 1706.6 us)
Sparse Core Ops, SparseCore 0:
  157.5 16.6 reduce-scatter.32
  177.1 19.3 all-reduce.42
  198.7 14.6 all-gather.18
  419.0 18.1 all-reduce.44
  452.6 16.6 reduce-scatter.34
  543.3 16.6 reduce-scatter.36
  566.5 14.7 all-gather.22
  582.8 14.6 all-gather.20
  795.6 9.3 all-gather.26
  923.2 16.6 reduce-scatter.38
  945.8 14.7 all-gather.24
  1118.8 9.3 all-gather.28
  1131.4 55.7 all-reduce.46
  1189.5 280.8 reduce-scatter.46
  1472.6 281.2 reduce-scatter.44
  1756.3 281.0 reduce-scatter.42
  2039.5 281.0 reduce-scatter.40
where the time goes:
time: 2350 us; the launch traced here: 2340 us
  waiting for transfers between devices  1110 us (47%)
  blocking collectives  522 us (22%)
  local copies, waits for them, and re-layouts  382 us (16%)
  matrix products  146 us (6%)
  other arithmetic  128 us (5%)
  starting transfers between devices  32.3 us (1%)
    reduce_scatter x2, waiting for transfers between devices, per_device(): lax.psum_scatter(grad_w_in, 'dp', scatter_dimension=0, tiled=True)  559 us
    reduce_scatter x2, waiting for transfers between devices, per_device(): lax.psum_scatter(grad_w_out, 'dp', scatter_dimension=0, tiled=True)  453 us
    unnamed x11, blocking collectives  281 us
    all_gather x8, blocking collectives, gather_rows(): return lax.all_gather(values, 'row', axis=0, tiled=True)  107 us
    psum x2, blocking collectives, expert_backward(): grad_gates = lax.psum(gate_part, ('row', 'col'))  65.5 us
    unnamed x313, local copies, waits for them, and re-layouts  58.2 us
    reduce_scatter x4, waiting for transfers between devices, sum_halves(): return lax.psum_scatter(values, 'col', scatter_dimension=0, tiled=True)  48.4 us
  transfers between devices with their start and end apart: 29, of which 19 were waited for; matrix products, arithmetic and copies ran while one was open for 16% of the time, Pallas kernels for 0%

commit v1 on v0

--- a/solution.py
+++ b/solution.py
@@ -1,6 +1,10 @@
+import functools
+
 import jax
 import jax.numpy as jnp
 from jax import lax
+from jax.experimental import pallas as pl
+from jax.experimental.pallas import tpu as pltpu
 from jax.sharding import PartitionSpec as P
 
 HDIM = 64
@@ -362,6 +366,582 @@
     )
 
 
+def exchange(values, axis, offset):
+    count = lax.axis_size(axis)
+    return lax.ppermute(values, axis, [(place, place ^ offset) for place in range(count)])
+
+
+def contract(left, right, left_dim, right_dim):
+    return lax.dot_general(
+        left, right, (((left_dim,), (right_dim,)), ((), ())), preferred_element_type=jnp.float32
+    )
+
+
+def layer_norm_parts(values):
+    center = jnp.mean(values, axis=1, keepdims=True)
+    shifted = values - center
+    spread = jnp.mean(shifted * shifted, axis=1, keepdims=True)
+    inverse = lax.rsqrt(spread + EPSILON)
+    return (shifted * inverse, inverse)
+
+
+def layer_norm_pull(upstream, normal, inverse, gain_row):
+    scaled = upstream * gain_row
+    first = jnp.mean(scaled, axis=1, keepdims=True)
+    second = jnp.mean(scaled * normal, axis=1, keepdims=True)
+    return inverse * (scaled - first - normal * second)
+
+
+def gelu_parts(values):
+    factor = (2.0 / jnp.pi) ** 0.5
+    squares = values * values
+    curve = jnp.tanh(values * (factor + (factor * 0.044715) * squares))
+    half = 0.5 + 0.5 * curve
+    slope = half + (0.5 * values) * (1.0 - curve * curve) * (
+        factor + (3.0 * factor * 0.044715) * squares
+    )
+    return (values * half, slope)
+
+
+def head_probs(query_head, key_pair, valid):
+    scores = contract(query_head, key_pair, 1, 1) * HDIM ** (-0.5)
+    scores = jnp.where(valid, scores, -1e30)
+    powers = jnp.exp(scores - jnp.max(scores, axis=1, keepdims=True))
+    return powers / jnp.sum(powers, axis=1, keepdims=True)
+
+
+def assemble_weights(place_ref, block_refs, full_ref, rows, features):
+    half = features // 2
+    strip = features // rows
+    for position, block_ref in enumerate(block_refs):
+        other, offset = divmod(position, rows)
+        side = lax.bitwise_xor(place_ref[2], other)
+        top = pl.multiple_of(side * half, half)
+        for part in range(3):
+            full_ref[pl.ds(top, half), pl.ds(part * features + offset * strip, strip)] = block_ref[
+                :, pl.ds(part * strip, strip)
+            ]
+        for piece in range(half // strip):
+            left = pl.multiple_of(3 * features + side * half + piece * strip, strip)
+            full_ref[pl.ds(offset * strip, strip), pl.ds(left, strip)] = block_ref[
+                pl.ds(piece * strip, strip), pl.ds(3 * strip, strip)
+            ]
+
+
+def attention_forward_kernel(rows, place_ref, *refs):
+    block_refs = refs[: 2 * rows]
+    norm_ref, stream_ref = refs[2 * rows : 2 * rows + 2]
+    part_refs = refs[2 * rows + 2 : -6]
+    start_ref, middle_ref, first_ref, packed_ref, mixed_ref, second_ref, full_ref = refs[-7:]
+    part_refs = refs[2 * rows + 2 : -7]
+    features = stream_ref.shape[1]
+    padded = stream_ref.shape[0]
+    assemble_weights(place_ref, block_refs, full_ref, rows, features)
+    stream = stream_ref[...].astype(jnp.float32)
+    for part_ref in part_refs:
+        stream = stream + part_ref[...].astype(jnp.float32)
+    start_ref[...] = stream
+    normal, _ = layer_norm_parts(stream)
+    normed = (normal * norm_ref[0:1] + norm_ref[2:3]).astype(jnp.bfloat16)
+    first_ref[...] = normed
+    for part in range(3):
+        columns = pl.ds(part * features, features)
+        packed_ref[:, columns] = contract(normed, full_ref[:, columns], 1, 0).astype(jnp.bfloat16)
+    valid = lax.broadcasted_iota(jnp.int32, (padded, padded), 1) < SEQ
+    lower = lax.broadcasted_iota(jnp.int32, (padded, 2 * HDIM), 1) < HDIM
+    for pair in range(features // (2 * HDIM)):
+        query = packed_ref[:, pl.ds(pair * 2 * HDIM, 2 * HDIM)]
+        keys = packed_ref[:, pl.ds(features + pair * 2 * HDIM, 2 * HDIM)]
+        values = packed_ref[:, pl.ds(2 * features + pair * 2 * HDIM, 2 * HDIM)]
+        blank = jnp.zeros_like(query)
+        results = []
+        for query_head in (jnp.where(lower, query, blank), jnp.where(lower, blank, query)):
+            probs = head_probs(query_head, keys, valid).astype(jnp.bfloat16)
+            results.append(contract(probs, values, 1, 0))
+        mixed_ref[:, pl.ds(pair * 2 * HDIM, 2 * HDIM)] = jnp.where(
+            lower, results[0], results[1]
+        ).astype(jnp.bfloat16)
+    stream = stream + contract(mixed_ref[...], full_ref[:, pl.ds(3 * features, features)], 1, 0)
+    middle_ref[...] = stream
+    normal, _ = layer_norm_parts(stream)
+    second_ref[...] = (normal * norm_ref[1:2] + norm_ref[3:4]).astype(jnp.bfloat16)
+
+
+def attention_backward_kernel(rows, place_ref, *refs):
+    (
+        full_ref,
+        norm_ref,
+        start_ref,
+        middle_ref,
+        first_ref,
+        packed_ref,
+        mixed_ref,
+        grad_ref,
+        router_ref,
+    ) = refs[:9]
+    part_refs = refs[9:-5]
+    result_ref, branch_ref, blocks_ref, gpacked_ref, gmixed_ref = refs[-5:]
+    features = start_ref.shape[1]
+    padded = start_ref.shape[0]
+    upstream = part_refs[0][...].astype(jnp.float32)
+    for part_ref in part_refs[1:]:
+        upstream = upstream + part_ref[...].astype(jnp.float32)
+    normal, inverse = layer_norm_parts(middle_ref[...])
+    gain_two = jnp.sum(upstream * normal, axis=0, keepdims=True)
+    shift_two = jnp.sum(upstream, axis=0, keepdims=True)
+    grad_middle = grad_ref[...].astype(jnp.float32) + layer_norm_pull(
+        upstream, normal, inverse, norm_ref[1:2]
+    )
+    grad_attn = grad_middle.astype(jnp.bfloat16)
+    gmixed_ref[...] = contract(
+        grad_attn, full_ref[:, pl.ds(3 * features, features)], 1, 1
+    ).astype(jnp.bfloat16)
+    valid = lax.broadcasted_iota(jnp.int32, (padded, padded), 1) < SEQ
+    lower = lax.broadcasted_iota(jnp.int32, (padded, 2 * HDIM), 1) < HDIM
+    scale = HDIM ** (-0.5)
+    for pair in range(features // (2 * HDIM)):
+        spans = [pl.ds(part * features + pair * 2 * HDIM, 2 * HDIM) for part in range(3)]
+        query, keys, values = [packed_ref[:, span] for span in spans]
+        gmixed = gmixed_ref[:, spans[0]]
+        blank = jnp.zeros_like(query)
+        found = []
+        for side in range(2):
+            keep = lower if side == 0 else jnp.logical_not(lower)
+            probs = head_probs(jnp.where(keep, query, blank), keys, valid)
+            grad_probs = contract(jnp.where(keep, gmixed, blank), values, 1, 1)
+            grad_values = contract(probs.astype(jnp.bfloat16), gmixed, 0, 0)
+            grad_scores = (
+                probs * (grad_probs - jnp.sum(probs * grad_probs, axis=1, keepdims=True))
+            ).astype(jnp.bfloat16)
+            grad_query = contract(grad_scores, keys, 1, 0) * scale
+            grad_keys = contract(grad_scores, query, 0, 0) * scale
+            found.append((grad_query, grad_keys, grad_values))
+        for part in range(3):
+            gpacked_ref[:, spans[part]] = jnp.where(lower, found[0][part], found[1][part]).astype(
+                jnp.bfloat16
+            )
+    upstream = contract(gpacked_ref[...], full_ref[:, pl.ds(0, 3 * features)], 1, 1)
+    normal, inverse = layer_norm_parts(start_ref[...])
+    gain_one = jnp.sum(upstream * normal, axis=0, keepdims=True)
+    shift_one = jnp.sum(upstream, axis=0, keepdims=True)
+    result = grad_middle + layer_norm_pull(upstream, normal, inverse, norm_ref[0:1])
+    result_ref[...] = result
+    branch_ref[...] = result.astype(jnp.bfloat16)
+    half = features // 2
+    strip = features // rows
+    extra = jnp.concatenate(
+        [
+            router_ref[...],
+            gain_one,
+            gain_two,
+            shift_one,
+            shift_two,
+            jnp.zeros((blocks_ref.shape[1] - 4 * strip - router_ref.shape[0] - 4, features), jnp.float32),
+        ],
+        axis=0,
+    ).astype(jnp.bfloat16)
+    grad_proj = contract(mixed_ref[...], grad_attn, 0, 0).astype(jnp.bfloat16)
+    for offset in range(rows):
+        spot = lax.bitwise_xor(place_ref[1], offset) * 2
+        for side in range(2):
+            columns = slice(side * half, (side + 1) * half)
+            blocks_ref[spot + side, pl.ds(3 * strip, strip), :] = grad_proj[
+                offset * strip : (offset + 1) * strip, columns
+            ]
+            blocks_ref[spot + side, pl.ds(4 * strip, extra.shape[0]), :] = extra[:, columns]
+    for part in range(3):
+        grad_part = contract(
+            gpacked_ref[:, pl.ds(part * features, features)], first_ref[...], 0, 0
+        ).astype(jnp.bfloat16)
+        for offset in range(rows):
+            spot = lax.bitwise_xor(place_ref[1], offset) * 2
+            for side in range(2):
+                blocks_ref[spot + side, pl.ds(part * strip, strip), :] = grad_part[
+                    offset * strip : (offset + 1) * strip, side * half : (side + 1) * half
+                ]
+
+
+def dispatch_kernel(room, codes_ref, *refs):
+    groups = codes_ref.shape[1]
+    block_refs, out_refs = refs[:-groups], refs[-groups:]
+    padded = block_refs[0].shape[0]
+    rows_of = lax.broadcasted_iota(jnp.int32, (room, padded), 0)
+    for group in range(groups):
+        total = jnp.zeros((room, block_refs[0].shape[1]), jnp.float32)
+        for image, block_ref in enumerate(block_refs):
+            picks = (codes_ref[image, group : group + 1, :] == rows_of).astype(jnp.float32)
+            total = total + contract(picks.astype(jnp.bfloat16), block_ref[...], 1, 0)
+        out_refs[group][...] = total.astype(jnp.bfloat16)
+
+
+def combine_kernel(rows, codes_ref, *refs):
+    slot_refs, out_refs = refs[: codes_ref.shape[1]], refs[codes_ref.shape[1] :]
+    room = slot_refs[0].shape[0]
+    padded = out_refs[0].shape[0]
+    lanes = lax.broadcasted_iota(jnp.int32, (padded, room), 1)
+    for image in range(rows):
+        total = jnp.zeros(out_refs[0].shape, jnp.float32)
+        for source, slot_ref in enumerate(slot_refs):
+            codes = codes_ref[pl.ds(image * padded, padded), source : source + 1]
+            picks = (codes == lanes).astype(jnp.float32)
+            total = total + contract(picks.astype(jnp.bfloat16), slot_ref[...], 1, 0)
+        out_refs[image][...] = total.astype(jnp.bfloat16)
+
+
+def expert_router(place_ref, buffer, wrouter):
+    router = softmax_rows(contract(buffer, wrouter, 1, 1))
+    chosen = lax.broadcasted_iota(jnp.int32, router.shape, 1) == place_ref[3]
+    gate = jnp.sum(jnp.where(chosen, router, 0.0), axis=1, keepdims=True)
+    return (router, chosen, gate)
+
+
+def expert_forward_kernel(groups, place_ref, wrouter_ref, win_ref, wout_ref, *refs):
+    buffer = jnp.concatenate([ref[...] for ref in refs[:groups]], axis=0)
+    room = refs[0].shape[0]
+    half = buffer.shape[1] // 2
+    _, _, gate = expert_router(place_ref, buffer, wrouter_ref[...])
+    sums = [jnp.zeros((buffer.shape[0], half), jnp.float32) for _ in range(2)]
+    for quarter in range(win_ref.shape[0] // 2):
+        hidden = contract(buffer[:, :half], win_ref[2 * quarter], 1, 0) + contract(
+            buffer[:, half:], win_ref[2 * quarter + 1], 1, 0
+        )
+        active = gelu_parts(hidden)[0].astype(jnp.bfloat16)
+        for side in range(2):
+            sums[side] = sums[side] + contract(active, wout_ref[2 * quarter + side], 1, 0)
+    for group in range(groups):
+        span = slice(group * room, (group + 1) * room)
+        for side in range(2):
+            refs[groups + group][:, pl.ds(side * half, half)] = (
+                gate[span] * sums[side][span]
+            ).astype(jnp.bfloat16)
+
+
+def expert_full_kernel(groups, with_output, place_ref, wrouter_ref, win_ref, wout_ref, *refs):
+    buffer = jnp.concatenate([ref[...] for ref in refs[:groups]], axis=0)
+    grads = jnp.concatenate([ref[...] for ref in refs[groups : 2 * groups]], axis=0)
+    back_refs = refs[2 * groups : 3 * groups]
+    out_refs = refs[3 * groups : -3]
+    gin_ref, gout_ref, grouter_ref = refs[-3:]
+    room = refs[0].shape[0]
+    half = buffer.shape[1] // 2
+    router, chosen, gate = expert_router(place_ref, buffer, wrouter_ref[...])
+    grad_slot = (gate * grads.astype(jnp.float32)).astype(jnp.bfloat16)
+    flipped = buffer.T
+    sums = [jnp.zeros((buffer.shape[0], half), jnp.float32) for _ in range(2)]
+    backs = [jnp.zeros((buffer.shape[0], half), jnp.float32) for _ in range(2)]
+    grad_gate = jnp.zeros((buffer.shape[0], 1), jnp.float32)
+    for quarter in range(win_ref.shape[0] // 2):
+        hidden = contract(buffer[:, :half], win_ref[2 * quarter], 1, 0) + contract(
+            buffer[:, half:], win_ref[2 * quarter + 1], 1, 0
+        )
+        value, slope = gelu_parts(hidden)
+        active = value.astype(jnp.bfloat16)
+        if with_output:
+            for side in range(2):
+                sums[side] = sums[side] + contract(active, wout_ref[2 * quarter + side], 1, 0)
+        pulled = contract(grads[:, :half], wout_ref[2 * quarter], 1, 1) + contract(
+            grads[:, half:], wout_ref[2 * quarter + 1], 1, 1
+        )
+        grad_gate = grad_gate + jnp.sum(
+            pulled * active.astype(jnp.float32), axis=1, keepdims=True
+        )
+        grad_hidden = (gate * pulled * slope).astype(jnp.bfloat16)
+        turned = active.T
+        for side in range(2):
+            block = 2 * quarter + side
+            span = slice(side * half, (side + 1) * half)
+            backs[side] = backs[side] + contract(grad_hidden, win_ref[block], 1, 1)
+            gin_ref[block] = contract(flipped[span], grad_hidden, 1, 0).astype(jnp.bfloat16)
+            gout_ref[block] = contract(turned, grad_slot[:, span], 1, 0).astype(jnp.bfloat16)
+    grad_logits = (
+        router * (jnp.where(chosen, grad_gate, 0.0) - gate * grad_gate)
+    ).astype(jnp.bfloat16)
+    grouter_ref[...] = contract(grad_logits, buffer, 0, 0)
+    router_back = contract(grad_logits, wrouter_ref[...], 1, 0)
+    for group in range(groups):
+        span = slice(group * room, (group + 1) * room)
+        for side in range(2):
+            columns = slice(side * half, (side + 1) * half)
+            back_refs[group][:, columns] = (
+                backs[side][span] + router_back[span, columns]
+            ).astype(jnp.bfloat16)
+            if with_output:
+                out_refs[group][:, columns] = (gate[span] * sums[side][span]).astype(jnp.bfloat16)
+
+
+SMALL = pl.BlockSpec(memory_space=pltpu.SMEM)
+LOCAL = pl.BlockSpec(memory_space=pltpu.VMEM)
+
+
+def run_kernel(body, place, operands, results, scratch=()):
+    specs = [LOCAL] * len(operands)
+    arguments = list(operands)
+    if place is not None:
+        specs = [SMALL] + specs
+        arguments = [place] + arguments
+    return pl.pallas_call(
+        body,
+        in_specs=specs,
+        out_specs=[LOCAL] * len(results),
+        out_shape=[jax.ShapeDtypeStruct(shape, kind) for shape, kind in results],
+        scratch_shapes=list(scratch),
+        compiler_params=pltpu.CompilerParams(vmem_limit_bytes=48 * 1024 * 1024),
+    )(*arguments)
+
+
+def gather_group(values):
+    near = [values]
+    for offset in range(1, lax.axis_size("row")):
+        near.append(exchange(values, "row", offset))
+    return near + [exchange(piece, "col", 1) for piece in near]
+
+
+def scatter_pieces(pieces, axis):
+    return [
+        piece if offset == 0 else exchange(piece, axis, offset)
+        for offset, piece in enumerate(pieces)
+    ]
+
+
+def group_device(
+    tokens,
+    norm_gain,
+    norm_shift,
+    w_qkv,
+    w_proj,
+    w_router,
+    w_in,
+    w_out,
+    expert_ids,
+    slot_ids,
+    cotangent,
+):
+    low = jnp.bfloat16
+    groups, rows = lax.axis_size("dp"), lax.axis_size("row")
+    members = 2 * rows
+    at_dp, at_row, at_col = [lax.axis_index(name) for name in ("dp", "row", "col")]
+    layer_count = w_qkv.shape[0]
+    expert_count = w_in.shape[1]
+    half = tokens.shape[1]
+    features = 2 * half
+    strip = features // rows
+    padded = -(-SEQ // 16) * 16
+    owner = at_dp * members + at_row * 2 + at_col
+    place = jnp.stack([at_dp, at_row, at_col, owner]).astype(jnp.int32)
+
+    def join(mine, other):
+        return jnp.where(
+            at_col == 0,
+            jnp.concatenate([mine, other], axis=-1),
+            jnp.concatenate([other, mine], axis=-1),
+        )
+
+    small = jnp.concatenate(
+        [
+            jnp.concatenate([norm_gain, norm_shift], axis=1).reshape(-1, half),
+            w_router.transpose(0, 2, 1).reshape(-1, half).astype(jnp.float32),
+        ],
+        axis=0,
+    )
+    small = join(small, exchange(small, "col", 1))
+    norms = small[: 4 * layer_count].reshape(layer_count, 4, features)
+    routers = small[4 * layer_count :].reshape(layer_count, expert_count, features).astype(low)
+    both = jnp.stack([tokens, cotangent]).reshape(2, 2, SEQ, half)
+    mine = lax.dynamic_index_in_dim(both, at_col, 1, keepdims=False)
+    other = exchange(lax.dynamic_index_in_dim(both, 1 - at_col, 1, keepdims=False), "col", 1)
+    both = jnp.pad(join(mine, other), ((0, 0), (0, padded - SEQ), (0, 0)))
+
+    attention_blocks = []
+    for layer in range(layer_count):
+        block = jnp.concatenate(
+            [
+                w_qkv[layer].reshape(half, -1),
+                jnp.concatenate(
+                    [
+                        w_proj[layer][:, piece * strip : (piece + 1) * strip]
+                        for piece in range(half // strip)
+                    ],
+                    axis=0,
+                ),
+            ],
+            axis=1,
+        )
+        attention_blocks.append(gather_group(block))
+
+    weights_in, weights_out = [], []
+    for layer in range(layer_count):
+        for store, source in ((weights_in, w_in), (weights_out, w_out)):
+            local = lax.dynamic_slice_in_dim(source[layer], at_dp * members, members, 0)
+            store.append(
+                lax.all_to_all(local, ("row", "col"), split_axis=0, concat_axis=0, tiled=True)
+            )
+
+    capacity = 2 * ((5 * members * SEQ + 4 * expert_count - 1) // (4 * expert_count))
+    room = -(-capacity // 16) * 16
+    images = jnp.stack(
+        [(at_row ^ offset) * 2 + (at_col ^ side) for side in range(2) for offset in range(rows)]
+    )
+    named = jnp.stack(
+        [
+            (at_dp ^ offset) * members + at_row * 2 + (at_col ^ side)
+            for side in range(2)
+            for offset in range(groups)
+        ]
+    )
+    chosen = jnp.take(expert_ids.reshape(layer_count, members, SEQ, -1), images, axis=1)
+    slots = jnp.take(slot_ids.reshape(layer_count, members, SEQ, -1), images, axis=1)
+    codes = jnp.max(
+        jnp.where(chosen[..., None] == named, slots[..., None], -1), axis=3
+    )
+    codes = jnp.pad(codes, ((0, 0), (0, 0), (0, padded - SEQ), (0, 0)), constant_values=-1)
+    send_codes = codes[..., :groups].transpose(0, 1, 3, 2)
+    back_codes = codes[:, :rows].reshape(layer_count, rows * padded, 2 * groups)
+
+    token_block = ((padded, features), low)
+    slot_block = ((room, features), low)
+
+    def send_out(layer, values):
+        blocks = run_kernel(
+            functools.partial(dispatch_kernel, room),
+            None,
+            [send_codes[layer]] + gather_group(values),
+            [slot_block] * groups,
+        )
+        return scatter_pieces(blocks, "dp")
+
+    def bring_back(layer, blocks):
+        blocks = scatter_pieces(blocks, "dp")
+        blocks = blocks + [exchange(piece, "col", 1) for piece in blocks]
+        pieces = run_kernel(
+            functools.partial(combine_kernel, rows),
+            None,
+            [back_codes[layer]] + blocks,
+            [token_block] * rows,
+        )
+        return scatter_pieces(pieces, "row")
+
+    stream, parts = both[0], []
+    kept, buffers = [], []
+    branches = send_out(layer_count - 1, both[1])
+    grad_parts = None
+    for layer in range(layer_count):
+        saved = run_kernel(
+            functools.partial(attention_forward_kernel, rows),
+            place,
+            attention_blocks[layer] + [norms[layer], stream] + parts,
+            [
+                ((padded, features), jnp.float32),
+                ((padded, features), jnp.float32),
+                token_block,
+                ((padded, 3 * features), low),
+                token_block,
+                token_block,
+                ((features, 4 * features), low),
+            ],
+        )
+        kept.append(saved)
+        buffer = send_out(layer, saved[5])
+        buffers.append(buffer)
+        stream = saved[1]
+        if layer < layer_count - 1:
+            result = run_kernel(
+                functools.partial(expert_forward_kernel, groups),
+                place,
+                [routers[layer], weights_in[layer], weights_out[layer]] + buffer,
+                [slot_block] * groups,
+            )
+            parts = bring_back(layer, result)
+    grad = both[1]
+    results = {}
+    for layer in reversed(range(layer_count)):
+        last = layer == layer_count - 1
+        found = run_kernel(
+            functools.partial(expert_full_kernel, groups, last),
+            place,
+            [routers[layer], weights_in[layer], weights_out[layer]] + buffers[layer] + branches,
+            [slot_block] * (2 * groups if last else groups)
+            + [
+                ((members, half, w_in.shape[3]), low),
+                ((members, w_out.shape[2], half), low),
+                ((expert_count, features), jnp.float32),
+            ],
+        )
+        grad_parts = bring_back(layer, list(found[:groups]))
+        if last:
+            parts = bring_back(layer, list(found[groups : 2 * groups]))
+        grad_in, grad_out = [
+            lax.all_to_all(piece, ("row", "col"), split_axis=0, concat_axis=0, tiled=True)
+            for piece in found[-3:-1]
+        ]
+        saved = kept[layer]
+        height = -(-(4 * strip + expert_count + 4) // 16) * 16
+        grad, branch, blocks = run_kernel(
+            functools.partial(attention_backward_kernel, rows),
+            place,
+            [saved[6], norms[layer], saved[0], saved[1], saved[2], saved[3], saved[4], grad]
+            + [found[-1]]
+            + grad_parts,
+            [
+                ((padded, features), jnp.float32),
+                token_block,
+                ((members, height, half), low),
+            ],
+            [pltpu.VMEM((padded, 3 * features), low), pltpu.VMEM((padded, features), low)],
+        )
+        blocks = lax.all_to_all(blocks, ("row", "col"), split_axis=0, concat_axis=0, tiled=True)
+        shared = lax.psum(jnp.sum(blocks.astype(jnp.float32), axis=0), "dp")
+        results[layer] = (grad_in, grad_out, shared)
+        if layer > 0:
+            branches = send_out(layer - 1, branch)
+    for part in parts:
+        stream = stream + part.astype(jnp.float32)
+
+    def split(values):
+        pieces = values[:SEQ].reshape(SEQ, 2, half)
+        mine = lax.dynamic_index_in_dim(pieces, at_col, 1, keepdims=False)
+        other = exchange(lax.dynamic_index_in_dim(pieces, 1 - at_col, 1, keepdims=False), "col", 1)
+        return jnp.where(
+            at_col == 0,
+            jnp.concatenate([mine, other], axis=0),
+            jnp.concatenate([other, mine], axis=0),
+        )
+
+    output = split(stream.astype(low))
+    grad_input = split(grad)
+    ordered = [results[layer] for layer in range(layer_count)]
+    grad_in = jnp.stack([found[0] for found in ordered]).astype(jnp.float32)
+    grad_out = jnp.stack([found[1] for found in ordered]).astype(jnp.float32)
+    shared = jnp.stack([found[2] for found in ordered])
+    grad_qkv = (
+        shared[:, : 3 * strip].reshape(layer_count, 3, strip, half).transpose(0, 3, 1, 2)
+    )
+    grad_proj = shared[:, 3 * strip : 4 * strip]
+    grad_router = shared[:, 4 * strip : 4 * strip + expert_count].transpose(0, 2, 1)
+    tail = shared[:, 4 * strip + expert_count : 4 * strip + expert_count + 4]
+    return (
+        output,
+        grad_input,
+        grad_qkv,
+        grad_proj,
+        grad_router,
+        grad_in,
+        grad_out,
+        tail[:, :2],
+        tail[:, 2:],
+    )
+
+
+def fits_groups(mesh, tokens, w_in):
+    groups, rows, sides = mesh.shape["dp"], mesh.shape["row"], mesh.shape["col"]
+    powers = all(size & (size - 1) == 0 for size in (groups, rows))
+    return (
+        sides == 2
+        and powers
+        and tokens.shape[0] == groups * rows * sides * SEQ
+        and w_in.shape[1] == groups * rows * sides
+    )
+
+
 def solution(mesh):
     in_specs = (
         P(("dp", "row"), "col"),
@@ -387,6 +967,15 @@
         P(None, None, "col"),
         P(None, None, "col"),
     )
-    return jax.shard_map(
-        per_device, mesh=mesh, in_specs=in_specs, out_specs=out_specs, check_vma=False
-    )
+
+    def program(*arguments):
+        fits = fits_groups(mesh, arguments[0], arguments[6])
+        return jax.shard_map(
+            group_device if fits else per_device,
+            mesh=mesh,
+            in_specs=in_specs,
+            out_specs=out_specs,
+            check_vma=False,
+        )(*arguments)
+
+    return program

time: 2350 us -> 630 us (0.27)
  waiting for transfers between devices: 1110 us -> 275 us
  blocking collectives: 522 us -> 29.8 us
  local copies, waits for them, and re-layouts: 382 us -> 83.7 us
  matrix products: 146 us -> 0 us
  other arithmetic: 128 us -> 22.3 us
  starting transfers between devices: 32.3 us -> 127 us
  Pallas kernels: 0 us -> 69.4 us
    reduce_scatter x8 -> x0, waiting for transfers between devices: 1060 us -> none  [the longest x2 559 us: per_device(): lax.psum_scatter(grad_w_in, 'dp', scatter_dimension=0, tiled=True)]
    unnamed x11 -> x0, blocking collectives: 281 us -> none
    ppermute x0 -> x98, waiting for transfers between devices: none -> 189 us  [exchange(): lax.ppermute(values, axis, [(place, place ^ offset) for place in range(co...]
    gather x14 -> x2, local copies, waits for them, and re-layouts: 151 us -> 1.18 us  [the longest x1 0.59 us: group_device(): jnp.take(expert_ids.reshape(layer_count, members, SEQ, -1), images, axis=1)]
    dot_general x42 -> x0, matrix products: 146 us -> none  [the longest x2 23.5 us: expert_backward(): jnp.einsum('ecf,ecd->efd', active_all, grad_slot, preferred_element_type=...]
    psum x11 -> x0, blocking collectives: 129 us -> none  [the longest x2 65.5 us: expert_backward(): grad_gates = lax.psum(gate_part, ('row', 'col'))]
    all_gather x10 -> x0, blocking collectives: 111 us -> none  [the longest x8 107 us: gather_rows(): return lax.all_gather(values, 'row', axis=0, tiled=True)]
    reshape x23 -> x8, local copies, waits for them, and re-layouts: 89.2 us -> 1.91 us  [the longest x1 1.15 us: group_device(): shared[:, :3 * strip].reshape(layer_count, 3, strip, half)]
  transfers between devices with their start and end apart: 29 -> 108, of which waited for: 19 -> 46; matrix products, arithmetic and copies ran while one was open for 16% -> 9% of each run, Pallas kernels for 0% -> 9%
where the time goes in v1:
time: 630 us; the launch traced here: 622 us
  waiting for transfers between devices  275 us (44%)
  starting transfers between devices  127 us (20%)
  local copies, waits for them, and re-layouts  83.7 us (13%)
  Pallas kernels  69.4 us (11%)
  blocking collectives  29.8 us (5%)
  other arithmetic  22.3 us (4%)
  between operations  15.4 us (2%)
    ppermute x98, waiting for transfers between devices, exchange(): lax.ppermute(values, axis, [(place, place ^ offset) for place in range(co...  189 us
    ppermute x98, starting transfers between devices, exchange(): lax.ppermute(values, axis, [(place, place ^ offset) for place in range(co...  85.3 us
    pallas_call x15, Pallas kernels, run_kernel(): pl.pallas_call(body, in_specs=specs, out_specs=[LOCAL] * len(results), ou...  69.4 us
    psum x1, waiting for transfers between devices, group_device(): shared = lax.psum(jnp.sum(blocks.astype(jnp.float32), axis=0), 'dp')  38.5 us
    unnamed x194, local copies, waits for them, and re-layouts  35.4 us
    all_to_all x4, waiting for transfers between devices, group_device(): lax.all_to_all(local, ('row', 'col'), split_axis=0, concat_axis=0, tiled=...  34.1 us
    all_to_all x1, blocking collectives, group_device(): lax.all_to_all(piece, ('row', 'col'), split_axis=0, concat_axis=0, tiled=...  29.8 us
    slice x2, local copies, waits for them, and re-layouts, group_device(): local = lax.dynamic_slice_in_dim(source[layer], at_dp * members, members, 0)  20.6 us
  transfers between devices with their start and end apart: 108, of which 46 were waited for; matrix products, arithmetic and copies ran while one was open for 9% of the time, Pallas kernels for 9%

profile of v1, /device:TPU:0, one launch (start us, length us, event | category | flops | bytes accessed | tf_op | source)
XLA Modules:
  0.0 622.3 jit_solution(2831854759115209363)
XLA Ops:
  7.2 11.6 %fusion.9 = (bf16[1,32,256,512]{3,2,1,0:T(8,128)(2,1)}, bf16[1,32,256,512]{3,2,1,0:T(8,128)(2,1)}) fusion(bf16[2,32,256,512]{3,2,1,0:T(8,128)(2,1)} %param.19), kind=kLoop, calls=%fused_computation.59 | loop fusion | bytes 33554432 | tf_op jit(solution)/shard_map/slice | solution.py:774
  21.9 5.3 all-to-all-start.2
  37.3 17.1 %all-to-all-done.2.win_ref = bf16[8,256,512]{2,1,0:T(8,128)(2,1)S(1)} async-done(((bf16[8,256,512]{2,1,0:T(8,128)(2,1)}), bf16[8,256,512]{2,1,0:T(8,128)(2,1)S(1)}, u32[]{:S(2)}, u32[]{:S(2)}) %all-to-all-start.2) | async-done | bytes 2097184 | tf_op jit(solution)/shard_map/all_to_all | solution.py:776
  55.7 3.6 all-to-all-start
  60.1 9.0 %fusion.8 = (bf16[1,32,512,256]{3,2,1,0:T(8,128)(2,1)}, bf16[1,32,512,256]{3,2,1,0:T(8,128)(2,1)S(1)}) fusion(bf16[2,32,512,256]{3,2,1,0:T(8,128)(2,1)} %param.20), kind=kLoop, calls=%fused_computation.58 | loop fusion | bytes 33554432 | tf_op jit(solution)/shard_map/slice | solution.py:774
  70.6 17.0 %all-to-all-done.win_ref = bf16[8,256,512]{2,1,0:T(8,128)(2,1)S(1)} async-done(((bf16[8,256,512]{2,1,0:T(8,128)(2,1)}), bf16[8,256,512]{2,1,0:T(8,128)(2,1)S(1)}, u32[]{:S(2)}, u32[]{:S(2)}) %all-to-all-start) | async-done | bytes 2097184 | tf_op jit(solution)/shard_map/all_to_all | solution.py:776
  87.6 4.3 all-to-all-start.1
  102.8 4.4 shard_map.178
  118.7 4.9 collective-permute-done.18.refs_3_
  123.6 4.0 collective-permute-done.17.refs_2_
  128.2 4.5 all-to-all-start.3
  149.4 3.8 collective-permute-done.25.refs_3_
  153.2 4.7 shard_map.180
  161.6 3.7 collective-permute-done.2.refs_3_
  165.3 3.6 collective-permute-start.28
  189.1 8.1 %collective-permute-done.34.refs_12_ = bf16[208,512]{1,0:T(8,128)(2,1)S(1)} collective-permute-done((bf16[208,512]{1,0:T(8,128)(2,1)S(1)}, bf16[208,512]{1,0:T(8,128)(2,1)S(1)}, u32[]{:S(2)}, u32[]{:S(2)}) %collective-permute-start.34) | collective-permute-done | bytes 213024 | tf_op jit(solution)/shard_map/ppermute | solution.py:371
  197.2 5.0 shard_map.182
  208.6 5.0 collective-permute-done.38.refs_3_
  213.6 4.1 collective-permute-done.37.refs_2_
  231.1 4.5 collective-permute-done.54.refs_6_
  235.7 11.2 %collective-permute-done.44.refs_2_ = bf16[128,512]{1,0:T(8,128)(2,1)S(1)} collective-permute-done((bf16[128,512]{1,0:T(8,128)(2,1)S(1)}, bf16[128,512]{1,0:T(8,128)(2,1)S(1)}, u32[]{:S(2)}, u32[]{:S(2)}) %collective-permute-start.44) | collective-permute-done | bytes 131104 | tf_op jit(solution)/shard_map/ppermute | solution.py:371
  246.9 12.1 %shard_map.185 = (bf16[128,512]{1,0:T(8,128)(2,1)}, bf16[128,512]{1,0:T(8,128)(2,1)S(1)}, bf16[128,512]{1,0:T(8,128)(2,1)S(1)}, bf16[128,512]{1,0:T(8,128)(2,1)S...) custom-call(s32[4]{0:T(128)S(1)} %copy-done.62, ...), custom_call_target="tpu_custom_call" | custom-call | tf_op jit(solution)/shard_map/pallas_call | solution.py:682
  259.1 29.8 %all_to_all.50 = bf16[8,256,512]{2,1,0:T(8,128)(2,1)} all-to-all(bf16[8,256,512]{2,1,0:T(8,128)(2,1)S(1)} %get-tuple-element.153), channel_id=1, replica_groups=mesh['dp'=4,'row'=4,'col'=2] {'row','col'}, dimensions={0} | all-to-all | bytes 4194304 | tf_op jit(solution)/shard_map/all_to_all | solution.py:873
  288.9 4.9 all-to-all-start.9
  298.6 3.8 collective-permute-done.67.refs_1_
  302.4 6.8 %collective-permute-done.68.refs_2_ = bf16[128,512]{1,0:T(8,128)(2,1)} collective-permute-done((bf16[128,512]{1,0:T(8,128)(2,1)S(1)}, bf16[128,512]{1,0:T(8,128)(2,1)}, u32[]{:S(2)}, u32[]{:S(2)}) %collective-permute-start.68) | collective-permute-done | bytes 131104 | tf_op jit(solution)/shard_map/ppermute | solution.py:371
  317.8 6.7 %collective-permute-done.74.refs_10_ = bf16[208,512]{1,0:T(8,128)(2,1)S(1)} collective-permute-done((bf16[208,512]{1,0:T(8,128)(2,1)S(1)}, bf16[208,512]{1,0:T(8,128)(2,1)S(1)}, u32[]{:S(2)}, u32[]{:S(2)}) %collective-permute-start.74) | collective-permute-done | bytes 213024 | tf_op jit(solution)/shard_map/ppermute | solution.py:371
  325.4 4.1 collective-permute-done.76.refs_12_
  336.7 7.7 %shard_map.188 = (f32[208,512]{1,0:T(8,128)S(1)}, bf16[208,512]{1,0:T(8,128)(2,1)S(1)}, bf16[8,560,256]{2,1,0:T(8,128)(2,1)}) custom-call(s32[4]{0:T(128)S(1)} %copy-done.63, bf16[512,2048]{1,0:T(8,128)(2,1)S(1)} %copy-done.2, f32[4,512]{1,0:T(4,128)S(1)} %copy-done.55, f32[208,512]{1,0:T(8,128)S(1)} %copy-done.18, f32[208,512]{1,0:T(8,128)S(1)} %copy-done.7, ...), custom_call_target="tpu_custom_call" | custom-call | tf_op jit(solution)/shard_map/pallas_call | solution.py:682
  345.9 4.7 all-to-all-start.5
  354.2 30.1 %collective-permute-done.79.refs_3_ = bf16[208,512]{1,0:T(8,128)(2,1)S(1)} collective-permute-done((bf16[208,512]{1,0:T(8,128)(2,1)S(1)}, bf16[208,512]{1,0:T(8,128)(2,1)S(1)}, u32[]{:S(2)}, u32[]{:S(2)}) %collective-permute-start.79) | collective-permute-done | bytes 213024 | tf_op jit(solution)/shard_map/ppermute | solution.py:371
  398.4 7.2 %collective-permute-done.85.refs_6_ = bf16[128,512]{1,0:T(8,128)(2,1)S(1)} collective-permute-done((bf16[128,512]{1,0:T(8,128)(2,1)S(1)}, bf16[128,512]{1,0:T(8,128)(2,1)S(1)}, u32[]{:S(2)}, u32[]{:S(2)}) %collective-permute-start.85) | collective-permute-done | bytes 131104 | tf_op jit(solution)/shard_map/ppermute | solution.py:371
  405.6 11.0 %shard_map.190 = (bf16[128,512]{1,0:T(8,128)(2,1)S(1)}, bf16[128,512]{1,0:T(8,128)(2,1)S(1)}, bf16[128,512]{1,0:T(8,128)(2,1)S(1)}, bf16[128,512]{1,0:T(8,128)(2...) custom-call(s32[4]{0:T(128)S(1)} %copy-done.64, ...), custom_call_target="tpu_custom_call" | custom-call | tf_op jit(solution)/shard_map/pallas_call | solution.py:682
  421.2 4.8 all-to-all-start.8
  430.9 3.9 collective-permute-done.87.refs_1_
  434.8 6.8 %collective-permute-done.88.refs_2_ = bf16[128,512]{1,0:T(8,128)(2,1)S(1)} collective-permute-done((bf16[128,512]{1,0:T(8,128)(2,1)}, bf16[128,512]{1,0:T(8,128)(2,1)S(1)}, u32[]{:S(2)}, u32[]{:S(2)}) %collective-permute-start.88) | collective-permute-done | bytes 131104 | tf_op jit(solution)/shard_map/ppermute | solution.py:371
  448.7 8.0 %collective-permute-done.94.refs_10_ = bf16[208,512]{1,0:T(8,128)(2,1)S(1)} collective-permute-done((bf16[208,512]{1,0:T(8,128)(2,1)S(1)}, bf16[208,512]{1,0:T(8,128)(2,1)S(1)}, u32[]{:S(2)}, u32[]{:S(2)}) %collective-permute-start.94) | collective-permute-done | bytes 213024 | tf_op jit(solution)/shard_map/ppermute | solution.py:371
  457.6 4.2 collective-permute-done.96.refs_12_
  467.6 7.7 %shard_map.192 = (f32[208,512]{1,0:T(8,128)S(1)}, bf16[208,512]{1,0:T(8,128)(2,1)}, bf16[8,560,256]{2,1,0:T(8,128)(2,1)}) custom-call(s32[4]{0:T(128)S(1)} %copy-done.65, bf16[512,2048]{1,0:T(8,128)(2,1)S(1)} %copy-done.1, f32[4,512]{1,0:T(4,128)S(1)} %copy-done.53, f32[208,512]{1,0:T(8,128)S(1)} %copy-done.16, f32[208,512]{1,0:T(8,128)S(1)} %copy-done.5, ...), custom_call_target="tpu_custom_call" | custom-call | tf_op jit(solution)/shard_map/pallas_call | solution.py:682
  476.1 4.5 all-to-all-start.4
  488.9 7.1 %collective-permute-done.57.refs_2_ = bf16[128,512]{1,0:T(8,128)(2,1)S(1)} collective-permute-done((bf16[128,512]{1,0:T(8,128)(2,1)S(1)}, bf16[128,512]{1,0:T(8,128)(2,1)S(1)}, u32[]{:S(2)}, u32[]{:S(2)}) %collective-permute-start.57) | collective-permute-done | bytes 131104 | tf_op jit(solution)/shard_map/ppermute | solution.py:371
  496.5 12.9 %all-to-all-done.4 = bf16[8,560,256]{2,1,0:T(8,128)(2,1)} async-done(((bf16[8,560,256]{2,1,0:T(8,128)(2,1)}), bf16[8,560,256]{2,1,0:T(8,128)(2,1)}, u32[]{:S(2)}, u32[]{:S(2)}) %all-to-all-start.4) | async-done | bytes 2293792 | tf_op jit(solution)/shard_map/all_to_all | solution.py:891
  509.4 4.5 all-to-all-start.6
  519.8 24.8 %collective-permute-done.63 = bf16[208,512]{1,0:T(8,128)(2,1)S(1)} collective-permute-done((bf16[208,512]{1,0:T(8,128)(2,1)S(1)}, bf16[208,512]{1,0:T(8,128)(2,1)S(1)}, u32[]{:S(2)}, u32[]{:S(2)}) %collective-permute-start.63) | collective-permute-done | bytes 213024 | tf_op jit(solution)/shard_map/ppermute | solution.py:371
  544.6 5.0 collective-permute-done.65
  559.4 6.4 %maximum_convert_fusion.1 = f32[2,8,512,256]{3,2,1,0:T(8,128)} fusion(bf16[1,8,512,256]{3,2,1,0:T(8,128)(2,1)} %bitcast.50, bf16[1,8,512,256]{3,2,1,0:T(8,128)(2,1)} %bitcast.49), kind=kLoop, calls=%fused_computation.5 | loop fusion | flops 4194304 | bytes 12582912 | tf_op jit(solution)/shard_map/convert_element_type | solution.py:913
  565.8 5.5 maximum_convert_fusion
  571.3 38.5 %all-reduce.5.cloned.1.call-done = (f32[1,560,256]{2,1,0:T(8,128)}, f32[1,560,256]{2,1,0:T(8,128)}) async-done(((f32[1,560,256]{2,1,0:T(8,128)}, f32[1,560,256]{2,1,0:T(8,128)}), (f32[1,560,256]{2,1,0:T(8,128)}, f32[1,560,256]{2,1,0:T(8,128)})) %all-reduce.5.cloned.1.call-update) | async-done | bytes 1146896 | tf_op jit(solution)/shard_map/psum | solution.py:892
  (442 shorter events, 193.9 us)
Async XLA Ops:
  21.9 32.5 %all-to-all-start.2 = ((bf16[8,256,512]{2,1,0:T(8,128)(2,1)}), bf16[8,256,512]{2,1,0:T(8,128)(2,1)S(1)}, u32[]{:S(2)}, u32[]{:S(2)}) async-start(bf16[8,256,512]{2,1,0:T(8,128)(2,1)} %dynamic-slice_bitcast_fusion.1), calls=%async_computation.2 | async-start | bytes 4194304 | tf_op jit(solution)/shard_map/all_to_all | solution.py:776
  29.0 71.8 %collective-permute-start.11 = (bf16[256,512]{1,0:T(8,128)(2,1)S(1)}, bf16[256,512]{1,0:T(8,128)(2,1)S(1)}, u32[]{:S(2)}, u32[]{:S(2)}) collective-permute-start(bf16[256,512]{1,0:T(8,128)(2,1)S(1)} %maximum_maximum_fusion.1.refs_0_), channel_id=1, source_target_pairs={{0,1},{1,0},{2,3},{3,2},{4,5},{5,4},{6,7},{7,6},{8,9},{9,8},{10,11... | collective-permute-start | bytes 786440 | tf_op jit(solution)/shard_map/ppermute | solution.py:371
  29.5 69.8 %collective-permute-start.10 = (bf16[256,512]{1,0:T(8,128)(2,1)S(1)}, bf16[256,512]{1,0:T(8,128)(2,1)S(1)}, u32[]{:S(2)}, u32[]{:S(2)}) collective-permute-start(bf16[256,512]{1,0:T(8,128)(2,1)S(1)} %maximum_maximum_fusion.1.refs_0_), channel_id=1, source_target_pairs={{0,6},{2,4},{4,2},{6,0},{1,7},{3,5},{5,3},{7,1},{8,14},{10,12},{12... | collective-permute-start | bytes 786440 | tf_op jit(solution)/shard_map/ppermute | solution.py:371
  32.1 67.4 %collective-permute-start.9 = (bf16[256,512]{1,0:T(8,128)(2,1)S(1)}, bf16[256,512]{1,0:T(8,128)(2,1)}, u32[]{:S(2)}, u32[]{:S(2)}) collective-permute-start(bf16[256,512]{1,0:T(8,128)(2,1)S(1)} %maximum_maximum_fusion.1.refs_0_), channel_id=1, source_target_pairs={{0,4},{2,6},{4,0},{6,2},{1,5},{3,7},{5,1},{7,3},{8,12},{10,14},{12... | collective-permute-start | bytes 786440 | tf_op jit(solution)/shard_map/ppermute | solution.py:371
  32.6 67.2 %collective-permute-start.8 = (bf16[256,512]{1,0:T(8,128)(2,1)S(1)}, bf16[256,512]{1,0:T(8,128)(2,1)}, u32[]{:S(2)}, u32[]{:S(2)}) collective-permute-start(bf16[256,512]{1,0:T(8,128)(2,1)S(1)} %maximum_maximum_fusion.1.refs_0_), channel_id=1, source_target_pairs={{0,2},{2,0},{4,6},{6,4},{1,3},{3,1},{5,7},{7,5},{8,10},{10,8},{12,... | collective-permute-start | bytes 786440 | tf_op jit(solution)/shard_map/ppermute | solution.py:371
  33.1 64.2 %collective-permute-start.7 = (f32[72,256]{1,0:T(8,128)S(1)}, f32[72,256]{1,0:T(8,128)}, u32[]{:S(2)}, u32[]{:S(2)}) collective-permute-start(f32[72,256]{1,0:T(8,128)S(1)} %pad_maximum_fusion), channel_id=1, source_target_pairs={{0,1},{1,0},{2,3},{3,2},{4,5},{5,4},{6,7},{7,6},{8,9},{9,8},{10,11... | collective-permute-start | bytes 221192 | tf_op jit(solution)/shard_map/ppermute | solution.py:371
  55.7 31.9 %all-to-all-start = ((bf16[8,256,512]{2,1,0:T(8,128)(2,1)}), bf16[8,256,512]{2,1,0:T(8,128)(2,1)S(1)}, u32[]{:S(2)}, u32[]{:S(2)}) async-start(bf16[8,256,512]{2,1,0:T(8,128)(2,1)} %dynamic-slice_bitcast_fusion.3), calls=%async_computation | async-start | bytes 4194304 | tf_op jit(solution)/shard_map/all_to_all | solution.py:776
  87.6 40.5 %all-to-all-start.1 = ((bf16[8,512,256]{2,1,0:T(8,128)(2,1)}), bf16[8,512,256]{2,1,0:T(8,128)(2,1)}, u32[]{:S(2)}, u32[]{:S(2)}) async-start(bf16[8,512,256]{2,1,0:T(8,128)(2,1)} %dynamic-slice_bitcast_fusion.2), calls=%async_computation.1 | async-start | bytes 4194304 | tf_op jit(solution)/shard_map/all_to_all | solution.py:776
  110.1 13.4 %collective-permute-start.18 = (bf16[208,512]{1,0:T(8,128)(2,1)}, bf16[208,512]{1,0:T(8,128)(2,1)S(1)}, u32[]{:S(2)}, u32[]{:S(2)}) collective-permute-start(bf16[208,512]{1,0:T(8,128)(2,1)} %get-tuple-element.84.refs_0_), channel_id=1, source_target_pairs={{0,6},{2,4},{4,2},{6,0},{1,7},{3,5},{5,3},{7,1},{8,14},{10,12},{12... | collective-permute-start | bytes 638984 | tf_op jit(solution)/shard_map/ppermute | solution.py:371
  112.8 14.9 %collective-permute-start.17 = (bf16[208,512]{1,0:T(8,128)(2,1)}, bf16[208,512]{1,0:T(8,128)(2,1)S(1)}, u32[]{:S(2)}, u32[]{:S(2)}) collective-permute-start(bf16[208,512]{1,0:T(8,128)(2,1)} %get-tuple-element.84.refs_0_), channel_id=1, source_target_pairs={{0,4},{2,6},{4,0},{6,2},{1,5},{3,7},{5,1},{7,3},{8,12},{10,14},{12... | collective-permute-start | bytes 638984 | tf_op jit(solution)/shard_map/ppermute | solution.py:371
  113.3 14.4 %collective-permute-start.16 = (bf16[208,512]{1,0:T(8,128)(2,1)}, bf16[208,512]{1,0:T(8,128)(2,1)}, u32[]{:S(2)}, u32[]{:S(2)}) collective-permute-start(bf16[208,512]{1,0:T(8,128)(2,1)} %get-tuple-element.84.refs_0_), channel_id=1, source_target_pairs={{0,2},{2,0},{4,6},{6,4},{1,3},{3,1},{5,7},{7,5},{8,10},{10,8},{12,... | collective-permute-start | bytes 638984 | tf_op jit(solution)/shard_map/ppermute | solution.py:371
  118.7 14.0 %collective-permute-start.19 = (bf16[208,512]{1,0:T(8,128)(2,1)}, bf16[208,512]{1,0:T(8,128)(2,1)}, u32[]{:S(2)}, u32[]{:S(2)}) collective-permute-start(bf16[208,512]{1,0:T(8,128)(2,1)} %get-tuple-element.84.refs_0_), channel_id=1, source_target_pairs={{0,1},{1,0},{2,3},{3,2},{4,5},{5,4},{6,7},{7,6},{8,9},{9,8},{10,11... | collective-permute-start | bytes 638984 | tf_op jit(solution)/shard_map/ppermute | solution.py:371
  128.2 107.5 %all-to-all-start.3 = ((bf16[8,512,256]{2,1,0:T(8,128)(2,1)}), bf16[8,512,256]{2,1,0:T(8,128)(2,1)}, u32[]{:S(2)}, u32[]{:S(2)}) async-start(bf16[8,512,256]{2,1,0:T(8,128)(2,1)} %dynamic-slice_bitcast_fusion), calls=%async_computation.3 | async-start | bytes 4194304 | tf_op jit(solution)/shard_map/all_to_all | solution.py:776
  140.6 18.6 %collective-permute-start.3 = (bf16[256,512]{1,0:T(8,128)(2,1)S(1)}, bf16[256,512]{1,0:T(8,128)(2,1)S(1)}, u32[]{:S(2)}, u32[]{:S(2)}) collective-permute-start(bf16[256,512]{1,0:T(8,128)(2,1)S(1)} %maximum_maximum_fusion.refs_0_), channel_id=1, source_target_pairs={{0,1},{1,0},{2,3},{3,2},{4,5},{5,4},{6,7},{7,6},{8,9},{9,8},{10,11... | collective-permute-start | bytes 786440 | tf_op jit(solution)/shard_map/ppermute | solution.py:371
  140.7 24.6 %collective-permute-start.2 = (bf16[256,512]{1,0:T(8,128)(2,1)S(1)}, bf16[256,512]{1,0:T(8,128)(2,1)}, u32[]{:S(2)}, u32[]{:S(2)}) collective-permute-start(bf16[256,512]{1,0:T(8,128)(2,1)S(1)} %maximum_maximum_fusion.refs_0_), channel_id=1, source_target_pairs={{0,6},{2,4},{4,2},{6,0},{1,7},{3,5},{5,3},{7,1},{8,14},{10,12},{12... | collective-permute-start | bytes 786440 | tf_op jit(solution)/shard_map/ppermute | solution.py:371
  143.6 25.9 %collective-permute-start.1 = (bf16[256,512]{1,0:T(8,128)(2,1)S(1)}, bf16[256,512]{1,0:T(8,128)(2,1)}, u32[]{:S(2)}, u32[]{:S(2)}) collective-permute-start(bf16[256,512]{1,0:T(8,128)(2,1)S(1)} %maximum_maximum_fusion.refs_0_), channel_id=1, source_target_pairs={{0,4},{2,6},{4,0},{6,2},{1,5},{3,7},{5,1},{7,3},{8,12},{10,14},{12... | collective-permute-start | bytes 786440 | tf_op jit(solution)/shard_map/ppermute | solution.py:371
  144.1 28.0 %collective-permute-start = (bf16[256,512]{1,0:T(8,128)(2,1)S(1)}, bf16[256,512]{1,0:T(8,128)(2,1)}, u32[]{:S(2)}, u32[]{:S(2)}) collective-permute-start(bf16[256,512]{1,0:T(8,128)(2,1)S(1)} %maximum_maximum_fusion.refs_0_), channel_id=1, source_target_pairs={{0,2},{2,0},{4,6},{6,4},{1,3},{3,1},{5,7},{7,5},{8,10},{10,8},{12,... | collective-permute-start | bytes 786440 | tf_op jit(solution)/shard_map/ppermute | solution.py:371
  173.8 13.6 %collective-permute-start.5 = (bf16[256,512]{1,0:T(8,128)(2,1)}, bf16[256,512]{1,0:T(8,128)(2,1)S(1)}, u32[]{:S(2)}, u32[]{:S(2)}) collective-permute-start(bf16[256,512]{1,0:T(8,128)(2,1)} %collective-permute-done.1.refs_2_), channel_id=1, source_target_pairs={{0,1},{1,0},{2,3},{3,2},{4,5},{5,4},{6,7},{7,6},{8,9},{9,8},{10,11... | collective-permute-start | bytes 786440 | tf_op jit(solution)/shard_map/ppermute | solution.py:371
  175.0 12.5 %collective-permute-start.4 = (bf16[256,512]{1,0:T(8,128)(2,1)}, bf16[256,512]{1,0:T(8,128)(2,1)S(1)}, u32[]{:S(2)}, u32[]{:S(2)}) collective-permute-start(bf16[256,512]{1,0:T(8,128)(2,1)} %collective-permute-done.refs_1_), channel_id=1, source_target_pairs={{0,1},{1,0},{2,3},{3,2},{4,5},{5,4},{6,7},{7,6},{8,9},{9,8},{10,11... | collective-permute-start | bytes 786440 | tf_op jit(solution)/shard_map/ppermute | solution.py:371
  187.4 18.4 %collective-permute-start.49 = (bf16[208,512]{1,0:T(8,128)(2,1)S(1)}, bf16[208,512]{1,0:T(8,128)(2,1)S(1)}, u32[]{:S(2)}, u32[]{:S(2)}) collective-permute-start(bf16[208,512]{1,0:T(8,128)(2,1)S(1)} %get-tuple-element.166.refs_0_.refs_7_), channel_id=1, source_target_pairs={{0,1},{1,0},{2,3},{3,2},{4,5},{5,4},{6,7},{7,6},{8,9},{9,8},{10,11... | collective-permute-start | bytes 638984 | tf_op jit(solution)/shard_map/ppermute | solution.py:371
  187.4 19.2 %collective-permute-start.46 = (bf16[208,512]{1,0:T(8,128)(2,1)S(1)}, bf16[208,512]{1,0:T(8,128)(2,1)S(1)}, u32[]{:S(2)}, u32[]{:S(2)}) collective-permute-start(bf16[208,512]{1,0:T(8,128)(2,1)S(1)} %get-tuple-element.166.refs_0_.refs_7_), channel_id=1, source_target_pairs={{0,2},{2,0},{4,6},{6,4},{1,3},{3,1},{5,7},{7,5},{8,10},{10,8},{12,... | collective-permute-start | bytes 638984 | tf_op jit(solution)/shard_map/ppermute | solution.py:371
  188.9 19.1 %collective-permute-start.52 = (bf16[208,512]{1,0:T(8,128)(2,1)}, bf16[208,512]{1,0:T(8,128)(2,1)S(1)}, u32[]{:S(2)}, u32[]{:S(2)}) collective-permute-start(bf16[208,512]{1,0:T(8,128)(2,1)} %collective-permute-done.48.refs_3_), channel_id=1, source_target_pairs={{0,1},{1,0},{2,3},{3,2},{4,5},{5,4},{6,7},{7,6},{8,9},{9,8},{10,11... | collective-permute-start | bytes 638984 | tf_op jit(solution)/shard_map/ppermute | solution.py:371
  208.1 14.6 %collective-permute-start.39 = (bf16[208,512]{1,0:T(8,128)(2,1)S(1)}, bf16[208,512]{1,0:T(8,128)(2,1)S(1)}, u32[]{:S(2)}, u32[]{:S(2)}) collective-permute-start(bf16[208,512]{1,0:T(8,128)(2,1)S(1)} %get-tuple-element.98.refs_0_), channel_id=1, source_target_pairs={{0,1},{1,0},{2,3},{3,2},{4,5},{5,4},{6,7},{7,6},{8,9},{9,8},{10,11... | collective-permute-start | bytes 638984 | tf_op jit(solution)/shard_map/ppermute | solution.py:371
  222.7 13.0 %collective-permute-start.54 = (bf16[128,512]{1,0:T(8,128)(2,1)S(1)}, bf16[128,512]{1,0:T(8,128)(2,1)S(1)}, u32[]{:S(2)}, u32[]{:S(2)}) collective-permute-start(bf16[128,512]{1,0:T(8,128)(2,1)S(1)} %get-tuple-element.105), channel_id=1, source_target_pairs={{0,16},{8,24},{16,0},{24,8},{1,17},{9,25},{17,1},{25,9},{2,18},{10... | collective-permute-start | bytes 393224 | tf_op jit(solution)/shard_map/ppermute | solution.py:371
  227.7 19.1 %collective-permute-start.44 = (bf16[128,512]{1,0:T(8,128)(2,1)S(1)}, bf16[128,512]{1,0:T(8,128)(2,1)S(1)}, u32[]{:S(2)}, u32[]{:S(2)}) collective-permute-start(bf16[128,512]{1,0:T(8,128)(2,1)S(1)} %get-tuple-element.101), channel_id=1, source_target_pairs={{0,16},{8,24},{16,0},{24,8},{1,17},{9,25},{17,1},{25,9},{2,18},{10... | collective-permute-start | bytes 393224 | tf_op jit(solution)/shard_map/ppermute | solution.py:371
  229.9 17.0 %collective-permute-start.45 = (bf16[128,512]{1,0:T(8,128)(2,1)S(1)}, bf16[128,512]{1,0:T(8,128)(2,1)S(1)}, u32[]{:S(2)}, u32[]{:S(2)}) collective-permute-start(bf16[128,512]{1,0:T(8,128)(2,1)S(1)} %get-tuple-element.102), channel_id=1, source_target_pairs={{0,24},{8,16},{16,8},{24,0},{1,25},{9,17},{17,9},{25,1},{2,26},{10... | collective-permute-start | bytes 393224 | tf_op jit(solution)/shard_map/ppermute | solution.py:371
  288.9 56.9 %all-to-all-start.9 = ((bf16[8,512,256]{2,1,0:T(8,128)(2,1)}), bf16[8,512,256]{2,1,0:T(8,128)(2,1)}, u32[]{:S(2)}, u32[]{:S(2)}) async-start(bf16[8,512,256]{2,1,0:T(8,128)(2,1)} %get-tuple-element.155), calls=%async_computation.9 | async-start | bytes 4194304 | tf_op jit(solution)/shard_map/all_to_all | solution.py:873
  296.1 13.0 %collective-permute-start.68 = (bf16[128,512]{1,0:T(8,128)(2,1)S(1)}, bf16[128,512]{1,0:T(8,128)(2,1)}, u32[]{:S(2)}, u32[]{:S(2)}) collective-permute-start(bf16[128,512]{1,0:T(8,128)(2,1)S(1)} %copy-done.76), channel_id=1, source_target_pairs={{0,16},{8,24},{16,0},{24,8},{1,17},{9,25},{17,1},{25,9},{2,18},{10... | collective-permute-start | bytes 393224 | tf_op jit(solution)/shard_map/ppermute | solution.py:371
  345.9 75.3 %all-to-all-start.5 = ((bf16[8,560,256]{2,1,0:T(8,128)(2,1)}), bf16[8,560,256]{2,1,0:T(8,128)(2,1)}, u32[]{:S(2)}, u32[]{:S(2)}) async-start(bf16[8,560,256]{2,1,0:T(8,128)(2,1)} %get-tuple-element.151), calls=%async_computation.5 | async-start | bytes 4587520 | tf_op jit(solution)/shard_map/all_to_all | solution.py:891
  350.6 33.7 %collective-permute-start.79 = (bf16[208,512]{1,0:T(8,128)(2,1)S(1)}, bf16[208,512]{1,0:T(8,128)(2,1)S(1)}, u32[]{:S(2)}, u32[]{:S(2)}) collective-permute-start(bf16[208,512]{1,0:T(8,128)(2,1)S(1)} %copy-done.32), channel_id=1, source_target_pairs={{0,6},{2,4},{4,2},{6,0},{1,7},{3,5},{5,3},{7,1},{8,14},{10,12},{12... | collective-permute-start | bytes 638984 | tf_op jit(solution)/shard_map/ppermute | solution.py:371
  353.5 33.9 %collective-permute-start.78 = (bf16[208,512]{1,0:T(8,128)(2,1)S(1)}, bf16[208,512]{1,0:T(8,128)(2,1)S(1)}, u32[]{:S(2)}, u32[]{:S(2)}) collective-permute-start(bf16[208,512]{1,0:T(8,128)(2,1)S(1)} %copy-done.32), channel_id=1, source_target_pairs={{0,4},{2,6},{4,0},{6,2},{1,5},{3,7},{5,1},{7,3},{8,12},{10,14},{12... | collective-permute-start | bytes 638984 | tf_op jit(solution)/shard_map/ppermute | solution.py:371
  354.1 33.4 %collective-permute-start.77 = (bf16[208,512]{1,0:T(8,128)(2,1)S(1)}, bf16[208,512]{1,0:T(8,128)(2,1)S(1)}, u32[]{:S(2)}, u32[]{:S(2)}) collective-permute-start(bf16[208,512]{1,0:T(8,128)(2,1)S(1)} %copy-done.32), channel_id=1, source_target_pairs={{0,2},{2,0},{4,6},{6,4},{1,3},{3,1},{5,7},{7,5},{8,10},{10,8},{12,... | collective-permute-start | bytes 638984 | tf_op jit(solution)/shard_map/ppermute | solution.py:371
  354.2 33.7 %collective-permute-start.80 = (bf16[208,512]{1,0:T(8,128)(2,1)S(1)}, bf16[208,512]{1,0:T(8,128)(2,1)S(1)}, u32[]{:S(2)}, u32[]{:S(2)}) collective-permute-start(bf16[208,512]{1,0:T(8,128)(2,1)S(1)} %copy-done.32), channel_id=1, source_target_pairs={{0,1},{1,0},{2,3},{3,2},{4,5},{5,4},{6,7},{7,6},{8,9},{9,8},{10,11... | collective-permute-start | bytes 638984 | tf_op jit(solution)/shard_map/ppermute | solution.py:371
  392.7 12.9 %collective-permute-start.85 = (bf16[128,512]{1,0:T(8,128)(2,1)S(1)}, bf16[128,512]{1,0:T(8,128)(2,1)S(1)}, u32[]{:S(2)}, u32[]{:S(2)}) collective-permute-start(bf16[128,512]{1,0:T(8,128)(2,1)S(1)} %get-tuple-element.138), channel_id=1, source_target_pairs={{0,16},{8,24},{16,0},{24,8},{1,17},{9,25},{17,1},{25,9},{2,18},{10... | collective-permute-start | bytes 393224 | tf_op jit(solution)/shard_map/ppermute | solution.py:371
  421.2 54.9 %all-to-all-start.8 = ((bf16[8,512,256]{2,1,0:T(8,128)(2,1)}), bf16[8,512,256]{2,1,0:T(8,128)(2,1)}, u32[]{:S(2)}, u32[]{:S(2)}) async-start(bf16[8,512,256]{2,1,0:T(8,128)(2,1)} %copy-done.3), calls=%async_computation.8 | async-start | bytes 4194304 | tf_op jit(solution)/shard_map/all_to_all | solution.py:873
  428.5 13.1 %collective-permute-start.88 = (bf16[128,512]{1,0:T(8,128)(2,1)}, bf16[128,512]{1,0:T(8,128)(2,1)S(1)}, u32[]{:S(2)}, u32[]{:S(2)}) collective-permute-start(bf16[128,512]{1,0:T(8,128)(2,1)} %copy-done.77), channel_id=1, source_target_pairs={{0,16},{8,24},{16,0},{24,8},{1,17},{9,25},{17,1},{25,9},{2,18},{10... | collective-permute-start | bytes 393224 | tf_op jit(solution)/shard_map/ppermute | solution.py:371
  448.6 13.2 %collective-permute-start.96 = (bf16[208,512]{1,0:T(8,128)(2,1)S(1)}, bf16[208,512]{1,0:T(8,128)(2,1)S(1)}, u32[]{:S(2)}, u32[]{:S(2)}) collective-permute-start(bf16[208,512]{1,0:T(8,128)(2,1)S(1)} %get-tuple-element.148), channel_id=1, source_target_pairs={{0,6},{2,4},{4,2},{6,0},{1,7},{3,5},{5,3},{7,1},{8,14},{10,12},{12... | collective-permute-start | bytes 638984 | tf_op jit(solution)/shard_map/ppermute | solution.py:371
  476.1 33.3 %all-to-all-start.4 = ((bf16[8,560,256]{2,1,0:T(8,128)(2,1)}), bf16[8,560,256]{2,1,0:T(8,128)(2,1)}, u32[]{:S(2)}, u32[]{:S(2)}) async-start(bf16[8,560,256]{2,1,0:T(8,128)(2,1)} %get-tuple-element.150), calls=%async_computation.4 | async-start | bytes 4587520 | tf_op jit(solution)/shard_map/all_to_all | solution.py:891
  483.1 12.9 %collective-permute-start.57 = (bf16[128,512]{1,0:T(8,128)(2,1)S(1)}, bf16[128,512]{1,0:T(8,128)(2,1)S(1)}, u32[]{:S(2)}, u32[]{:S(2)}) collective-permute-start(bf16[128,512]{1,0:T(8,128)(2,1)S(1)} %copy-done.69), channel_id=1, source_target_pairs={{0,16},{8,24},{16,0},{24,8},{1,17},{9,25},{17,1},{25,9},{2,18},{10... | collective-permute-start | bytes 393224 | tf_op jit(solution)/shard_map/ppermute | solution.py:371
  485.5 28.7 %collective-permute-start.59 = (bf16[128,512]{1,0:T(8,128)(2,1)S(1)}, bf16[128,512]{1,0:T(8,128)(2,1)S(1)}, u32[]{:S(2)}, u32[]{:S(2)}) collective-permute-start(bf16[128,512]{1,0:T(8,128)(2,1)S(1)} %copy-done.43), channel_id=1, source_target_pairs={{0,1},{1,0},{2,3},{3,2},{4,5},{5,4},{6,7},{7,6},{8,9},{9,8},{10,11... | collective-permute-start | bytes 393224 | tf_op jit(solution)/shard_map/ppermute | solution.py:371
  488.9 25.3 %collective-permute-start.60 = (bf16[128,512]{1,0:T(8,128)(2,1)S(1)}, bf16[128,512]{1,0:T(8,128)(2,1)S(1)}, u32[]{:S(2)}, u32[]{:S(2)}) collective-permute-start(bf16[128,512]{1,0:T(8,128)(2,1)S(1)} %collective-permute-done.56.refs_1_), channel_id=1, source_target_pairs={{0,1},{1,0},{2,3},{3,2},{4,5},{5,4},{6,7},{7,6},{8,9},{9,8},{10,11... | collective-permute-start | bytes 393224 | tf_op jit(solution)/shard_map/ppermute | solution.py:371
  496.0 18.2 %collective-permute-start.61 = (bf16[128,512]{1,0:T(8,128)(2,1)S(1)}, bf16[128,512]{1,0:T(8,128)(2,1)S(1)}, u32[]{:S(2)}, u32[]{:S(2)}) collective-permute-start(bf16[128,512]{1,0:T(8,128)(2,1)S(1)} %collective-permute-done.57.refs_2_), channel_id=1, source_target_pairs={{0,1},{1,0},{2,3},{3,2},{4,5},{5,4},{6,7},{7,6},{8,9},{9,8},{10,11... | collective-permute-start | bytes 393224 | tf_op jit(solution)/shard_map/ppermute | solution.py:371
  496.0 18.2 %collective-permute-start.62 = (bf16[128,512]{1,0:T(8,128)(2,1)S(1)}, bf16[128,512]{1,0:T(8,128)(2,1)S(1)}, u32[]{:S(2)}, u32[]{:S(2)}) collective-permute-start(bf16[128,512]{1,0:T(8,128)(2,1)S(1)} %collective-permute-done.58.refs_3_), channel_id=1, source_target_pairs={{0,1},{1,0},{2,3},{3,2},{4,5},{5,4},{6,7},{7,6},{8,9},{9,8},{10,11... | collective-permute-start | bytes 393224 | tf_op jit(solution)/shard_map/ppermute | solution.py:371
  509.4 56.4 %all-to-all-start.6 = ((bf16[8,256,512]{2,1,0:T(8,128)(2,1)}), bf16[8,256,512]{2,1,0:T(8,128)(2,1)}, u32[]{:S(2)}, u32[]{:S(2)}) async-start(bf16[8,256,512]{2,1,0:T(8,128)(2,1)} %get-tuple-element.152), calls=%async_computation.6 | async-start | bytes 4194304 | tf_op jit(solution)/shard_map/all_to_all | solution.py:873
  513.9 95.9 %all-reduce.5.cloned.1.call-start = ((), (), s32[]{:S(2)}) async-start(), calls=%async_computation.10 | async-start | bytes 2293760 | tf_op jit(solution)/shard_map/psum | solution.py:892
  516.2 28.4 %collective-permute-start.63 = (bf16[208,512]{1,0:T(8,128)(2,1)S(1)}, bf16[208,512]{1,0:T(8,128)(2,1)S(1)}, u32[]{:S(2)}, u32[]{:S(2)}) collective-permute-start(bf16[208,512]{1,0:T(8,128)(2,1)S(1)} %get-tuple-element.112), channel_id=1, source_target_pairs={{0,2},{2,0},{4,6},{6,4},{1,3},{3,1},{5,7},{7,5},{8,10},{10,8},{12,... | collective-permute-start | bytes 638984 | tf_op jit(solution)/shard_map/ppermute | solution.py:371
  518.1 26.5 %collective-permute-start.64 = (bf16[208,512]{1,0:T(8,128)(2,1)S(1)}, bf16[208,512]{1,0:T(8,128)(2,1)S(1)}, u32[]{:S(2)}, u32[]{:S(2)}) collective-permute-start(bf16[208,512]{1,0:T(8,128)(2,1)S(1)} %get-tuple-element.113), channel_id=1, source_target_pairs={{0,4},{2,6},{4,0},{6,2},{1,5},{3,7},{5,1},{7,3},{8,12},{10,14},{12... | collective-permute-start | bytes 638984 | tf_op jit(solution)/shard_map/ppermute | solution.py:371
  519.6 30.0 %collective-permute-start.65 = (bf16[208,512]{1,0:T(8,128)(2,1)S(1)}, bf16[208,512]{1,0:T(8,128)(2,1)S(1)}, u32[]{:S(2)}, u32[]{:S(2)}) collective-permute-start(bf16[208,512]{1,0:T(8,128)(2,1)S(1)} %get-tuple-element.114), channel_id=1, source_target_pairs={{0,6},{2,4},{4,2},{6,0},{1,7},{3,5},{5,3},{7,1},{8,14},{10,12},{12... | collective-permute-start | bytes 638984 | tf_op jit(solution)/shard_map/ppermute | solution.py:371
  (153 other events, 1827.3 us)
Sparse Core Ops, SparseCore 0:
  555.9 53.9 all-reduce.4

commit v2 on v1

--- a/solution.py
+++ b/solution.py
@@ -431,22 +431,25 @@
 def attention_forward_kernel(rows, place_ref, *refs):
     block_refs = refs[: 2 * rows]
     norm_ref, stream_ref = refs[2 * rows : 2 * rows + 2]
-    part_refs = refs[2 * rows + 2 : -6]
     start_ref, middle_ref, first_ref, packed_ref, mixed_ref, second_ref, full_ref = refs[-7:]
     part_refs = refs[2 * rows + 2 : -7]
     features = stream_ref.shape[1]
     padded = stream_ref.shape[0]
     assemble_weights(place_ref, block_refs, full_ref, rows, features)
+    send(full_ref)
     stream = stream_ref[...].astype(jnp.float32)
     for part_ref in part_refs:
         stream = stream + part_ref[...].astype(jnp.float32)
     start_ref[...] = stream
+    send(start_ref)
     normal, _ = layer_norm_parts(stream)
     normed = (normal * norm_ref[0:1] + norm_ref[2:3]).astype(jnp.bfloat16)
     first_ref[...] = normed
+    send(first_ref)
     for part in range(3):
         columns = pl.ds(part * features, features)
         packed_ref[:, columns] = contract(normed, full_ref[:, columns], 1, 0).astype(jnp.bfloat16)
+    send(packed_ref)
     valid = lax.broadcasted_iota(jnp.int32, (padded, padded), 1) < SEQ
     lower = lax.broadcasted_iota(jnp.int32, (padded, 2 * HDIM), 1) < HDIM
     for pair in range(features // (2 * HDIM)):
@@ -461,8 +464,10 @@
         mixed_ref[:, pl.ds(pair * 2 * HDIM, 2 * HDIM)] = jnp.where(
             lower, results[0], results[1]
         ).astype(jnp.bfloat16)
+    send(mixed_ref)
     stream = stream + contract(mixed_ref[...], full_ref[:, pl.ds(3 * features, features)], 1, 0)
     middle_ref[...] = stream
+    send(middle_ref)
     normal, _ = layer_norm_parts(stream)
     second_ref[...] = (normal * norm_ref[1:2] + norm_ref[3:4]).astype(jnp.bfloat16)
 
@@ -536,27 +541,25 @@
             gain_two,
             shift_one,
             shift_two,
-            jnp.zeros((blocks_ref.shape[1] - 4 * strip - router_ref.shape[0] - 4, features), jnp.float32),
+            jnp.zeros((blocks_ref.shape[2] - 4 * strip - router_ref.shape[0] - 4, features), jnp.float32),
         ],
         axis=0,
     ).astype(jnp.bfloat16)
     grad_proj = contract(mixed_ref[...], grad_attn, 0, 0).astype(jnp.bfloat16)
     for offset in range(rows):
-        spot = lax.bitwise_xor(place_ref[1], offset) * 2
         for side in range(2):
             columns = slice(side * half, (side + 1) * half)
-            blocks_ref[spot + side, pl.ds(3 * strip, strip), :] = grad_proj[
+            blocks_ref[side, offset, pl.ds(3 * strip, strip), :] = grad_proj[
                 offset * strip : (offset + 1) * strip, columns
             ]
-            blocks_ref[spot + side, pl.ds(4 * strip, extra.shape[0]), :] = extra[:, columns]
+            blocks_ref[side, offset, pl.ds(4 * strip, extra.shape[0]), :] = extra[:, columns]
     for part in range(3):
         grad_part = contract(
             gpacked_ref[:, pl.ds(part * features, features)], first_ref[...], 0, 0
         ).astype(jnp.bfloat16)
         for offset in range(rows):
-            spot = lax.bitwise_xor(place_ref[1], offset) * 2
             for side in range(2):
-                blocks_ref[spot + side, pl.ds(part * strip, strip), :] = grad_part[
+                blocks_ref[side, offset, pl.ds(part * strip, strip), :] = grad_part[
                     offset * strip : (offset + 1) * strip, side * half : (side + 1) * half
                 ]
 
@@ -671,22 +674,121 @@
 
 SMALL = pl.BlockSpec(memory_space=pltpu.SMEM)
 LOCAL = pl.BlockSpec(memory_space=pltpu.VMEM)
-
-
-def run_kernel(body, place, operands, results, scratch=()):
-    specs = [LOCAL] * len(operands)
-    arguments = list(operands)
-    if place is not None:
-        specs = [SMALL] + specs
-        arguments = [place] + arguments
+FAR = pl.BlockSpec(memory_space=pltpu.HBM)
+
+
+def widen_kernel(narrow_ref, *refs):
+    refs[-1][0, 0] = narrow_ref[0].astype(jnp.float32)
+
+
+def widen_grads(layer, layer_count, narrow, previous):
+    members, *block = narrow.shape
+    anywhere = pl.BlockSpec(memory_space=pl.ANY)
     return pl.pallas_call(
-        body,
-        in_specs=specs,
-        out_specs=[LOCAL] * len(results),
-        out_shape=[jax.ShapeDtypeStruct(shape, kind) for shape, kind in results],
-        scratch_shapes=list(scratch),
-        compiler_params=pltpu.CompilerParams(vmem_limit_bytes=48 * 1024 * 1024),
+        widen_kernel,
+        name="widen",
+        grid=(members,),
+        in_specs=[pl.BlockSpec((1, *block), lambda step: (step, 0, 0))]
+        + [anywhere] * len(previous),
+        out_specs=pl.BlockSpec((1, 1, *block), lambda step: (layer, step, 0, 0)),
+        out_shape=jax.ShapeDtypeStruct((layer_count, members, *block), jnp.float32),
+        input_output_aliases={1: 0} if previous else {},
+        compiler_params=pltpu.CompilerParams(vmem_limit_bytes=4 * 1024 * 1024),
+    )(narrow, *previous)
+
+
+class Staged:
+    def __init__(self, ref, move=None):
+        self.ref, self.move = ref, move
+        self.shape, self.dtype = ref.shape, ref.dtype
+
+    def __getitem__(self, index):
+        if self.move is not None:
+            self.move.wait()
+            self.move = None
+        return self.ref[index]
+
+
+class Sent:
+    def __init__(self, ref, move):
+        self.ref, self.move, self.moving = ref, move, False
+        self.shape, self.dtype = ref.shape, ref.dtype
+
+    def __getitem__(self, index):
+        return self.ref[index]
+
+    def __setitem__(self, index, values):
+        self.ref[index] = values
+
+    def send(self):
+        if not self.moving:
+            self.move.start()
+            self.moving = True
+
+
+def send(ref):
+    if isinstance(ref, Sent):
+        ref.send()
+
+
+def staged_body(body, fixed_count, operand_count, far, *refs):
+    fixed, refs = refs[:fixed_count], refs[fixed_count:]
+    sources, refs = refs[:operand_count], refs[operand_count:]
+    targets, refs = list(refs[: len(far)]), refs[len(far) :]
+    copies, refs = refs[:operand_count], refs[operand_count:]
+    made, refs = refs[: sum(far)], refs[sum(far) :]
+    marks, scratch = refs[0], refs[1:]
+    staged = []
+    for place, (source, copy) in enumerate(zip(sources, copies)):
+        move = pltpu.make_async_copy(source, copy, marks.at[place])
+        move.start()
+        staged.append(Staged(copy, move))
+    made = list(made)
+    for place, apart in enumerate(far):
+        if apart:
+            near = made.pop(0)
+            move = pltpu.make_async_copy(near, targets[place], marks.at[operand_count + place])
+            targets[place] = Sent(near, move)
+    body(*fixed, *staged, *targets, *scratch)
+    for piece in staged:
+        if piece.move is not None:
+            piece.move.wait()
+    for target in targets:
+        if isinstance(target, Sent):
+            target.send()
+    for target in targets:
+        if isinstance(target, Sent):
+            target.move.wait()
+
+
+def run_kernel(title, body, place, operands, results, work, scratch=(), room=16, far=()):
+    fixed = [] if place is None else [place]
+    arguments = fixed + [pltpu.with_memory_space_constraint(piece, pltpu.HBM) for piece in operands]
+    apart = [place in far for place in range(len(results))]
+    return pl.pallas_call(
+        functools.partial(staged_body, body, len(fixed), len(operands), apart),
+        name=title,
+        in_specs=[SMALL] * len(fixed) + [FAR] * len(operands),
+        out_specs=[FAR if away else LOCAL for away in apart],
+        out_shape=[
+            pltpu.HBM(shape, kind) if away else jax.ShapeDtypeStruct(shape, kind)
+            for away, (shape, kind) in zip(apart, results)
+        ],
+        scratch_shapes=[pltpu.VMEM(piece.shape, piece.dtype) for piece in operands]
+        + [pltpu.VMEM(shape, kind) for away, (shape, kind) in zip(apart, results) if away]
+        + [pltpu.SemaphoreType.DMA((len(operands) + len(results),))]
+        + list(scratch),
+        compiler_params=pltpu.CompilerParams(vmem_limit_bytes=room * 1024 * 1024),
+        cost_estimate=pl.CostEstimate(
+            flops=work,
+            bytes_accessed=sum(piece.size * piece.dtype.itemsize for piece in arguments),
+            transcendentals=0,
+        ),
     )(*arguments)
+
+
+def after(values, *earlier):
+    return lax.optimization_barrier((values, *earlier))[0]
 
 
 def gather_group(values):
@@ -701,6 +803,36 @@
         piece if offset == 0 else exchange(piece, axis, offset)
         for offset, piece in enumerate(pieces)
     ]
+
+
+def add_pieces(pieces):
+    total = pieces[0].astype(jnp.float32)
+    for piece in pieces[1:]:
+        total = total + piece.astype(jnp.float32)
+    return total
+
+
+def sum_chip(blocks, at_col):
+    mine = lax.dynamic_index_in_dim(blocks, at_col, 0, keepdims=False)
+    other = exchange(lax.dynamic_index_in_dim(blocks, 1 - at_col, 0, keepdims=False), "col", 1)
+    return add_pieces([mine, other]).astype(blocks.dtype)
+
+
+def sum_groups(plane):
+    groups, at_dp = lax.axis_size("dp"), lax.axis_index("dp")
+    part = plane.shape[0] // groups
+    pieces = [
+        lax.dynamic_slice_in_dim(plane, (at_dp ^ offset) * part, part, 0)
+        for offset in range(groups)
+    ]
+    owned = add_pieces(scatter_pieces(pieces, "dp")).astype(plane.dtype)
+    result = jnp.zeros(plane.shape, jnp.float32)
+    for offset in range(groups):
+        piece = owned if offset == 0 else exchange(owned, "dp", offset)
+        result = lax.dynamic_update_slice_in_dim(
+            result, piece.astype(jnp.float32), (at_dp ^ offset) * part, 0
+        )
+    return result
 
 
 def group_device(
@@ -751,8 +883,7 @@
     other = exchange(lax.dynamic_index_in_dim(both, 1 - at_col, 1, keepdims=False), "col", 1)
     both = jnp.pad(join(mine, other), ((0, 0), (0, padded - SEQ), (0, 0)))
 
-    attention_blocks = []
-    for layer in range(layer_count):
+    def fetch_attention(layer, *earlier):
         block = jnp.concatenate(
             [
                 w_qkv[layer].reshape(half, -1),
@@ -766,15 +897,18 @@
             ],
             axis=1,
         )
-        attention_blocks.append(gather_group(block))
-
-    weights_in, weights_out = [], []
-    for layer in range(layer_count):
-        for store, source in ((weights_in, w_in), (weights_out, w_out)):
-            local = lax.dynamic_slice_in_dim(source[layer], at_dp * members, members, 0)
-            store.append(
-                lax.all_to_all(local, ("row", "col"), split_axis=0, concat_axis=0, tiled=True)
-            )
+        return gather_group(after(block, *earlier) if earlier else block)
+
+    def own_experts(layer, source):
+        own = lax.dynamic_slice(
+            source, (layer, at_dp * members, 0, 0), (1, members, *source.shape[2:])
+        )
+        return own[0]
+
+    def fetch_weights(own, *earlier):
+        return lax.all_to_all(
+            after(own, *earlier), ("row", "col"), split_axis=0, concat_axis=0, tiled=True
+        )
 
     capacity = 2 * ((5 * members * SEQ + 4 * expert_count - 1) // (4 * expert_count))
     room = -(-capacity // 16) * 16
@@ -800,35 +934,60 @@
     token_block = ((padded, features), low)
     slot_block = ((room, features), low)
 
-    def send_out(layer, values):
-        blocks = run_kernel(
+    def dispatch(layer, images):
+        return run_kernel(
+            "dispatch",
             functools.partial(dispatch_kernel, room),
             None,
-            [send_codes[layer]] + gather_group(values),
+            [send_codes[layer]] + images,
             [slot_block] * groups,
-        )
-        return scatter_pieces(blocks, "dp")
-
-    def bring_back(layer, blocks):
+            2 * members * padded * groups * room * features,
+        )
+
+    def bring_back(blocks):
         blocks = scatter_pieces(blocks, "dp")
-        blocks = blocks + [exchange(piece, "col", 1) for piece in blocks]
-        pieces = run_kernel(
+        return blocks + [exchange(piece, "col", 1) for piece in blocks]
+
+    def combine(layer, blocks):
+        return run_kernel(
+            "combine",
             functools.partial(combine_kernel, rows),
             None,
             [back_codes[layer]] + blocks,
             [token_block] * rows,
-        )
-        return scatter_pieces(pieces, "row")
-
+            4 * rows * padded * groups * room * features,
+        )
+
+    def split(values):
+        pieces = values[:SEQ].reshape(SEQ, 2, half)
+        mine = lax.dynamic_index_in_dim(pieces, at_col, 1, keepdims=False)
+        other = exchange(lax.dynamic_index_in_dim(pieces, 1 - at_col, 1, keepdims=False), "col", 1)
+        return jnp.where(
+            at_col == 0,
+            jnp.concatenate([mine, other], axis=0),
+            jnp.concatenate([other, mine], axis=0),
+        )
+
+    def after_all(pieces, *earlier):
+        return [after(piece, *earlier) for piece in pieces]
+
+    work = 4 * groups * room * members * half * w_in.shape[3]
     stream, parts = both[0], []
-    kept, buffers = [], []
-    branches = send_out(layer_count - 1, both[1])
-    grad_parts = None
+    kept, buffers, weights = [], [], []
+    attention_blocks = fetch_attention(0)
+    ready = attention_blocks[1:rows]
     for layer in range(layer_count):
+        last = layer == layer_count - 1
+        weight_in = fetch_weights(own_experts(layer, w_in), *ready)
+        own_out = own_experts(layer, w_out)
+        upstream = []
+        if last:
+            upstream = gather_group(after(both[1], *parts[1:]))
         saved = run_kernel(
+            "attention_forward",
             functools.partial(attention_forward_kernel, rows),
             place,
-            attention_blocks[layer] + [norms[layer], stream] + parts,
+            attention_blocks + [norms[layer], stream] + parts,
             [
                 ((padded, features), jnp.float32),
                 ((padded, features), jnp.float32),
@@ -838,44 +997,62 @@
                 token_block,
                 ((features, 4 * features), low),
             ],
+            16 * padded * features * features,
+            far=(0, 1, 2, 3, 4, 6),
         )
         kept.append(saved)
-        buffer = send_out(layer, saved[5])
-        buffers.append(buffer)
         stream = saved[1]
-        if layer < layer_count - 1:
+        images = gather_group(saved[5])
+        weight_out = fetch_weights(own_out, *images[1:rows], *upstream[1:rows])
+        weights.append([weight_in, weight_out])
+        buffers.append(scatter_pieces(dispatch(layer, images), "dp"))
+        if last:
+            branches = scatter_pieces(dispatch(layer, upstream), "dp")
+        else:
             result = run_kernel(
+                "expert_forward",
                 functools.partial(expert_forward_kernel, groups),
                 place,
-                [routers[layer], weights_in[layer], weights_out[layer]] + buffer,
+                [routers[layer]] + weights[layer] + buffers[layer],
                 [slot_block] * groups,
+                work,
             )
-            parts = bring_back(layer, result)
+            ready = [result[0]]
+            attention_blocks = fetch_attention(layer + 1, result[0])
+            parts = scatter_pieces(combine(layer, bring_back(result)), "row")
     grad = both[1]
-    results = {}
+    shared = [None] * layer_count
+    grad_in, grad_out, sooner = [], [], []
     for layer in reversed(range(layer_count)):
         last = layer == layer_count - 1
         found = run_kernel(
+            "expert_full",
             functools.partial(expert_full_kernel, groups, last),
             place,
-            [routers[layer], weights_in[layer], weights_out[layer]] + buffers[layer] + branches,
+            [routers[layer]] + weights[layer] + buffers[layer] + branches,
             [slot_block] * (2 * groups if last else groups)
             + [
-                ((members, half, w_in.shape[3]), low),
-                ((members, w_out.shape[2], half), low),
+                (weights[layer][0].shape, low),
+                (weights[layer][1].shape, low),
                 ((expert_count, features), jnp.float32),
             ],
-        )
-        grad_parts = bring_back(layer, list(found[:groups]))
+            3 * work,
+            room=24,
+        )
+        blocks = bring_back(list(found[:groups]))
+        pieces = combine(layer, after_all(blocks, *grad_out, *sooner))
         if last:
-            parts = bring_back(layer, list(found[groups : 2 * groups]))
-        grad_in, grad_out = [
-            lax.all_to_all(piece, ("row", "col"), split_axis=0, concat_axis=0, tiled=True)
-            for piece in found[-3:-1]
-        ]
+            moved_in = fetch_weights(found[-3])
+            pieces = after_all(pieces, moved_in)
+        grad_parts = scatter_pieces(pieces, "row")
+        if not last:
+            moved_in = fetch_weights(found[-3], *grad_parts[1:])
+        if last:
+            outputs = bring_back(after_all(list(found[groups : 2 * groups]), pieces[0]))
         saved = kept[layer]
-        height = -(-(4 * strip + expert_count + 4) // 16) * 16
+        height = -(-(4 * strip + expert_count + 4) // (16 * groups)) * (16 * groups)
         grad, branch, blocks = run_kernel(
+            "attention_backward",
             functools.partial(attention_backward_kernel, rows),
             place,
             [saved[6], norms[layer], saved[0], saved[1], saved[2], saved[3], saved[4], grad]
@@ -884,34 +1061,39 @@
             [
                 ((padded, features), jnp.float32),
                 token_block,
-                ((members, height, half), low),
+                ((2, rows, height, half), low),
             ],
+            32 * padded * features * features,
             [pltpu.VMEM((padded, 3 * features), low), pltpu.VMEM((padded, features), low)],
         )
-        blocks = lax.all_to_all(blocks, ("row", "col"), split_axis=0, concat_axis=0, tiled=True)
-        shared = lax.psum(jnp.sum(blocks.astype(jnp.float32), axis=0), "dp")
-        results[layer] = (grad_in, grad_out, shared)
+        chip = sum_chip(blocks, at_col)
         if layer > 0:
-            branches = send_out(layer - 1, branch)
-    for part in parts:
-        stream = stream + part.astype(jnp.float32)
-
-    def split(values):
-        pieces = values[:SEQ].reshape(SEQ, 2, half)
-        mine = lax.dynamic_index_in_dim(pieces, at_col, 1, keepdims=False)
-        other = exchange(lax.dynamic_index_in_dim(pieces, 1 - at_col, 1, keepdims=False), "col", 1)
-        return jnp.where(
-            at_col == 0,
-            jnp.concatenate([mine, other], axis=0),
-            jnp.concatenate([other, mine], axis=0),
-        )
-
-    output = split(stream.astype(low))
+            images = gather_group(after(branch, *outputs) if last else branch)
+            moved_out = fetch_weights(found[-2], *images[1:rows])
+            grad_in = [widen_grads(layer, layer_count, moved_in, grad_in)]
+            branches = scatter_pieces(dispatch(layer - 1, images), "dp")
+            earlier = list(grad_in)
+            if last:
+                outputs = combine(layer, outputs)
+                earlier = earlier + list(outputs)
+                parts = scatter_pieces(after_all(outputs, moved_out), "row")
+            branches = after_all(branches, *earlier)
+            arrived = scatter_pieces(after_all(list(chip), moved_out), "row")
+            grad_out = [widen_grads(layer, layer_count, moved_out, grad_out)]
+            sooner = arrived[1:] + parts[1:]
+            for part in parts:
+                stream = stream + part.astype(jnp.float32)
+            parts = []
+        else:
+            grad_in = [widen_grads(layer, layer_count, moved_in, grad_in)]
+            arrived = scatter_pieces(after_all(list(chip), *shared[1:]), "row")
+            moved_out = fetch_weights(found[-2], *arrived[1:])
+            output = split(stream.astype(low))
+            arrived = after_all(arrived, *grad_in, output)
+            grad_out = [widen_grads(layer, layer_count, moved_out, grad_out)]
+        shared[layer] = sum_groups(add_pieces(arrived).astype(low))
     grad_input = split(grad)
-    ordered = [results[layer] for layer in range(layer_count)]
-    grad_in = jnp.stack([found[0] for found in ordered]).astype(jnp.float32)
-    grad_out = jnp.stack([found[1] for found in ordered]).astype(jnp.float32)
-    shared = jnp.stack([found[2] for found in ordered])
+    shared = jnp.stack(shared)
     grad_qkv = (
         shared[:, : 3 * strip].reshape(layer_count, 3, strip, half).transpose(0, 3, 1, 2)
     )
@@ -924,8 +1106,8 @@
         grad_qkv,
         grad_proj,
         grad_router,
-        grad_in,
-        grad_out,
+        grad_in[0],
+        grad_out[0],
         tail[:, :2],
         tail[:, 2:],
     )

time: 630 us -> 505 us (0.80)
  waiting for transfers between devices: 275 us -> 175 us
  Pallas kernels: 69.4 us -> 104 us
  blocking collectives: 29.8 us -> 0 us
  local copies, waits for them, and re-layouts: 83.7 us -> 59.8 us
  starting transfers between devices: 127 us -> 140 us
  between operations: 15.4 us -> 2.64 us
  other arithmetic: 22.3 us -> 13.7 us
    psum x1 -> x0, waiting for transfers between devices: 38.5 us -> none  [group_device(): shared = lax.psum(jnp.sum(blocks.astype(jnp.float32), axis=0), 'dp')]
    all_to_all x9 -> x8, waiting for transfers between devices: 47 us -> 8.51 us  [fetch_weights(): lax.all_to_all(after(own, *earlier), ('row', 'col'), split_axis=0, concat...]
    pallas_call x15 -> x19, Pallas kernels: 69.4 us -> 104 us  [the longest x15 87.3 us: run_kernel(): pl.pallas_call(functools.partial(staged_body, body, len(fixed), len(opera...]
    all_to_all x1 -> x0, blocking collectives: 29.8 us -> none  [group_device(): lax.all_to_all(piece, ('row', 'col'), split_axis=0, concat_axis=0, tiled=...]
    ppermute x98 -> x118, starting transfers between devices: 85.3 us -> 108 us  [exchange(): lax.ppermute(values, axis, [(place, place ^ offset) for place in range(co...]
    ppermute x98 -> x118, waiting for transfers between devices: 189 us -> 167 us  [exchange(): lax.ppermute(values, axis, [(place, place ^ offset) for place in range(co...]
    slice x9 -> x4, local copies, waits for them, and re-layouts: 24.1 us -> 2.02 us  [the longest x1 1.05 us: fetch_attention(): w_qkv[layer].reshape(half, -1)]
    squeeze x4 -> x8, local copies, waits for them, and re-layouts: 0.97 us -> 14.9 us  [the longest x2 9.24 us: own_experts(): return own[0]]
  transfers between devices with their start and end apart: 108 -> 126, of which waited for: 46 -> 49; matrix products, arithmetic and copies ran while one was open for 9% -> 8% of each run, Pallas kernels for 9% -> 16%
where the time goes in v2:
time: 505 us; the launch traced here: 496 us
  waiting for transfers between devices  175 us (35%)
  starting transfers between devices  140 us (28%)
  Pallas kernels  104 us (21%)
  local copies, waits for them, and re-layouts  59.8 us (12%)
  other arithmetic  13.7 us (3%)
    ppermute x118, waiting for transfers between devices, exchange(): lax.ppermute(values, axis, [(place, place ^ offset) for place in range(co...  167 us
    ppermute x118, starting transfers between devices, exchange(): lax.ppermute(values, axis, [(place, place ^ offset) for place in range(co...  108 us
    pallas_call x15, Pallas kernels, run_kernel(): pl.pallas_call(functools.partial(staged_body, body, len(fixed), len(opera...  87.3 us
    unnamed x257, local copies, waits for them, and re-layouts  33 us
    all_to_all x8, starting transfers between devices, fetch_weights(): lax.all_to_all(after(own, *earlier), ('row', 'col'), split_axis=0, concat...  32.1 us
    pallas_call x4, Pallas kernels, widen_grads(): pl.pallas_call(widen_kernel, name='widen', grid=(members,), in_specs=[pl....  16.8 us
  transfers between devices with their start and end apart: 126, of which 49 were waited for; matrix products, arithmetic and copies ran while one was open for 8% of the time, Pallas kernels for 16%

profile of v2, /device:TPU:0, one launch (start us, length us, event | category | flops | bytes accessed | tf_op | source)
XLA Modules:
  0.0 495.8 jit_solution(6848790383225573907)
XLA Ops:
  7.5 4.6 dynamic-slice_bitcast_fusion.1
  13.1 6.2 %collective-permute-done.2.refs_3_ = bf16[256,512]{1,0:T(8,128)(2,1)S(1)} collective-permute-done((bf16[256,512]{1,0:T(8,128)(2,1)S(1)}, bf16[256,512]{1,0:T(8,128)(2,1)S(1)}, u32[]{:S(2)}, u32[]{:S(2)}) %collective-permute-start.2) | collective-permute-done | bytes 262176 | tf_op jit(solution)/shard_map/ppermute | solution.py:371
  20.8 3.6 all-to-all-start
  31.5 5.0 %attention_forward.2 = (f32[208,512]{1,0:T(8,128)}, f32[208,512]{1,0:T(8,128)}, bf16[208,512]{1,0:T(8,128)(2,1)}, bf16[208,1536]{1,0:T(8,128)(2,1)}, bf16[208,51...) custom-call(s32[4]{0:T(128)S(1)} %pad_add_fusion.refs_0_, bf16[256,512]{1,0:T(8,128)(2,1)} %copy-done.37, ...), custom_call_target="tpu_custom_call" | custom-call | flops 872415232 | bytes 2318352 | tf_op jit(solution)/shard_map/attention_forward/pallas_call | solution.py:768
  40.2 4.6 dynamic-slice_bitcast_fusion
  44.8 10.3 %collective-permute-done.9.refs_2_ = bf16[208,512]{1,0:T(8,128)(2,1)S(1)} collective-permute-done((bf16[208,512]{1,0:T(8,128)(2,1)S(1)}, bf16[208,512]{1,0:T(8,128)(2,1)S(1)}, u32[]{:S(2)}, u32[]{:S(2)}) %collective-permute-start.9) | collective-permute-done | bytes 213024 | tf_op jit(solution)/shard_map/ppermute | solution.py:371
  55.1 5.0 %collective-permute-done.11.refs_4_ = bf16[208,512]{1,0:T(8,128)(2,1)S(1)} collective-permute-done((bf16[208,512]{1,0:T(8,128)(2,1)S(1)}, bf16[208,512]{1,0:T(8,128)(2,1)S(1)}, u32[]{:S(2)}, u32[]{:S(2)}) %collective-permute-start.11) | collective-permute-done | bytes 213024 | tf_op jit(solution)/shard_map/ppermute | solution.py:371
  62.2 4.4 all-to-all-start.1
  82.3 6.7 %collective-permute-done.17.refs_6_ = bf16[128,512]{1,0:T(8,128)(2,1)S(1)} collective-permute-done((bf16[128,512]{1,0:T(8,128)(2,1)S(1)}, bf16[128,512]{1,0:T(8,128)(2,1)S(1)}, u32[]{:S(2)}, u32[]{:S(2)}) %collective-permute-start.17) | collective-permute-done | bytes 131104 | tf_op jit(solution)/shard_map/ppermute | solution.py:371
  89.0 4.2 all-to-all-done.1.refs_3_
  93.2 6.9 %expert_forward.1 = (bf16[128,512]{1,0:T(8,128)(2,1)S(1)}, bf16[128,512]{1,0:T(8,128)(2,1)S(1)}, bf16[128,512]{1,0:T(8,128)(2,1)S(1)}, bf16[128,512]{1,0:T(8,128)(2,1)S(1)}) custom-call(s32[4]{0:T(128)S(1)} %pad_add_fusion.refs_0_, bf16[32,512]{1,0:T(8,128)(2,1)} %get-tuple-element.291.refs_1_, bf16[8,256,512]{2,1,0:T(8,128)(2,1)} %copy-done.26, ...), custom_call_target="tpu_custom_call" | custom-call | flops 2147483648 | bytes 4751376 | tf_op jit(solution)/shard_map/expert_forward/pallas_call | solution.py:768
  100.1 3.8 all-to-all-start.2
  112.2 6.4 %collective-permute-done.27.refs_3_ = bf16[128,512]{1,0:T(8,128)(2,1)} collective-permute-done((bf16[128,512]{1,0:T(8,128)(2,1)S(1)}, bf16[128,512]{1,0:T(8,128)(2,1)}, u32[]{:S(2)}, u32[]{:S(2)}) %collective-permute-start.27) | collective-permute-done | bytes 131104 | tf_op jit(solution)/shard_map/ppermute | solution.py:371
  123.7 3.5 combine.4
  131.3 4.4 collective-permute-done.19.refs_2_
  137.2 5.1 %collective-permute-done.21.refs_4_ = bf16[256,512]{1,0:T(8,128)(2,1)S(1)} collective-permute-done((bf16[256,512]{1,0:T(8,128)(2,1)S(1)}, bf16[256,512]{1,0:T(8,128)(2,1)S(1)}, u32[]{:S(2)}, u32[]{:S(2)}) %collective-permute-start.21) | collective-permute-done | bytes 262176 | tf_op jit(solution)/shard_map/ppermute | solution.py:371
  142.3 3.6 collective-permute-done.33.refs_12_
  146.4 4.5 collective-permute-done.35.refs_14_
  155.3 5.4 %attention_forward.3 = (f32[208,512]{1,0:T(8,128)}, f32[208,512]{1,0:T(8,128)}, bf16[208,512]{1,0:T(8,128)(2,1)}, bf16[208,1536]{1,0:T(8,128)(2,1)}, bf16[208,51...) custom-call(s32[4]{0:T(128)S(1)} %pad_add_fusion.refs_0_, bf16[256,512]{1,0:T(8,128)(2,1)} %copy-done.29, ...), custom_call_target="tpu_custom_call" | custom-call | flops 872415232 | bytes 3383312 | tf_op jit(solution)/shard_map/attention_forward/pallas_call | solution.py:768
  164.2 4.8 collective-permute-done.36.refs_2_
  173.9 4.8 all-to-all-start.3
  202.4 8.6 %collective-permute-done.47.refs_6_ = bf16[128,512]{1,0:T(8,128)(2,1)S(1)} collective-permute-done((bf16[128,512]{1,0:T(8,128)(2,1)S(1)}, bf16[128,512]{1,0:T(8,128)(2,1)S(1)}, u32[]{:S(2)}, u32[]{:S(2)}) %collective-permute-start.47) | collective-permute-done | bytes 131104 | tf_op jit(solution)/shard_map/ppermute | solution.py:371
  211.7 13.1 %expert_full.2 = (bf16[128,512]{1,0:T(8,128)(2,1)S(1)}, bf16[128,512]{1,0:T(8,128)(2,1)S(1)}, bf16[128,512]{1,0:T(8,128)(2,1)S(1)}, bf16[128,512]{1,0:T(8,128)(2...) custom-call(s32[4]{0:T(128)S(1)} %pad_add_fusion.refs_0_, ...), custom_call_target="tpu_custom_call" | custom-call | flops 6442450944 | bytes 5275664 | tf_op jit(solution)/shard_map/expert_full/pallas_call | solution.py:768
  228.2 4.0 all-to-all-start.4
  236.9 4.0 collective-permute-done.56.refs_2_
  240.9 6.5 %collective-permute-done.57.refs_3_ = bf16[128,512]{1,0:T(8,128)(2,1)S(1)} collective-permute-done((bf16[128,512]{1,0:T(8,128)(2,1)S(1)}, bf16[128,512]{1,0:T(8,128)(2,1)S(1)}, u32[]{:S(2)}, u32[]{:S(2)}) %collective-permute-start.57) | collective-permute-done | bytes 131104 | tf_op jit(solution)/shard_map/ppermute | solution.py:371
  250.2 3.5 combine.5
  254.5 4.3 all-to-all-done.4.narrow_ref
  267.1 8.0 %collective-permute-done.64.refs_3_ = bf16[128,512]{1,0:T(8,128)(2,1)S(1)} collective-permute-done((bf16[128,512]{1,0:T(8,128)(2,1)S(1)}, bf16[128,512]{1,0:T(8,128)(2,1)S(1)}, u32[]{:S(2)}, u32[]{:S(2)}) %collective-permute-start.64) | collective-permute-done | bytes 131104 | tf_op jit(solution)/shard_map/ppermute | solution.py:371
  276.8 9.9 %attention_backward.2 = (f32[208,512]{1,0:T(8,128)S(1)}, bf16[208,512]{1,0:T(8,128)(2,1)S(1)}, bf16[2,4,576,256]{3,2,1,0:T(8,128)(2,1)S(1)}) custom-call(s32[4]{0:T(128)S(1)} %pad_add_fusion.refs_0_, bf16[512,2048]{1,0:T(8,128)(2,1)} %get-tuple-element.176.refs_1_, f32[4,512]{1,0:T(4,128)} %get-tuple-element.284.refs_9_.refs_2_, ...), custom_call_target="tpu_custom_call" | custom-call | flops 1744830464 | bytes 5152784 | tf_op jit(solution)/shard_map/attention_backward/pallas_call | solution.py:768
  292.4 4.6 collective-permute-done.73.refs_2_
  297.0 4.5 collective-permute-done.74.refs_3_
  301.5 4.4 all-to-all-start.5
  321.3 3.7 widen.4.refs_0_
  325.0 3.5 combine.6
  333.1 12.0 %expert_full.3 = (bf16[128,512]{1,0:T(8,128)(2,1)S(1)}, bf16[128,512]{1,0:T(8,128)(2,1)S(1)}, bf16[128,512]{1,0:T(8,128)(2,1)S(1)}, bf16[128,512]{1,0:T(8,128)(2...) custom-call(s32[4]{0:T(128)S(1)} %pad_add_fusion.refs_0_, ...), custom_call_target="tpu_custom_call" | custom-call | flops 6442450944 | bytes 5275664 | tf_op jit(solution)/shard_map/expert_full/pallas_call | solution.py:768
  356.3 5.9 %collective-permute-done.92.refs_3_ = bf16[128,512]{1,0:T(8,128)(2,1)} collective-permute-done((bf16[128,512]{1,0:T(8,128)(2,1)S(1)}, bf16[128,512]{1,0:T(8,128)(2,1)}, u32[]{:S(2)}, u32[]{:S(2)}) %collective-permute-start.92) | collective-permute-done | bytes 131104 | tf_op jit(solution)/shard_map/ppermute | solution.py:371
  365.7 6.9 %collective-permute-done.77 = bf16[208,512]{1,0:T(8,128)(2,1)S(1)} collective-permute-done((bf16[208,512]{1,0:T(8,128)(2,1)S(1)}, bf16[208,512]{1,0:T(8,128)(2,1)S(1)}, u32[]{:S(2)}, u32[]{:S(2)}) %collective-permute-start.77) | collective-permute-done | bytes 213024 | tf_op jit(solution)/shard_map/ppermute | solution.py:371
  373.6 6.2 %widen.5.refs_0_ = f32[2,8,512,256]{3,2,1,0:T(8,128)} custom-call(bf16[8,512,256]{2,1,0:T(8,128)(2,1)} %all-to-all-done.5.narrow_ref), custom_call_target="tpu_custom_call" | custom-call | tf_op jit(solution)/shard_map/widen/pallas_call | solution.py:687
  393.7 4.6 collective-permute-done.99.refs_12_
  399.1 10.0 %attention_backward.3 = (f32[208,512]{1,0:T(8,128)S(1)}, bf16[208,512]{1,0:T(8,128)(2,1)}, bf16[2,4,576,256]{3,2,1,0:T(8,128)(2,1)S(1)}) custom-call(s32[4]{0:T(128)S(1)} %pad_add_fusion.refs_0_, bf16[512,2048]{1,0:T(8,128)(2,1)} %get-tuple-element.198.refs_1_, f32[4,512]{1,0:T(4,128)} %get-tuple-element.285.refs_9_.refs_2_, ...), custom_call_target="tpu_custom_call" | custom-call | flops 1744830464 | bytes 5365776 | tf_op jit(solution)/shard_map/attention_backward/pallas_call | solution.py:768
  412.7 3.6 all-to-all-start.6
  423.0 4.3 collective-permute-done.107
  438.4 11.4 %collective-permute-done.111 = bf16[576,256]{1,0:T(8,128)(2,1)} collective-permute-done((bf16[576,256]{1,0:T(8,128)(2,1)}, bf16[576,256]{1,0:T(8,128)(2,1)}, u32[]{:S(2)}, u32[]{:S(2)}) %collective-permute-start.111) | collective-permute-done | bytes 294944 | tf_op jit(solution)/shard_map/ppermute | solution.py:371
  449.8 4.8 collective-permute-done.110
  456.1 3.6 all-to-all-start.7
  473.1 3.6 collective-permute-done.113
  482.1 3.8 collective-permute-done.116
  (554 shorter events, 222.0 us)
Async XLA Ops:
  6.0 13.4 %collective-permute-start.2 = (bf16[256,512]{1,0:T(8,128)(2,1)S(1)}, bf16[256,512]{1,0:T(8,128)(2,1)S(1)}, u32[]{:S(2)}, u32[]{:S(2)}) collective-permute-start(bf16[256,512]{1,0:T(8,128)(2,1)S(1)} %maximum_maximum_fusion.1.refs_1_), channel_id=1, source_target_pairs={{0,4},{2,6},{4,0},{6,2},{1,5},{3,7},{5,1},{7,3},{8,12},{10,14},{12... | collective-permute-start | bytes 786440 | tf_op jit(solution)/shard_map/ppermute | solution.py:371
  20.8 40.1 %all-to-all-start = ((bf16[8,256,512]{2,1,0:T(8,128)(2,1)}), bf16[8,256,512]{2,1,0:T(8,128)(2,1)S(1)}, u32[]{:S(2)}, u32[]{:S(2)}) async-start(bf16[8,256,512]{2,1,0:T(8,128)(2,1)} %get-tuple-element.129), calls=%async_computation | async-start | bytes 4194304 | tf_op jit(solution)/shard_map/all_to_all | solution.py:909
  36.6 18.5 %collective-permute-start.9 = (bf16[208,512]{1,0:T(8,128)(2,1)S(1)}, bf16[208,512]{1,0:T(8,128)(2,1)S(1)}, u32[]{:S(2)}, u32[]{:S(2)}) collective-permute-start(bf16[208,512]{1,0:T(8,128)(2,1)S(1)} %get-tuple-element.130.refs_1_), channel_id=1, source_target_pairs={{0,2},{2,0},{4,6},{6,4},{1,3},{3,1},{5,7},{7,5},{8,10},{10,8},{12,... | collective-permute-start | bytes 638984 | tf_op jit(solution)/shard_map/ppermute | solution.py:371
  38.6 16.6 %collective-permute-start.10 = (bf16[208,512]{1,0:T(8,128)(2,1)S(1)}, bf16[208,512]{1,0:T(8,128)(2,1)S(1)}, u32[]{:S(2)}, u32[]{:S(2)}) collective-permute-start(bf16[208,512]{1,0:T(8,128)(2,1)S(1)} %get-tuple-element.130.refs_1_), channel_id=1, source_target_pairs={{0,4},{2,6},{4,0},{6,2},{1,5},{3,7},{5,1},{7,3},{8,12},{10,14},{12... | collective-permute-start | bytes 638984 | tf_op jit(solution)/shard_map/ppermute | solution.py:371
  40.0 20.1 %collective-permute-start.11 = (bf16[208,512]{1,0:T(8,128)(2,1)S(1)}, bf16[208,512]{1,0:T(8,128)(2,1)S(1)}, u32[]{:S(2)}, u32[]{:S(2)}) collective-permute-start(bf16[208,512]{1,0:T(8,128)(2,1)S(1)} %get-tuple-element.130.refs_1_), channel_id=1, source_target_pairs={{0,6},{2,4},{4,2},{6,0},{1,7},{3,5},{5,3},{7,1},{8,14},{10,12},{12... | collective-permute-start | bytes 638984 | tf_op jit(solution)/shard_map/ppermute | solution.py:371
  62.2 31.0 %all-to-all-start.1 = ((bf16[8,512,256]{2,1,0:T(8,128)(2,1)}), bf16[8,512,256]{2,1,0:T(8,128)(2,1)}, u32[]{:S(2)}, u32[]{:S(2)}) async-start(bf16[8,512,256]{2,1,0:T(8,128)(2,1)} %get-tuple-element.131), calls=%async_computation.1 | async-start | bytes 4194304 | tf_op jit(solution)/shard_map/all_to_all | solution.py:909
  76.1 12.9 %collective-permute-start.17 = (bf16[128,512]{1,0:T(8,128)(2,1)S(1)}, bf16[128,512]{1,0:T(8,128)(2,1)S(1)}, u32[]{:S(2)}, u32[]{:S(2)}) collective-permute-start(bf16[128,512]{1,0:T(8,128)(2,1)S(1)} %get-tuple-element.134), channel_id=1, source_target_pairs={{0,16},{8,24},{16,0},{24,8},{1,17},{9,25},{17,1},{25,9},{2,18},{10... | collective-permute-start | bytes 393224 | tf_op jit(solution)/shard_map/ppermute | solution.py:371
  100.1 72.5 %all-to-all-start.2 = ((bf16[8,256,512]{2,1,0:T(8,128)(2,1)}), bf16[8,256,512]{2,1,0:T(8,128)(2,1)S(1)}, u32[]{:S(2)}, u32[]{:S(2)}) async-start(bf16[8,256,512]{2,1,0:T(8,128)(2,1)} %get-tuple-element.147), calls=%async_computation.2 | async-start | bytes 4194304 | tf_op jit(solution)/shard_map/all_to_all | solution.py:909
  105.6 13.0 %collective-permute-start.27 = (bf16[128,512]{1,0:T(8,128)(2,1)S(1)}, bf16[128,512]{1,0:T(8,128)(2,1)}, u32[]{:S(2)}, u32[]{:S(2)}) collective-permute-start(bf16[128,512]{1,0:T(8,128)(2,1)S(1)} %get-tuple-element.140), channel_id=1, source_target_pairs={{0,16},{8,24},{16,0},{24,8},{1,17},{9,25},{17,1},{25,9},{2,18},{10... | collective-permute-start | bytes 393224 | tf_op jit(solution)/shard_map/ppermute | solution.py:371
  108.7 13.4 %collective-permute-start.29 = (bf16[128,512]{1,0:T(8,128)(2,1)S(1)}, bf16[128,512]{1,0:T(8,128)(2,1)}, u32[]{:S(2)}, u32[]{:S(2)}) collective-permute-start(bf16[128,512]{1,0:T(8,128)(2,1)S(1)} %get-tuple-element.136.refs_1_), channel_id=1, source_target_pairs={{0,1},{1,0},{2,3},{3,2},{4,5},{5,4},{6,7},{7,6},{8,9},{9,8},{10,11... | collective-permute-start | bytes 393224 | tf_op jit(solution)/shard_map/ppermute | solution.py:371
  119.1 16.5 %collective-permute-start.19 = (bf16[256,512]{1,0:T(8,128)(2,1)S(1)}, bf16[256,512]{1,0:T(8,128)(2,1)S(1)}, u32[]{:S(2)}, u32[]{:S(2)}) collective-permute-start(bf16[256,512]{1,0:T(8,128)(2,1)S(1)} %maximum_maximum_fusion.refs_1_), channel_id=1, source_target_pairs={{0,2},{2,0},{4,6},{6,4},{1,3},{3,1},{5,7},{7,5},{8,10},{10,8},{12,... | collective-permute-start | bytes 786440 | tf_op jit(solution)/shard_map/ppermute | solution.py:371
  122.1 15.1 %collective-permute-start.20 = (bf16[256,512]{1,0:T(8,128)(2,1)S(1)}, bf16[256,512]{1,0:T(8,128)(2,1)S(1)}, u32[]{:S(2)}, u32[]{:S(2)}) collective-permute-start(bf16[256,512]{1,0:T(8,128)(2,1)S(1)} %maximum_maximum_fusion.refs_1_), channel_id=1, source_target_pairs={{0,4},{2,6},{4,0},{6,2},{1,5},{3,7},{5,1},{7,3},{8,12},{10,14},{12... | collective-permute-start | bytes 786440 | tf_op jit(solution)/shard_map/ppermute | solution.py:371
  123.6 18.7 %collective-permute-start.21 = (bf16[256,512]{1,0:T(8,128)(2,1)S(1)}, bf16[256,512]{1,0:T(8,128)(2,1)S(1)}, u32[]{:S(2)}, u32[]{:S(2)}) collective-permute-start(bf16[256,512]{1,0:T(8,128)(2,1)S(1)} %maximum_maximum_fusion.refs_1_), channel_id=1, source_target_pairs={{0,6},{2,4},{4,2},{6,0},{1,7},{3,5},{5,3},{7,1},{8,14},{10,12},{12... | collective-permute-start | bytes 786440 | tf_op jit(solution)/shard_map/ppermute | solution.py:371
  127.9 18.0 %collective-permute-start.33 = (bf16[208,512]{1,0:T(8,128)(2,1)S(1)}, bf16[208,512]{1,0:T(8,128)(2,1)S(1)}, u32[]{:S(2)}, u32[]{:S(2)}) collective-permute-start(bf16[208,512]{1,0:T(8,128)(2,1)S(1)} %get-tuple-element.143), channel_id=1, source_target_pairs={{0,2},{2,0},{4,6},{6,4},{1,3},{3,1},{5,7},{7,5},{8,10},{10,8},{12,... | collective-permute-start | bytes 638984 | tf_op jit(solution)/shard_map/ppermute | solution.py:371
  129.8 16.1 %collective-permute-start.34 = (bf16[208,512]{1,0:T(8,128)(2,1)S(1)}, bf16[208,512]{1,0:T(8,128)(2,1)S(1)}, u32[]{:S(2)}, u32[]{:S(2)}) collective-permute-start(bf16[208,512]{1,0:T(8,128)(2,1)S(1)} %get-tuple-element.144), channel_id=1, source_target_pairs={{0,4},{2,6},{4,0},{6,2},{1,5},{3,7},{5,1},{7,3},{8,12},{10,14},{12... | collective-permute-start | bytes 638984 | tf_op jit(solution)/shard_map/ppermute | solution.py:371
  135.7 15.3 %collective-permute-start.35 = (bf16[208,512]{1,0:T(8,128)(2,1)S(1)}, bf16[208,512]{1,0:T(8,128)(2,1)S(1)}, u32[]{:S(2)}, u32[]{:S(2)}) collective-permute-start(bf16[208,512]{1,0:T(8,128)(2,1)S(1)} %get-tuple-element.145), channel_id=1, source_target_pairs={{0,6},{2,4},{4,2},{6,0},{1,7},{3,5},{5,3},{7,1},{8,14},{10,12},{12... | collective-permute-start | bytes 638984 | tf_op jit(solution)/shard_map/ppermute | solution.py:371
  137.2 14.3 %collective-permute-start.22 = (bf16[256,512]{1,0:T(8,128)(2,1)S(1)}, bf16[256,512]{1,0:T(8,128)(2,1)S(1)}, u32[]{:S(2)}, u32[]{:S(2)}) collective-permute-start(bf16[256,512]{1,0:T(8,128)(2,1)S(1)} %maximum_maximum_fusion.refs_1_), channel_id=1, source_target_pairs={{0,1},{1,0},{2,3},{3,2},{4,5},{5,4},{6,7},{7,6},{8,9},{9,8},{10,11... | collective-permute-start | bytes 786440 | tf_op jit(solution)/shard_map/ppermute | solution.py:371
  151.5 12.7 %collective-permute-start.40 = (bf16[208,512]{1,0:T(8,128)(2,1)S(1)}, bf16[208,512]{1,0:T(8,128)(2,1)S(1)}, u32[]{:S(2)}, u32[]{:S(2)}) collective-permute-start(bf16[208,512]{1,0:T(8,128)(2,1)S(1)} %get-tuple-element.149.refs_1_.refs_8_), channel_id=1, source_target_pairs={{0,4},{2,6},{4,0},{6,2},{1,5},{3,7},{5,1},{7,3},{8,12},{10,14},{12... | collective-permute-start | bytes 638984 | tf_op jit(solution)/shard_map/ppermute | solution.py:371
  173.9 37.2 %all-to-all-start.3 = ((bf16[8,512,256]{2,1,0:T(8,128)(2,1)}), bf16[8,512,256]{2,1,0:T(8,128)(2,1)}, u32[]{:S(2)}, u32[]{:S(2)}) async-start(bf16[8,512,256]{2,1,0:T(8,128)(2,1)} %get-tuple-element.150), calls=%async_computation.3 | async-start | bytes 4194304 | tf_op jit(solution)/shard_map/all_to_all | solution.py:909
  185.3 13.3 %collective-permute-start.53 = (bf16[128,512]{1,0:T(8,128)(2,1)S(1)}, bf16[128,512]{1,0:T(8,128)(2,1)S(1)}, u32[]{:S(2)}, u32[]{:S(2)}) collective-permute-start(bf16[128,512]{1,0:T(8,128)(2,1)S(1)} %get-tuple-element.156), channel_id=1, source_target_pairs={{0,8},{8,0},{16,24},{24,16},{1,9},{9,1},{17,25},{25,17},{2,10},{10... | collective-permute-start | bytes 393224 | tf_op jit(solution)/shard_map/ppermute | solution.py:371
  186.8 13.0 %collective-permute-start.54 = (bf16[128,512]{1,0:T(8,128)(2,1)S(1)}, bf16[128,512]{1,0:T(8,128)(2,1)S(1)}, u32[]{:S(2)}, u32[]{:S(2)}) collective-permute-start(bf16[128,512]{1,0:T(8,128)(2,1)S(1)} %get-tuple-element.157), channel_id=1, source_target_pairs={{0,16},{8,24},{16,0},{24,8},{1,17},{9,25},{17,1},{25,9},{2,18},{10... | collective-permute-start | bytes 393224 | tf_op jit(solution)/shard_map/ppermute | solution.py:371
  195.1 15.9 %collective-permute-start.47 = (bf16[128,512]{1,0:T(8,128)(2,1)S(1)}, bf16[128,512]{1,0:T(8,128)(2,1)S(1)}, u32[]{:S(2)}, u32[]{:S(2)}) collective-permute-start(bf16[128,512]{1,0:T(8,128)(2,1)S(1)} %get-tuple-element.153), channel_id=1, source_target_pairs={{0,16},{8,24},{16,0},{24,8},{1,17},{9,25},{17,1},{25,9},{2,18},{10... | collective-permute-start | bytes 393224 | tf_op jit(solution)/shard_map/ppermute | solution.py:371
  228.2 30.6 %all-to-all-start.4 = ((bf16[8,256,512]{2,1,0:T(8,128)(2,1)}), bf16[8,256,512]{2,1,0:T(8,128)(2,1)S(1)}, u32[]{:S(2)}, u32[]{:S(2)}) async-start(bf16[8,256,512]{2,1,0:T(8,128)(2,1)} %copy-done.8), calls=%async_computation.4 | async-start | bytes 4194304 | tf_op jit(solution)/shard_map/all_to_all | solution.py:909
  234.5 12.9 %collective-permute-start.57 = (bf16[128,512]{1,0:T(8,128)(2,1)S(1)}, bf16[128,512]{1,0:T(8,128)(2,1)S(1)}, u32[]{:S(2)}, u32[]{:S(2)}) collective-permute-start(bf16[128,512]{1,0:T(8,128)(2,1)S(1)} %get-tuple-element.162), channel_id=1, source_target_pairs={{0,16},{8,24},{16,0},{24,8},{1,17},{9,25},{17,1},{25,9},{2,18},{10... | collective-permute-start | bytes 393224 | tf_op jit(solution)/shard_map/ppermute | solution.py:371
  261.1 14.5 %collective-permute-start.70 = (bf16[208,512]{1,0:T(8,128)(2,1)S(1)}, bf16[208,512]{1,0:T(8,128)(2,1)S(1)}, u32[]{:S(2)}, u32[]{:S(2)}) collective-permute-start(bf16[208,512]{1,0:T(8,128)(2,1)S(1)} %get-tuple-element.183), channel_id=1, source_target_pairs={{0,2},{2,0},{4,6},{6,4},{1,3},{3,1},{5,7},{7,5},{8,10},{10,8},{12,... | collective-permute-start | bytes 638984 | tf_op jit(solution)/shard_map/ppermute | solution.py:371
  261.6 14.1 %collective-permute-start.71 = (bf16[208,512]{1,0:T(8,128)(2,1)S(1)}, bf16[208,512]{1,0:T(8,128)(2,1)S(1)}, u32[]{:S(2)}, u32[]{:S(2)}) collective-permute-start(bf16[208,512]{1,0:T(8,128)(2,1)S(1)} %get-tuple-element.185), channel_id=1, source_target_pairs={{0,4},{2,6},{4,0},{6,2},{1,5},{3,7},{5,1},{7,3},{8,12},{10,14},{12... | collective-permute-start | bytes 638984 | tf_op jit(solution)/shard_map/ppermute | solution.py:371
  262.3 13.9 %collective-permute-start.72 = (bf16[208,512]{1,0:T(8,128)(2,1)S(1)}, bf16[208,512]{1,0:T(8,128)(2,1)S(1)}, u32[]{:S(2)}, u32[]{:S(2)}) collective-permute-start(bf16[208,512]{1,0:T(8,128)(2,1)S(1)} %get-tuple-element.187), channel_id=1, source_target_pairs={{0,6},{2,4},{4,2},{6,0},{1,7},{3,5},{5,3},{7,1},{8,14},{10,12},{12... | collective-permute-start | bytes 638984 | tf_op jit(solution)/shard_map/ppermute | solution.py:371
  275.1 13.0 %collective-permute-start.66 = (bf16[128,512]{1,0:T(8,128)(2,1)S(1)}, bf16[128,512]{1,0:T(8,128)(2,1)S(1)}, u32[]{:S(2)}, u32[]{:S(2)}) collective-permute-start(bf16[128,512]{1,0:T(8,128)(2,1)S(1)} %get-tuple-element.167.refs_1_), channel_id=1, source_target_pairs={{0,1},{1,0},{2,3},{3,2},{4,5},{5,4},{6,7},{7,6},{8,9},{9,8},{10,11... | collective-permute-start | bytes 393224 | tf_op jit(solution)/shard_map/ppermute | solution.py:371
  275.1 13.0 %collective-permute-start.67 = (bf16[128,512]{1,0:T(8,128)(2,1)S(1)}, bf16[128,512]{1,0:T(8,128)(2,1)S(1)}, u32[]{:S(2)}, u32[]{:S(2)}) collective-permute-start(bf16[128,512]{1,0:T(8,128)(2,1)S(1)} %collective-permute-done.63.refs_2_), channel_id=1, source_target_pairs={{0,1},{1,0},{2,3},{3,2},{4,5},{5,4},{6,7},{7,6},{8,9},{9,8},{10,11... | collective-permute-start | bytes 393224 | tf_op jit(solution)/shard_map/ppermute | solution.py:371
  275.6 12.5 %collective-permute-start.68 = (bf16[128,512]{1,0:T(8,128)(2,1)S(1)}, bf16[128,512]{1,0:T(8,128)(2,1)S(1)}, u32[]{:S(2)}, u32[]{:S(2)}) collective-permute-start(bf16[128,512]{1,0:T(8,128)(2,1)S(1)} %collective-permute-done.64.refs_3_), channel_id=1, source_target_pairs={{0,1},{1,0},{2,3},{3,2},{4,5},{5,4},{6,7},{7,6},{8,9},{9,8},{10,11... | collective-permute-start | bytes 393224 | tf_op jit(solution)/shard_map/ppermute | solution.py:371
  301.5 51.0 %all-to-all-start.5 = ((bf16[8,512,256]{2,1,0:T(8,128)(2,1)}), bf16[8,512,256]{2,1,0:T(8,128)(2,1)}, u32[]{:S(2)}, u32[]{:S(2)}) async-start(bf16[8,512,256]{2,1,0:T(8,128)(2,1)} %copy-done.7), calls=%async_computation.5 | async-start | bytes 4194304 | tf_op jit(solution)/shard_map/all_to_all | solution.py:909
  307.3 45.0 %collective-permute-start.87 = (bf16[4,576,256]{2,1,0:T(8,128)(2,1)S(1)}, bf16[4,576,256]{2,1,0:T(8,128)(2,1)S(1)}, u32[]{:S(2)}, u32[]{:S(2)}) collective-permute-start(bf16[4,576,256]{2,1,0:T(8,128)(2,1)S(1)} %dynamic-slice_bitcast_fusion.5), channel_id=1, source_target_pairs={{0,1},{1,0},{2,3},{3,2},{4,5},{5,4},{6,7},{7,6},{8,9},{9,8},{10,11... | collective-permute-start | bytes 3538952 | tf_op jit(solution)/shard_map/ppermute | solution.py:371
  315.8 12.7 %collective-permute-start.84 = (bf16[128,512]{1,0:T(8,128)(2,1)S(1)}, bf16[128,512]{1,0:T(8,128)(2,1)S(1)}, u32[]{:S(2)}, u32[]{:S(2)}) collective-permute-start(bf16[128,512]{1,0:T(8,128)(2,1)S(1)} %get-tuple-element.206), channel_id=1, source_target_pairs={{0,8},{8,0},{16,24},{24,16},{1,9},{9,1},{17,25},{25,17},{2,10},{10... | collective-permute-start | bytes 393224 | tf_op jit(solution)/shard_map/ppermute | solution.py:371
  318.9 12.9 %collective-permute-start.85 = (bf16[128,512]{1,0:T(8,128)(2,1)S(1)}, bf16[128,512]{1,0:T(8,128)(2,1)S(1)}, u32[]{:S(2)}, u32[]{:S(2)}) collective-permute-start(bf16[128,512]{1,0:T(8,128)(2,1)S(1)} %get-tuple-element.208), channel_id=1, source_target_pairs={{0,16},{8,24},{16,0},{24,8},{1,17},{9,25},{17,1},{25,9},{2,18},{10... | collective-permute-start | bytes 393224 | tf_op jit(solution)/shard_map/ppermute | solution.py:371
  350.7 13.0 %collective-permute-start.93 = (bf16[128,512]{1,0:T(8,128)(2,1)S(1)}, bf16[128,512]{1,0:T(8,128)(2,1)}, u32[]{:S(2)}, u32[]{:S(2)}) collective-permute-start(bf16[128,512]{1,0:T(8,128)(2,1)S(1)} %get-tuple-element.223), channel_id=1, source_target_pairs={{0,24},{8,16},{16,8},{24,0},{1,25},{9,17},{17,9},{25,1},{2,26},{10... | collective-permute-start | bytes 393224 | tf_op jit(solution)/shard_map/ppermute | solution.py:371
  352.6 12.6 %collective-permute-start.78 = (bf16[208,512]{1,0:T(8,128)(2,1)S(1)}, bf16[208,512]{1,0:T(8,128)(2,1)S(1)}, u32[]{:S(2)}, u32[]{:S(2)}) collective-permute-start(bf16[208,512]{1,0:T(8,128)(2,1)S(1)} %get-tuple-element.197), channel_id=1, source_target_pairs={{0,6},{2,4},{4,2},{6,0},{1,7},{3,5},{5,3},{7,1},{8,14},{10,12},{12... | collective-permute-start | bytes 638984 | tf_op jit(solution)/shard_map/ppermute | solution.py:371
  355.5 17.6 %collective-permute-start.88 = (bf16[576,256]{1,0:T(8,128)(2,1)S(1)}, bf16[576,256]{1,0:T(8,128)(2,1)S(1)}, u32[]{:S(2)}, u32[]{:S(2)}) collective-permute-start(bf16[576,256]{1,0:T(8,128)(2,1)S(1)} %get-tuple-element.215), channel_id=1, source_target_pairs={{0,2},{2,0},{4,6},{6,4},{1,3},{3,1},{5,7},{7,5},{8,10},{10,8},{12,... | collective-permute-start | bytes 884744 | tf_op jit(solution)/shard_map/ppermute | solution.py:371
  356.1 17.4 %collective-permute-start.89 = (bf16[576,256]{1,0:T(8,128)(2,1)S(1)}, bf16[576,256]{1,0:T(8,128)(2,1)S(1)}, u32[]{:S(2)}, u32[]{:S(2)}) collective-permute-start(bf16[576,256]{1,0:T(8,128)(2,1)S(1)} %get-tuple-element.216), channel_id=1, source_target_pairs={{0,4},{2,6},{4,0},{6,2},{1,5},{3,7},{5,1},{7,3},{8,12},{10,14},{12... | collective-permute-start | bytes 884744 | tf_op jit(solution)/shard_map/ppermute | solution.py:371
  365.2 14.7 %collective-permute-start.90 = (bf16[576,256]{1,0:T(8,128)(2,1)S(1)}, bf16[576,256]{1,0:T(8,128)(2,1)S(1)}, u32[]{:S(2)}, u32[]{:S(2)}) collective-permute-start(bf16[576,256]{1,0:T(8,128)(2,1)S(1)} %get-tuple-element.217), channel_id=1, source_target_pairs={{0,6},{2,4},{4,2},{6,0},{1,7},{3,5},{5,3},{7,1},{8,14},{10,12},{12... | collective-permute-start | bytes 884744 | tf_op jit(solution)/shard_map/ppermute | solution.py:371
  388.6 23.0 %collective-permute-start.105 = (bf16[144,256]{1,0:T(8,128)(2,1)S(1)}, bf16[144,256]{1,0:T(8,128)(2,1)S(1)}, u32[]{:S(2)}, u32[]{:S(2)}) collective-permute-start(bf16[144,256]{1,0:T(8,128)(2,1)S(1)} %get-tuple-element.280), channel_id=1, source_target_pairs={{0,24},{8,16},{16,8},{24,0},{1,25},{9,17},{17,9},{25,1},{2,26},{10... | collective-permute-start | bytes 221192 | tf_op jit(solution)/shard_map/ppermute | solution.py:371
  390.9 20.7 %collective-permute-start.104 = (bf16[144,256]{1,0:T(8,128)(2,1)S(1)}, bf16[144,256]{1,0:T(8,128)(2,1)S(1)}, u32[]{:S(2)}, u32[]{:S(2)}) collective-permute-start(bf16[144,256]{1,0:T(8,128)(2,1)S(1)} %get-tuple-element.281), channel_id=1, source_target_pairs={{0,16},{8,24},{16,0},{24,8},{1,17},{9,25},{17,1},{25,9},{2,18},{10... | collective-permute-start | bytes 221192 | tf_op jit(solution)/shard_map/ppermute | solution.py:371
  393.0 18.7 %collective-permute-start.103 = (bf16[144,256]{1,0:T(8,128)(2,1)S(1)}, bf16[144,256]{1,0:T(8,128)(2,1)S(1)}, u32[]{:S(2)}, u32[]{:S(2)}) collective-permute-start(bf16[144,256]{1,0:T(8,128)(2,1)S(1)} %get-tuple-element.279), channel_id=1, source_target_pairs={{0,8},{8,0},{16,24},{24,16},{1,9},{9,1},{17,25},{25,17},{2,10},{10... | collective-permute-start | bytes 221192 | tf_op jit(solution)/shard_map/ppermute | solution.py:371
  411.6 15.8 %collective-permute-start.102 = (bf16[4,576,256]{2,1,0:T(8,128)(2,1)}, bf16[4,576,256]{2,1,0:T(8,128)(2,1)}, u32[]{:S(2)}, u32[]{:S(2)}) collective-permute-start(bf16[4,576,256]{2,1,0:T(8,128)(2,1)} %dynamic-slice_bitcast_fusion.4), channel_id=1, source_target_pairs={{0,1},{1,0},{2,3},{3,2},{4,5},{5,4},{6,7},{7,6},{8,9},{9,8},{10,11... | collective-permute-start | bytes 3538952 | tf_op jit(solution)/shard_map/ppermute | solution.py:371
  412.7 42.1 %all-to-all-start.6 = ((bf16[8,256,512]{2,1,0:T(8,128)(2,1)}), bf16[8,256,512]{2,1,0:T(8,128)(2,1)S(1)}, u32[]{:S(2)}, u32[]{:S(2)}) async-start(bf16[8,256,512]{2,1,0:T(8,128)(2,1)} %copy-done.6), calls=%async_computation.6 | async-start | bytes 4194304 | tf_op jit(solution)/shard_map/all_to_all | solution.py:909
  430.3 19.5 %collective-permute-start.111 = (bf16[576,256]{1,0:T(8,128)(2,1)}, bf16[576,256]{1,0:T(8,128)(2,1)}, u32[]{:S(2)}, u32[]{:S(2)}) collective-permute-start(bf16[576,256]{1,0:T(8,128)(2,1)} %get-tuple-element.244), channel_id=1, source_target_pairs={{0,6},{2,4},{4,2},{6,0},{1,7},{3,5},{5,3},{7,1},{8,14},{10,12},{12... | collective-permute-start | bytes 884744 | tf_op jit(solution)/shard_map/ppermute | solution.py:371
  433.2 21.4 %collective-permute-start.110 = (bf16[576,256]{1,0:T(8,128)(2,1)}, bf16[576,256]{1,0:T(8,128)(2,1)}, u32[]{:S(2)}, u32[]{:S(2)}) collective-permute-start(bf16[576,256]{1,0:T(8,128)(2,1)} %get-tuple-element.242), channel_id=1, source_target_pairs={{0,4},{2,6},{4,0},{6,2},{1,5},{3,7},{5,1},{7,3},{8,12},{10,14},{12... | collective-permute-start | bytes 884744 | tf_op jit(solution)/shard_map/ppermute | solution.py:371
  433.8 21.0 %collective-permute-start.109 = (bf16[576,256]{1,0:T(8,128)(2,1)}, bf16[576,256]{1,0:T(8,128)(2,1)}, u32[]{:S(2)}, u32[]{:S(2)}) collective-permute-start(bf16[576,256]{1,0:T(8,128)(2,1)} %get-tuple-element.240), channel_id=1, source_target_pairs={{0,2},{2,0},{4,6},{6,4},{1,3},{3,1},{5,7},{7,5},{8,10},{10,8},{12,... | collective-permute-start | bytes 884744 | tf_op jit(solution)/shard_map/ppermute | solution.py:371
  456.1 35.8 %all-to-all-start.7 = ((bf16[8,512,256]{2,1,0:T(8,128)(2,1)}), bf16[8,512,256]{2,1,0:T(8,128)(2,1)S(1)}, u32[]{:S(2)}, u32[]{:S(2)}) async-start(bf16[8,512,256]{2,1,0:T(8,128)(2,1)} %copy-done.5), calls=%async_computation.7 | async-start | bytes 4194304 | tf_op jit(solution)/shard_map/all_to_all | solution.py:909
  (203 other events, 1499.9 us)

commit v3 on v2

--- a/solution.py
+++ b/solution.py
@@ -702,10 +702,13 @@
         self.ref, self.move = ref, move
         self.shape, self.dtype = ref.shape, ref.dtype
 
-    def __getitem__(self, index):
+    def wait(self):
         if self.move is not None:
             self.move.wait()
             self.move = None
+
+    def __getitem__(self, index):
+        self.wait()
         return self.ref[index]
 
 
@@ -731,50 +734,57 @@
         ref.send()
 
 
-def staged_body(body, fixed_count, operand_count, far, *refs):
+def staged_body(body, fixed_count, staged, far, *refs):
     fixed, refs = refs[:fixed_count], refs[fixed_count:]
-    sources, refs = refs[:operand_count], refs[operand_count:]
+    sources, refs = list(refs[: len(staged)]), refs[len(staged) :]
     targets, refs = list(refs[: len(far)]), refs[len(far) :]
-    copies, refs = refs[:operand_count], refs[operand_count:]
-    made, refs = refs[: sum(far)], refs[sum(far) :]
+    copies, refs = list(refs[: sum(staged)]), refs[sum(staged) :]
+    made, refs = list(refs[: sum(far)]), refs[sum(far) :]
     marks, scratch = refs[0], refs[1:]
-    staged = []
-    for place, (source, copy) in enumerate(zip(sources, copies)):
-        move = pltpu.make_async_copy(source, copy, marks.at[place])
-        move.start()
-        staged.append(Staged(copy, move))
-    made = list(made)
+    for place, moved in enumerate(staged):
+        if moved:
+            copy = copies.pop(0)
+            move = pltpu.make_async_copy(sources[place], copy, marks.at[place])
+            move.start()
+            sources[place] = Staged(copy, move)
     for place, apart in enumerate(far):
         if apart:
-            near = made.pop(0)
-            move = pltpu.make_async_copy(near, targets[place], marks.at[operand_count + place])
-            targets[place] = Sent(near, move)
-    body(*fixed, *staged, *targets, *scratch)
-    for piece in staged:
-        if piece.move is not None:
-            piece.move.wait()
+            source = made.pop(0)
+            move = pltpu.make_async_copy(source, targets[place], marks.at[len(staged) + place])
+            targets[place] = Sent(source, move)
+    body(*fixed, *sources, *targets, *scratch)
+    for source in sources:
+        if isinstance(source, Staged):
+            source.wait()
     for target in targets:
-        if isinstance(target, Sent):
-            target.send()
+        send(target)
     for target in targets:
         if isinstance(target, Sent):
             target.move.wait()
 
 
-def run_kernel(title, body, place, operands, results, work, scratch=(), room=16, far=()):
+def run_kernel(
+    title, body, place, operands, results, work, scratch=(), room=16, near=(), far=()
+):
     fixed = [] if place is None else [place]
-    arguments = fixed + [pltpu.with_memory_space_constraint(piece, pltpu.HBM) for piece in operands]
+    staged = [place not in near for place in range(len(operands))]
+    arguments = fixed + [
+        pltpu.with_memory_space_constraint(piece, pltpu.HBM) if moved else piece
+        for moved, piece in zip(staged, operands)
+    ]
     apart = [place in far for place in range(len(results))]
     return pl.pallas_call(
-        functools.partial(staged_body, body, len(fixed), len(operands), apart),
+        functools.partial(staged_body, body, len(fixed), staged, apart),
         name=title,
-        in_specs=[SMALL] * len(fixed) + [FAR] * len(operands),
+        in_specs=[SMALL] * len(fixed) + [FAR if moved else LOCAL for moved in staged],
         out_specs=[FAR if away else LOCAL for away in apart],
         out_shape=[
             pltpu.HBM(shape, kind) if away else jax.ShapeDtypeStruct(shape, kind)
             for away, (shape, kind) in zip(apart, results)
         ],
-        scratch_shapes=[pltpu.VMEM(piece.shape, piece.dtype) for piece in operands]
+        scratch_shapes=[
+            pltpu.VMEM(piece.shape, piece.dtype) for moved, piece in zip(staged, operands) if moved
+        ]
         + [pltpu.VMEM(shape, kind) for away, (shape, kind) in zip(apart, results) if away]
         + [pltpu.SemaphoreType.DMA((len(operands) + len(results),))]
         + list(scratch),
@@ -934,6 +944,9 @@
     token_block = ((padded, features), low)
     slot_block = ((room, features), low)
 
+    def after_all(pieces, *earlier):
+        return [after(piece, *earlier) for piece in pieces]
+
     def dispatch(layer, images):
         return run_kernel(
             "dispatch",
@@ -942,10 +955,11 @@
             [send_codes[layer]] + images,
             [slot_block] * groups,
             2 * members * padded * groups * room * features,
-        )
-
-    def bring_back(blocks):
-        blocks = scatter_pieces(blocks, "dp")
+            near=range(1, 1 + len(images)),
+        )
+
+    def bring_back(blocks, *earlier):
+        blocks = after_all(scatter_pieces(blocks, "dp"), *earlier)
         return blocks + [exchange(piece, "col", 1) for piece in blocks]
 
     def combine(layer, blocks):
@@ -967,9 +981,6 @@
             jnp.concatenate([mine, other], axis=0),
             jnp.concatenate([other, mine], axis=0),
         )
-
-    def after_all(pieces, *earlier):
-        return [after(piece, *earlier) for piece in pieces]
 
     work = 4 * groups * room * members * half * w_in.shape[3]
     stream, parts = both[0], []
@@ -1005,10 +1016,12 @@
         images = gather_group(saved[5])
         weight_out = fetch_weights(own_out, *images[1:rows], *upstream[1:rows])
         weights.append([weight_in, weight_out])
+        if last:
+            sent = dispatch(layer, upstream)
+            branches = scatter_pieces(sent, "dp")
+            images = after_all(images, sent[0])
         buffers.append(scatter_pieces(dispatch(layer, images), "dp"))
-        if last:
-            branches = scatter_pieces(dispatch(layer, upstream), "dp")
-        else:
+        if not last:
             result = run_kernel(
                 "expert_forward",
                 functools.partial(expert_forward_kernel, groups),
@@ -1022,7 +1035,7 @@
             parts = scatter_pieces(combine(layer, bring_back(result)), "row")
     grad = both[1]
     shared = [None] * layer_count
-    grad_in, grad_out, sooner = [], [], []
+    grad_in, grad_out = [], []
     for layer in reversed(range(layer_count)):
         last = layer == layer_count - 1
         found = run_kernel(
@@ -1039,16 +1052,25 @@
             3 * work,
             room=24,
         )
-        blocks = bring_back(list(found[:groups]))
-        pieces = combine(layer, after_all(blocks, *grad_out, *sooner))
         if last:
             moved_in = fetch_weights(found[-3])
-            pieces = after_all(pieces, moved_in)
-        grad_parts = scatter_pieces(pieces, "row")
-        if not last:
-            moved_in = fetch_weights(found[-3], *grad_parts[1:])
+            blocks = bring_back(list(found[:groups]))
+        else:
+            moved_in = fetch_weights(found[-3], moved_out)
+            moved_out = after(moved_out, found[0])
+            grad_out = [widen_grads(layer + 1, layer_count, moved_out, grad_out)]
+            blocks = bring_back(list(found[:groups]), *grad_out)
+        pieces = combine(layer, blocks)
         if last:
             outputs = bring_back(after_all(list(found[groups : 2 * groups]), pieces[0]))
+        grad_parts = scatter_pieces(after_all(pieces, moved_in), "row")
+        if last:
+            grad_parts[0] = after(grad_parts[0], *outputs[1:groups])
+        else:
+            outputs = scatter_pieces(after_all(outputs, *grad_parts[1:]), "row")
+            arrived = scatter_pieces(after_all(chip, *grad_parts[1:]), "row")
+            for part in outputs:
+                stream = stream + part.astype(jnp.float32)
         saved = kept[layer]
         height = -(-(4 * strip + expert_count + 4) // (16 * groups)) * (16 * groups)
         grad, branch, blocks = run_kernel(
@@ -1066,32 +1088,25 @@
             32 * padded * features * features,
             [pltpu.VMEM((padded, 3 * features), low), pltpu.VMEM((padded, features), low)],
         )
-        chip = sum_chip(blocks, at_col)
+        chip = list(sum_chip(blocks, at_col))
         if layer > 0:
-            images = gather_group(after(branch, *outputs) if last else branch)
+            images = gather_group(branch)
             moved_out = fetch_weights(found[-2], *images[1:rows])
             grad_in = [widen_grads(layer, layer_count, moved_in, grad_in)]
             branches = scatter_pieces(dispatch(layer - 1, images), "dp")
-            earlier = list(grad_in)
             if last:
                 outputs = combine(layer, outputs)
-                earlier = earlier + list(outputs)
-                parts = scatter_pieces(after_all(outputs, moved_out), "row")
-            branches = after_all(branches, *earlier)
-            arrived = scatter_pieces(after_all(list(chip), moved_out), "row")
+            branches = after_all(branches, *grad_in, *outputs)
+        else:
+            earlier = add_pieces(arrived).astype(low)
+            shared[layer + 1] = sum_groups(earlier)
+            arrived = scatter_pieces(after_all(chip, earlier, *outputs[1:]), "row")
+            moved_out = fetch_weights(found[-2], *arrived[1:])
+            grad_in = [widen_grads(layer, layer_count, after(moved_in, chip[0]), grad_in)]
+            output = split(stream.astype(low))
+            arrived = after_all(arrived, *grad_in, *shared[1:], output)
             grad_out = [widen_grads(layer, layer_count, moved_out, grad_out)]
-            sooner = arrived[1:] + parts[1:]
-            for part in parts:
-                stream = stream + part.astype(jnp.float32)
-            parts = []
-        else:
-            grad_in = [widen_grads(layer, layer_count, moved_in, grad_in)]
-            arrived = scatter_pieces(after_all(list(chip), *shared[1:]), "row")
-            moved_out = fetch_weights(found[-2], *arrived[1:])
-            output = split(stream.astype(low))
-            arrived = after_all(arrived, *grad_in, output)
-            grad_out = [widen_grads(layer, layer_count, moved_out, grad_out)]
-        shared[layer] = sum_groups(add_pieces(arrived).astype(low))
+            shared[layer] = sum_groups(add_pieces(arrived).astype(low))
     grad_input = split(grad)
     shared = jnp.stack(shared)
     grad_qkv = (

time: 505 us -> 475 us (0.941)
  waiting for transfers between devices: 175 us -> 155 us
  local copies, waits for them, and re-layouts: 59.8 us -> 50.9 us
    ppermute x118, waiting for transfers between devices: 167 us -> 144 us  [exchange(): lax.ppermute(values, axis, [(place, place ^ offset) for place in range(co...]
    unnamed x257 -> x195, local copies, waits for them, and re-layouts: 33 us -> 23.5 us
  transfers between devices with their start and end apart: 126 -> 126, of which waited for: 49 -> 58; matrix products, arithmetic and copies ran while one was open for 8% -> 8% of each run, Pallas kernels for 16% -> 15%
where the time goes in v3:
time: 475 us; the launch traced here: 466 us
  waiting for transfers between devices  155 us (33%)
  starting transfers between devices  144 us (30%)
  Pallas kernels  101 us (21%)
  local copies, waits for them, and re-layouts  50.9 us (11%)
  other arithmetic  12.7 us (3%)
    ppermute x118, waiting for transfers between devices, exchange(): lax.ppermute(values, axis, [(place, place ^ offset) for place in range(co...  144 us
    ppermute x118, starting transfers between devices, exchange(): lax.ppermute(values, axis, [(place, place ^ offset) for place in range(co...  109 us
    pallas_call x15, Pallas kernels, run_kernel(): pl.pallas_call(functools.partial(staged_body, body, len(fixed), staged, a...  84.8 us
    all_to_all x8, starting transfers between devices, fetch_weights(): lax.all_to_all(after(own, *earlier), ('row', 'col'), split_axis=0, concat...  35.3 us
    unnamed x195, local copies, waits for them, and re-layouts  23.5 us
    pallas_call x4, Pallas kernels, widen_grads(): pl.pallas_call(widen_kernel, name='widen', grid=(members,), in_specs=[pl....  16.5 us
    all_to_all x8, waiting for transfers between devices, fetch_weights(): lax.all_to_all(after(own, *earlier), ('row', 'col'), split_axis=0, concat...  10.2 us
  transfers between devices with their start and end apart: 126, of which 58 were waited for; matrix products, arithmetic and copies ran while one was open for 8% of the time, Pallas kernels for 15%

profile of v3, /device:TPU:0, one launch (start us, length us, event | category | flops | bytes accessed | tf_op | source)
XLA Modules:
  0.0 466.1 jit_solution(4231835363324872349)
XLA Ops:
  3.0 4.0 collective-permute-start.3
  7.6 4.6 dynamic-slice_bitcast_fusion.1
  14.1 4.7 %collective-permute-done.2.refs_3_ = bf16[256,512]{1,0:T(8,128)(2,1)S(1)} collective-permute-done((bf16[256,512]{1,0:T(8,128)(2,1)S(1)}, bf16[256,512]{1,0:T(8,128)(2,1)S(1)}, u32[]{:S(2)}, u32[]{:S(2)}) %collective-permute-start.2) | collective-permute-done | bytes 262176 | tf_op jit(solution)/shard_map/ppermute | solution.py:371
  19.2 4.5 all-to-all-start
  28.8 5.1 %attention_forward.2 = (f32[208,512]{1,0:T(8,128)}, f32[208,512]{1,0:T(8,128)}, bf16[208,512]{1,0:T(8,128)(2,1)}, bf16[208,1536]{1,0:T(8,128)(2,1)}, bf16[208,51...) custom-call(s32[4]{0:T(128)S(1)} %pad_add_fusion.refs_0_, bf16[256,512]{1,0:T(8,128)(2,1)} %copy-done.35, ...), custom_call_target="tpu_custom_call" | custom-call | flops 872415232 | bytes 2318352 | tf_op jit(solution)/shard_map/attention_forward/pallas_call | solution.py:776
  37.4 4.5 dynamic-slice_bitcast_fusion
  42.0 13.3 %collective-permute-done.11.refs_4_ = bf16[208,512]{1,0:T(8,128)(2,1)S(1)} collective-permute-done((bf16[208,512]{1,0:T(8,128)(2,1)S(1)}, bf16[208,512]{1,0:T(8,128)(2,1)S(1)}, u32[]{:S(2)}, u32[]{:S(2)}) %collective-permute-start.11) | collective-permute-done | bytes 213024 | tf_op jit(solution)/shard_map/ppermute | solution.py:371
  58.5 4.5 all-to-all-start.1
  77.4 6.7 %collective-permute-done.17.refs_6_ = bf16[128,512]{1,0:T(8,128)(2,1)S(1)} collective-permute-done((bf16[128,512]{1,0:T(8,128)(2,1)S(1)}, bf16[128,512]{1,0:T(8,128)(2,1)S(1)}, u32[]{:S(2)}, u32[]{:S(2)}) %collective-permute-start.17) | collective-permute-done | bytes 131104 | tf_op jit(solution)/shard_map/ppermute | solution.py:371
  84.1 5.5 %all-to-all-done.1.refs_3_ = bf16[8,512,256]{2,1,0:T(8,128)(2,1)} async-done(((bf16[8,512,256]{2,1,0:T(8,128)(2,1)}), bf16[8,512,256]{2,1,0:T(8,128)(2,1)}, u32[]{:S(2)}, u32[]{:S(2)}) %all-to-all-start.1) | async-done | bytes 2097184 | tf_op jit(solution)/shard_map/all_to_all | solution.py:919
  89.6 6.9 %expert_forward.1 = (bf16[128,512]{1,0:T(8,128)(2,1)S(1)}, bf16[128,512]{1,0:T(8,128)(2,1)S(1)}, bf16[128,512]{1,0:T(8,128)(2,1)S(1)}, bf16[128,512]{1,0:T(8,128)(2,1)S(1)}) custom-call(s32[4]{0:T(128)S(1)} %pad_add_fusion.refs_0_, bf16[32,512]{1,0:T(8,128)(2,1)} %get-tuple-element.311.refs_1_, bf16[8,256,512]{2,1,0:T(8,128)(2,1)} %all-to-all-done.refs_2_, ...), custom_call_target="tpu_custom_call" | custom-call | flops 2147483648 | bytes 4751376 | tf_op jit(solution)/shard_map/expert_forward/pallas_call | solution.py:776
  96.5 4.6 all-to-all-start.2
  105.9 3.3 collective-permute-done.26.refs_2_
  109.3 6.4 %collective-permute-done.27.refs_3_ = bf16[128,512]{1,0:T(8,128)(2,1)S(1)} collective-permute-done((bf16[128,512]{1,0:T(8,128)(2,1)S(1)}, bf16[128,512]{1,0:T(8,128)(2,1)S(1)}, u32[]{:S(2)}, u32[]{:S(2)}) %collective-permute-start.27) | collective-permute-done | bytes 131104 | tf_op jit(solution)/shard_map/ppermute | solution.py:371
  121.5 3.5 combine.4
  129.1 4.6 collective-permute-done.21.refs_4_
  133.9 5.1 %collective-permute-done.20.refs_3_ = bf16[256,512]{1,0:T(8,128)(2,1)S(1)} collective-permute-done((bf16[256,512]{1,0:T(8,128)(2,1)S(1)}, bf16[256,512]{1,0:T(8,128)(2,1)S(1)}, u32[]{:S(2)}, u32[]{:S(2)}) %collective-permute-start.20) | collective-permute-done | bytes 262176 | tf_op jit(solution)/shard_map/ppermute | solution.py:371
  139.5 3.5 collective-permute-done.33.refs_12_
  143.9 4.2 collective-permute-done.35.refs_14_
  152.4 5.4 %attention_forward.3 = (f32[208,512]{1,0:T(8,128)}, f32[208,512]{1,0:T(8,128)}, bf16[208,512]{1,0:T(8,128)(2,1)}, bf16[208,1536]{1,0:T(8,128)(2,1)}, bf16[208,51...) custom-call(s32[4]{0:T(128)S(1)} %pad_add_fusion.refs_0_, bf16[256,512]{1,0:T(8,128)(2,1)} %copy-done.24, ...), custom_call_target="tpu_custom_call" | custom-call | flops 872415232 | bytes 3383312 | tf_op jit(solution)/shard_map/attention_forward/pallas_call | solution.py:776
  161.3 5.6 %collective-permute-done.38.refs_4_ = bf16[208,512]{1,0:T(8,128)(2,1)S(1)} collective-permute-done((bf16[208,512]{1,0:T(8,128)(2,1)S(1)}, bf16[208,512]{1,0:T(8,128)(2,1)S(1)}, u32[]{:S(2)}, u32[]{:S(2)}) %collective-permute-start.38) | collective-permute-done | bytes 213024 | tf_op jit(solution)/shard_map/ppermute | solution.py:371
  168.9 4.8 %all-to-all-start.3 = ((bf16[8,512,256]{2,1,0:T(8,128)(2,1)}), bf16[8,512,256]{2,1,0:T(8,128)(2,1)}, u32[]{:S(2)}, u32[]{:S(2)}) async-start(bf16[8,512,256]{2,1,0:T(8,128)(2,1)} %get-tuple-element.160), calls=%async_computation.3 | async-start | bytes 4194304 | tf_op jit(solution)/shard_map/all_to_all | solution.py:919
  186.9 3.5 collective-permute-start.51
  194.5 10.3 %collective-permute-done.51.refs_6_ = bf16[128,512]{1,0:T(8,128)(2,1)S(1)} collective-permute-done((bf16[128,512]{1,0:T(8,128)(2,1)S(1)}, bf16[128,512]{1,0:T(8,128)(2,1)S(1)}, u32[]{:S(2)}, u32[]{:S(2)}) %collective-permute-start.51) | collective-permute-done | bytes 131104 | tf_op jit(solution)/shard_map/ppermute | solution.py:371
  205.6 12.9 %expert_full.2 = (bf16[128,512]{1,0:T(8,128)(2,1)S(1)}, bf16[128,512]{1,0:T(8,128)(2,1)S(1)}, bf16[128,512]{1,0:T(8,128)(2,1)S(1)}, bf16[128,512]{1,0:T(8,128)(2...) custom-call(s32[4]{0:T(128)S(1)} %pad_add_fusion.refs_0_, ...), custom_call_target="tpu_custom_call" | custom-call | flops 6442450944 | bytes 5275664 | tf_op jit(solution)/shard_map/expert_full/pallas_call | solution.py:776
  221.8 4.2 all-to-all-start.4
  230.9 4.0 collective-permute-done.56.refs_2_
  234.9 6.6 %collective-permute-done.57.refs_3_ = bf16[128,512]{1,0:T(8,128)(2,1)} collective-permute-done((bf16[128,512]{1,0:T(8,128)(2,1)S(1)}, bf16[128,512]{1,0:T(8,128)(2,1)}, u32[]{:S(2)}, u32[]{:S(2)}) %collective-permute-start.57) | collective-permute-done | bytes 131104 | tf_op jit(solution)/shard_map/ppermute | solution.py:371
  244.3 3.5 combine.5
  256.1 3.4 collective-permute-start.64
  260.8 7.2 %collective-permute-done.64.refs_3_ = bf16[128,512]{1,0:T(8,128)(2,1)S(1)} collective-permute-done((bf16[128,512]{1,0:T(8,128)(2,1)S(1)}, bf16[128,512]{1,0:T(8,128)(2,1)S(1)}, u32[]{:S(2)}, u32[]{:S(2)}) %collective-permute-start.64) | collective-permute-done | bytes 131104 | tf_op jit(solution)/shard_map/ppermute | solution.py:371
  269.0 9.9 %attention_backward.2 = (f32[208,512]{1,0:T(8,128)S(1)}, bf16[208,512]{1,0:T(8,128)(2,1)S(1)}, bf16[2,4,576,256]{3,2,1,0:T(8,128)(2,1)S(1)}) custom-call(s32[4]{0:T(128)S(1)} %pad_add_fusion.refs_0_, bf16[512,2048]{1,0:T(8,128)(2,1)} %get-tuple-element.191.refs_1_, f32[4,512]{1,0:T(4,128)} %get-tuple-element.304.refs_9_.refs_2_, ...), custom_call_target="tpu_custom_call" | custom-call | flops 1744830464 | bytes 5152784 | tf_op jit(solution)/shard_map/attention_backward/pallas_call | solution.py:776
  284.5 3.6 collective-permute-done.75.refs_4_
  290.6 4.7 %all-to-all-start.5 = ((bf16[8,512,256]{2,1,0:T(8,128)(2,1)}), bf16[8,512,256]{2,1,0:T(8,128)(2,1)}, u32[]{:S(2)}, u32[]{:S(2)}) async-start(bf16[8,512,256]{2,1,0:T(8,128)(2,1)} %copy-done.4), calls=%async_computation.5 | async-start | bytes 4194304 | tf_op jit(solution)/shard_map/all_to_all | solution.py:919
  301.4 3.7 collective-permute-start.81
  306.4 3.5 combine.6
  310.0 3.5 widen.4.refs_0_
  317.4 12.0 %expert_full.3 = (bf16[128,512]{1,0:T(8,128)(2,1)S(1)}, bf16[128,512]{1,0:T(8,128)(2,1)S(1)}, bf16[128,512]{1,0:T(8,128)(2,1)S(1)}, bf16[128,512]{1,0:T(8,128)(2...) custom-call(s32[4]{0:T(128)S(1)} %pad_add_fusion.refs_0_, ...), custom_call_target="tpu_custom_call" | custom-call | flops 6442450944 | bytes 5275664 | tf_op jit(solution)/shard_map/expert_full/pallas_call | solution.py:776
  332.8 4.3 all-to-all-start.6
  344.3 6.0 %widen.5.refs_0_ = f32[2,8,512,256]{3,2,1,0:T(8,128)} custom-call(bf16[8,512,256]{2,1,0:T(8,128)(2,1)} %all-to-all-done.5.narrow_ref), custom_call_target="tpu_custom_call" | custom-call | tf_op jit(solution)/shard_map/widen/pallas_call | solution.py:687
  356.0 3.5 combine.7
  382.1 10.0 %attention_backward.3 = (f32[208,512]{1,0:T(8,128)S(1)}, bf16[208,512]{1,0:T(8,128)(2,1)}, bf16[2,4,576,256]{3,2,1,0:T(8,128)(2,1)S(1)}) custom-call(s32[4]{0:T(128)S(1)} %pad_add_fusion.refs_0_, bf16[512,2048]{1,0:T(8,128)(2,1)} %get-tuple-element.241.refs_1_, f32[4,512]{1,0:T(4,128)} %get-tuple-element.305.refs_9_.refs_2_, ...), custom_call_target="tpu_custom_call" | custom-call | flops 1744830464 | bytes 5365776 | tf_op jit(solution)/shard_map/attention_backward/pallas_call | solution.py:776
  421.8 3.5 widen.6
  425.3 3.6 collective-permute-done.110
  431.0 3.7 all-to-all-start.7
  443.5 3.3 collective-permute-done.113
  452.1 3.6 collective-permute-done.116
  462.2 3.5 widen.7
  (492 shorter events, 206.9 us)
Async XLA Ops:
  6.9 11.9 %collective-permute-start.2 = (bf16[256,512]{1,0:T(8,128)(2,1)S(1)}, bf16[256,512]{1,0:T(8,128)(2,1)S(1)}, u32[]{:S(2)}, u32[]{:S(2)}) collective-permute-start(bf16[256,512]{1,0:T(8,128)(2,1)S(1)} %maximum_maximum_fusion.1.refs_1_), channel_id=1, source_target_pairs={{0,4},{2,6},{4,0},{6,2},{1,5},{3,7},{5,1},{7,3},{8,12},{10,14},{12... | collective-permute-start | bytes 786440 | tf_op jit(solution)/shard_map/ppermute | solution.py:371
  7.4 11.7 %collective-permute-start.1 = (bf16[256,512]{1,0:T(8,128)(2,1)S(1)}, bf16[256,512]{1,0:T(8,128)(2,1)S(1)}, u32[]{:S(2)}, u32[]{:S(2)}) collective-permute-start(bf16[256,512]{1,0:T(8,128)(2,1)S(1)} %maximum_maximum_fusion.1.refs_1_), channel_id=1, source_target_pairs={{0,2},{2,0},{4,6},{6,4},{1,3},{3,1},{5,7},{7,5},{8,10},{10,8},{12,... | collective-permute-start | bytes 786440 | tf_op jit(solution)/shard_map/ppermute | solution.py:371
  19.2 39.3 %all-to-all-start = ((bf16[8,256,512]{2,1,0:T(8,128)(2,1)}), bf16[8,256,512]{2,1,0:T(8,128)(2,1)}, u32[]{:S(2)}, u32[]{:S(2)}) async-start(bf16[8,256,512]{2,1,0:T(8,128)(2,1)} %get-tuple-element.139), calls=%async_computation | async-start | bytes 4194304 | tf_op jit(solution)/shard_map/all_to_all | solution.py:919
  33.9 21.4 %collective-permute-start.11 = (bf16[208,512]{1,0:T(8,128)(2,1)S(1)}, bf16[208,512]{1,0:T(8,128)(2,1)S(1)}, u32[]{:S(2)}, u32[]{:S(2)}) collective-permute-start(bf16[208,512]{1,0:T(8,128)(2,1)S(1)} %get-tuple-element.140.refs_1_), channel_id=1, source_target_pairs={{0,6},{2,4},{4,2},{6,0},{1,7},{3,5},{5,3},{7,1},{8,14},{10,12},{12... | collective-permute-start | bytes 638984 | tf_op jit(solution)/shard_map/ppermute | solution.py:371
  36.7 21.7 %collective-permute-start.10 = (bf16[208,512]{1,0:T(8,128)(2,1)S(1)}, bf16[208,512]{1,0:T(8,128)(2,1)S(1)}, u32[]{:S(2)}, u32[]{:S(2)}) collective-permute-start(bf16[208,512]{1,0:T(8,128)(2,1)S(1)} %get-tuple-element.140.refs_1_), channel_id=1, source_target_pairs={{0,4},{2,6},{4,0},{6,2},{1,5},{3,7},{5,1},{7,3},{8,12},{10,14},{12... | collective-permute-start | bytes 638984 | tf_op jit(solution)/shard_map/ppermute | solution.py:371
  37.3 21.2 %collective-permute-start.9 = (bf16[208,512]{1,0:T(8,128)(2,1)S(1)}, bf16[208,512]{1,0:T(8,128)(2,1)S(1)}, u32[]{:S(2)}, u32[]{:S(2)}) collective-permute-start(bf16[208,512]{1,0:T(8,128)(2,1)S(1)} %get-tuple-element.140.refs_1_), channel_id=1, source_target_pairs={{0,2},{2,0},{4,6},{6,4},{1,3},{3,1},{5,7},{7,5},{8,10},{10,8},{12,... | collective-permute-start | bytes 638984 | tf_op jit(solution)/shard_map/ppermute | solution.py:371
  58.5 31.2 %all-to-all-start.1 = ((bf16[8,512,256]{2,1,0:T(8,128)(2,1)}), bf16[8,512,256]{2,1,0:T(8,128)(2,1)}, u32[]{:S(2)}, u32[]{:S(2)}) async-start(bf16[8,512,256]{2,1,0:T(8,128)(2,1)} %get-tuple-element.141), calls=%async_computation.1 | async-start | bytes 4194304 | tf_op jit(solution)/shard_map/all_to_all | solution.py:919
  71.2 12.9 %collective-permute-start.17 = (bf16[128,512]{1,0:T(8,128)(2,1)S(1)}, bf16[128,512]{1,0:T(8,128)(2,1)S(1)}, u32[]{:S(2)}, u32[]{:S(2)}) collective-permute-start(bf16[128,512]{1,0:T(8,128)(2,1)S(1)} %get-tuple-element.144), channel_id=1, source_target_pairs={{0,16},{8,24},{16,0},{24,8},{1,17},{9,25},{17,1},{25,9},{2,18},{10... | collective-permute-start | bytes 393224 | tf_op jit(solution)/shard_map/ppermute | solution.py:371
  96.5 72.4 %all-to-all-start.2 = ((bf16[8,256,512]{2,1,0:T(8,128)(2,1)}), bf16[8,256,512]{2,1,0:T(8,128)(2,1)}, u32[]{:S(2)}, u32[]{:S(2)}) async-start(bf16[8,256,512]{2,1,0:T(8,128)(2,1)} %get-tuple-element.157), calls=%async_computation.2 | async-start | bytes 4194304 | tf_op jit(solution)/shard_map/all_to_all | solution.py:919
  102.7 12.9 %collective-permute-start.27 = (bf16[128,512]{1,0:T(8,128)(2,1)S(1)}, bf16[128,512]{1,0:T(8,128)(2,1)S(1)}, u32[]{:S(2)}, u32[]{:S(2)}) collective-permute-start(bf16[128,512]{1,0:T(8,128)(2,1)S(1)} %get-tuple-element.150), channel_id=1, source_target_pairs={{0,16},{8,24},{16,0},{24,8},{1,17},{9,25},{17,1},{25,9},{2,18},{10... | collective-permute-start | bytes 393224 | tf_op jit(solution)/shard_map/ppermute | solution.py:371
  105.9 14.3 %collective-permute-start.29 = (bf16[128,512]{1,0:T(8,128)(2,1)S(1)}, bf16[128,512]{1,0:T(8,128)(2,1)S(1)}, u32[]{:S(2)}, u32[]{:S(2)}) collective-permute-start(bf16[128,512]{1,0:T(8,128)(2,1)S(1)} %get-tuple-element.146.refs_1_), channel_id=1, source_target_pairs={{0,1},{1,0},{2,3},{3,2},{4,5},{5,4},{6,7},{7,6},{8,9},{9,8},{10,11... | collective-permute-start | bytes 393224 | tf_op jit(solution)/shard_map/ppermute | solution.py:371
  109.2 11.4 %collective-permute-start.30 = (bf16[128,512]{1,0:T(8,128)(2,1)S(1)}, bf16[128,512]{1,0:T(8,128)(2,1)S(1)}, u32[]{:S(2)}, u32[]{:S(2)}) collective-permute-start(bf16[128,512]{1,0:T(8,128)(2,1)S(1)} %collective-permute-done.26.refs_2_), channel_id=1, source_target_pairs={{0,1},{1,0},{2,3},{3,2},{4,5},{5,4},{6,7},{7,6},{8,9},{9,8},{10,11... | collective-permute-start | bytes 393224 | tf_op jit(solution)/shard_map/ppermute | solution.py:371
  116.2 17.5 %collective-permute-start.21 = (bf16[256,512]{1,0:T(8,128)(2,1)S(1)}, bf16[256,512]{1,0:T(8,128)(2,1)S(1)}, u32[]{:S(2)}, u32[]{:S(2)}) collective-permute-start(bf16[256,512]{1,0:T(8,128)(2,1)S(1)} %maximum_maximum_fusion.refs_1_), channel_id=1, source_target_pairs={{0,6},{2,4},{4,2},{6,0},{1,7},{3,5},{5,3},{7,1},{8,14},{10,12},{12... | collective-permute-start | bytes 786440 | tf_op jit(solution)/shard_map/ppermute | solution.py:371
  120.1 18.8 %collective-permute-start.20 = (bf16[256,512]{1,0:T(8,128)(2,1)S(1)}, bf16[256,512]{1,0:T(8,128)(2,1)S(1)}, u32[]{:S(2)}, u32[]{:S(2)}) collective-permute-start(bf16[256,512]{1,0:T(8,128)(2,1)S(1)} %maximum_maximum_fusion.refs_1_), channel_id=1, source_target_pairs={{0,4},{2,6},{4,0},{6,2},{1,5},{3,7},{5,1},{7,3},{8,12},{10,14},{12... | collective-permute-start | bytes 786440 | tf_op jit(solution)/shard_map/ppermute | solution.py:371
  120.7 18.3 %collective-permute-start.19 = (bf16[256,512]{1,0:T(8,128)(2,1)S(1)}, bf16[256,512]{1,0:T(8,128)(2,1)S(1)}, u32[]{:S(2)}, u32[]{:S(2)}) collective-permute-start(bf16[256,512]{1,0:T(8,128)(2,1)S(1)} %maximum_maximum_fusion.refs_1_), channel_id=1, source_target_pairs={{0,2},{2,0},{4,6},{6,4},{1,3},{3,1},{5,7},{7,5},{8,10},{10,8},{12,... | collective-permute-start | bytes 786440 | tf_op jit(solution)/shard_map/ppermute | solution.py:371
  125.7 17.3 %collective-permute-start.33 = (bf16[208,512]{1,0:T(8,128)(2,1)S(1)}, bf16[208,512]{1,0:T(8,128)(2,1)S(1)}, u32[]{:S(2)}, u32[]{:S(2)}) collective-permute-start(bf16[208,512]{1,0:T(8,128)(2,1)S(1)} %get-tuple-element.153), channel_id=1, source_target_pairs={{0,2},{2,0},{4,6},{6,4},{1,3},{3,1},{5,7},{7,5},{8,10},{10,8},{12,... | collective-permute-start | bytes 638984 | tf_op jit(solution)/shard_map/ppermute | solution.py:371
  127.6 16.2 %collective-permute-start.34 = (bf16[208,512]{1,0:T(8,128)(2,1)S(1)}, bf16[208,512]{1,0:T(8,128)(2,1)S(1)}, u32[]{:S(2)}, u32[]{:S(2)}) collective-permute-start(bf16[208,512]{1,0:T(8,128)(2,1)S(1)} %get-tuple-element.154), channel_id=1, source_target_pairs={{0,4},{2,6},{4,0},{6,2},{1,5},{3,7},{5,1},{7,3},{8,12},{10,14},{12... | collective-permute-start | bytes 638984 | tf_op jit(solution)/shard_map/ppermute | solution.py:371
  133.8 14.3 %collective-permute-start.35 = (bf16[208,512]{1,0:T(8,128)(2,1)S(1)}, bf16[208,512]{1,0:T(8,128)(2,1)S(1)}, u32[]{:S(2)}, u32[]{:S(2)}) collective-permute-start(bf16[208,512]{1,0:T(8,128)(2,1)S(1)} %get-tuple-element.155), channel_id=1, source_target_pairs={{0,6},{2,4},{4,2},{6,0},{1,7},{3,5},{5,3},{7,1},{8,14},{10,12},{12... | collective-permute-start | bytes 638984 | tf_op jit(solution)/shard_map/ppermute | solution.py:371
  148.1 11.8 %collective-permute-start.41 = (bf16[208,512]{1,0:T(8,128)(2,1)S(1)}, bf16[208,512]{1,0:T(8,128)(2,1)S(1)}, u32[]{:S(2)}, u32[]{:S(2)}) collective-permute-start(bf16[208,512]{1,0:T(8,128)(2,1)S(1)} %get-tuple-element.159.refs_1_.refs_8_), channel_id=1, source_target_pairs={{0,6},{2,4},{4,2},{6,0},{1,7},{3,5},{5,3},{7,1},{8,14},{10,12},{12... | collective-permute-start | bytes 638984 | tf_op jit(solution)/shard_map/ppermute | solution.py:371
  148.4 12.9 %collective-permute-start.40 = (bf16[208,512]{1,0:T(8,128)(2,1)S(1)}, bf16[208,512]{1,0:T(8,128)(2,1)S(1)}, u32[]{:S(2)}, u32[]{:S(2)}) collective-permute-start(bf16[208,512]{1,0:T(8,128)(2,1)S(1)} %get-tuple-element.159.refs_1_.refs_8_), channel_id=1, source_target_pairs={{0,4},{2,6},{4,0},{6,2},{1,5},{3,7},{5,1},{7,3},{8,12},{10,14},{12... | collective-permute-start | bytes 638984 | tf_op jit(solution)/shard_map/ppermute | solution.py:371
  150.1 11.2 %collective-permute-start.39 = (bf16[208,512]{1,0:T(8,128)(2,1)S(1)}, bf16[208,512]{1,0:T(8,128)(2,1)S(1)}, u32[]{:S(2)}, u32[]{:S(2)}) collective-permute-start(bf16[208,512]{1,0:T(8,128)(2,1)S(1)} %get-tuple-element.159.refs_1_.refs_8_), channel_id=1, source_target_pairs={{0,2},{2,0},{4,6},{6,4},{1,3},{3,1},{5,7},{7,5},{8,10},{10,8},{12,... | collective-permute-start | bytes 638984 | tf_op jit(solution)/shard_map/ppermute | solution.py:371
  168.9 36.0 %all-to-all-start.3 = ((bf16[8,512,256]{2,1,0:T(8,128)(2,1)}), bf16[8,512,256]{2,1,0:T(8,128)(2,1)}, u32[]{:S(2)}, u32[]{:S(2)}) async-start(bf16[8,512,256]{2,1,0:T(8,128)(2,1)} %get-tuple-element.160), calls=%async_computation.3 | async-start | bytes 4194304 | tf_op jit(solution)/shard_map/all_to_all | solution.py:919
  179.1 11.4 %collective-permute-start.53 = (bf16[128,512]{1,0:T(8,128)(2,1)S(1)}, bf16[128,512]{1,0:T(8,128)(2,1)S(1)}, u32[]{:S(2)}, u32[]{:S(2)}) collective-permute-start(bf16[128,512]{1,0:T(8,128)(2,1)S(1)} %get-tuple-element.174), channel_id=1, source_target_pairs={{0,8},{8,0},{16,24},{24,16},{1,9},{9,1},{17,25},{25,17},{2,10},{10... | collective-permute-start | bytes 393224 | tf_op jit(solution)/shard_map/ppermute | solution.py:371
  180.6 13.0 %collective-permute-start.54 = (bf16[128,512]{1,0:T(8,128)(2,1)S(1)}, bf16[128,512]{1,0:T(8,128)(2,1)S(1)}, u32[]{:S(2)}, u32[]{:S(2)}) collective-permute-start(bf16[128,512]{1,0:T(8,128)(2,1)S(1)} %get-tuple-element.175), channel_id=1, source_target_pairs={{0,16},{8,24},{16,0},{24,8},{1,17},{9,25},{17,1},{25,9},{2,18},{10... | collective-permute-start | bytes 393224 | tf_op jit(solution)/shard_map/ppermute | solution.py:371
  186.9 17.9 %collective-permute-start.51 = (bf16[128,512]{1,0:T(8,128)(2,1)S(1)}, bf16[128,512]{1,0:T(8,128)(2,1)S(1)}, u32[]{:S(2)}, u32[]{:S(2)}) collective-permute-start(bf16[128,512]{1,0:T(8,128)(2,1)S(1)} %get-tuple-element.172), channel_id=1, source_target_pairs={{0,16},{8,24},{16,0},{24,8},{1,17},{9,25},{17,1},{25,9},{2,18},{10... | collective-permute-start | bytes 393224 | tf_op jit(solution)/shard_map/ppermute | solution.py:371
  190.4 14.4 %collective-permute-start.52 = (bf16[128,512]{1,0:T(8,128)(2,1)S(1)}, bf16[128,512]{1,0:T(8,128)(2,1)S(1)}, u32[]{:S(2)}, u32[]{:S(2)}) collective-permute-start(bf16[128,512]{1,0:T(8,128)(2,1)S(1)} %get-tuple-element.173), channel_id=1, source_target_pairs={{0,24},{8,16},{16,8},{24,0},{1,25},{9,17},{17,9},{25,1},{2,26},{10... | collective-permute-start | bytes 393224 | tf_op jit(solution)/shard_map/ppermute | solution.py:371
  221.8 30.8 %all-to-all-start.4 = ((bf16[8,256,512]{2,1,0:T(8,128)(2,1)}), bf16[8,256,512]{2,1,0:T(8,128)(2,1)S(1)}, u32[]{:S(2)}, u32[]{:S(2)}) async-start(bf16[8,256,512]{2,1,0:T(8,128)(2,1)} %copy-done.6), calls=%async_computation.4 | async-start | bytes 4194304 | tf_op jit(solution)/shard_map/all_to_all | solution.py:919
  228.4 13.0 %collective-permute-start.57 = (bf16[128,512]{1,0:T(8,128)(2,1)S(1)}, bf16[128,512]{1,0:T(8,128)(2,1)}, u32[]{:S(2)}, u32[]{:S(2)}) collective-permute-start(bf16[128,512]{1,0:T(8,128)(2,1)S(1)} %get-tuple-element.180), channel_id=1, source_target_pairs={{0,16},{8,24},{16,0},{24,8},{1,17},{9,25},{17,1},{25,9},{2,18},{10... | collective-permute-start | bytes 393224 | tf_op jit(solution)/shard_map/ppermute | solution.py:371
  229.5 11.9 %collective-permute-start.58 = (bf16[128,512]{1,0:T(8,128)(2,1)S(1)}, bf16[128,512]{1,0:T(8,128)(2,1)}, u32[]{:S(2)}, u32[]{:S(2)}) collective-permute-start(bf16[128,512]{1,0:T(8,128)(2,1)S(1)} %get-tuple-element.181), channel_id=1, source_target_pairs={{0,24},{8,16},{16,8},{24,0},{1,25},{9,17},{17,9},{25,1},{2,26},{10... | collective-permute-start | bytes 393224 | tf_op jit(solution)/shard_map/ppermute | solution.py:371
  230.9 12.0 %collective-permute-start.59 = (bf16[128,512]{1,0:T(8,128)(2,1)S(1)}, bf16[128,512]{1,0:T(8,128)(2,1)}, u32[]{:S(2)}, u32[]{:S(2)}) collective-permute-start(bf16[128,512]{1,0:T(8,128)(2,1)S(1)} %get-tuple-element.178.refs_1_), channel_id=1, source_target_pairs={{0,1},{1,0},{2,3},{3,2},{4,5},{5,4},{6,7},{7,6},{8,9},{9,8},{10,11... | collective-permute-start | bytes 393224 | tf_op jit(solution)/shard_map/ppermute | solution.py:371
  252.6 15.5 %collective-permute-start.72 = (bf16[208,512]{1,0:T(8,128)(2,1)S(1)}, bf16[208,512]{1,0:T(8,128)(2,1)S(1)}, u32[]{:S(2)}, u32[]{:S(2)}) collective-permute-start(bf16[208,512]{1,0:T(8,128)(2,1)S(1)} %get-tuple-element.205), channel_id=1, source_target_pairs={{0,6},{2,4},{4,2},{6,0},{1,7},{3,5},{5,3},{7,1},{8,14},{10,12},{12... | collective-permute-start | bytes 638984 | tf_op jit(solution)/shard_map/ppermute | solution.py:371
  253.2 14.9 %collective-permute-start.71 = (bf16[208,512]{1,0:T(8,128)(2,1)S(1)}, bf16[208,512]{1,0:T(8,128)(2,1)S(1)}, u32[]{:S(2)}, u32[]{:S(2)}) collective-permute-start(bf16[208,512]{1,0:T(8,128)(2,1)S(1)} %get-tuple-element.203), channel_id=1, source_target_pairs={{0,4},{2,6},{4,0},{6,2},{1,5},{3,7},{5,1},{7,3},{8,12},{10,14},{12... | collective-permute-start | bytes 638984 | tf_op jit(solution)/shard_map/ppermute | solution.py:371
  254.6 13.6 %collective-permute-start.70 = (bf16[208,512]{1,0:T(8,128)(2,1)S(1)}, bf16[208,512]{1,0:T(8,128)(2,1)S(1)}, u32[]{:S(2)}, u32[]{:S(2)}) collective-permute-start(bf16[208,512]{1,0:T(8,128)(2,1)S(1)} %get-tuple-element.201), channel_id=1, source_target_pairs={{0,2},{2,0},{4,6},{6,4},{1,3},{3,1},{5,7},{7,5},{8,10},{10,8},{12,... | collective-permute-start | bytes 638984 | tf_op jit(solution)/shard_map/ppermute | solution.py:371
  256.1 12.0 %collective-permute-start.64 = (bf16[128,512]{1,0:T(8,128)(2,1)S(1)}, bf16[128,512]{1,0:T(8,128)(2,1)S(1)}, u32[]{:S(2)}, u32[]{:S(2)}) collective-permute-start(bf16[128,512]{1,0:T(8,128)(2,1)S(1)} %get-tuple-element.187), channel_id=1, source_target_pairs={{0,16},{8,24},{16,0},{24,8},{1,17},{9,25},{17,1},{25,9},{2,18},{10... | collective-permute-start | bytes 393224 | tf_op jit(solution)/shard_map/ppermute | solution.py:371
  290.6 42.2 %all-to-all-start.5 = ((bf16[8,512,256]{2,1,0:T(8,128)(2,1)}), bf16[8,512,256]{2,1,0:T(8,128)(2,1)}, u32[]{:S(2)}, u32[]{:S(2)}) async-start(bf16[8,512,256]{2,1,0:T(8,128)(2,1)} %copy-done.4), calls=%async_computation.5 | async-start | bytes 4194304 | tf_op jit(solution)/shard_map/all_to_all | solution.py:919
  300.1 13.4 %collective-permute-start.82 = (bf16[128,512]{1,0:T(8,128)(2,1)S(1)}, bf16[128,512]{1,0:T(8,128)(2,1)S(1)}, u32[]{:S(2)}, u32[]{:S(2)}) collective-permute-start(bf16[128,512]{1,0:T(8,128)(2,1)S(1)} %get-tuple-element.216), channel_id=1, source_target_pairs={{0,24},{8,16},{16,8},{24,0},{1,25},{9,17},{17,9},{25,1},{2,26},{10... | collective-permute-start | bytes 393224 | tf_op jit(solution)/shard_map/ppermute | solution.py:371
  301.4 14.7 %collective-permute-start.81 = (bf16[128,512]{1,0:T(8,128)(2,1)S(1)}, bf16[128,512]{1,0:T(8,128)(2,1)S(1)}, u32[]{:S(2)}, u32[]{:S(2)}) collective-permute-start(bf16[128,512]{1,0:T(8,128)(2,1)S(1)} %get-tuple-element.214), channel_id=1, source_target_pairs={{0,16},{8,24},{16,0},{24,8},{1,17},{9,25},{17,1},{25,9},{2,18},{10... | collective-permute-start | bytes 393224 | tf_op jit(solution)/shard_map/ppermute | solution.py:371
  332.8 30.9 %all-to-all-start.6 = ((bf16[8,256,512]{2,1,0:T(8,128)(2,1)}), bf16[8,256,512]{2,1,0:T(8,128)(2,1)S(1)}, u32[]{:S(2)}, u32[]{:S(2)}) async-start(bf16[8,256,512]{2,1,0:T(8,128)(2,1)} %copy-done.5), calls=%async_computation.6 | async-start | bytes 4194304 | tf_op jit(solution)/shard_map/all_to_all | solution.py:919
  339.4 27.7 %collective-permute-start.99 = (bf16[4,576,256]{2,1,0:T(8,128)(2,1)}, bf16[4,576,256]{2,1,0:T(8,128)(2,1)}, u32[]{:S(2)}, u32[]{:S(2)}) collective-permute-start(bf16[4,576,256]{2,1,0:T(8,128)(2,1)} %dynamic-slice_bitcast_fusion.4), channel_id=1, source_target_pairs={{0,1},{1,0},{2,3},{3,2},{4,5},{5,4},{6,7},{7,6},{8,9},{9,8},{10,11... | collective-permute-start | bytes 3538952 | tf_op jit(solution)/shard_map/ppermute | solution.py:371
  341.2 11.7 %collective-permute-start.84 = (bf16[128,512]{1,0:T(8,128)(2,1)S(1)}, bf16[128,512]{1,0:T(8,128)(2,1)}, u32[]{:S(2)}, u32[]{:S(2)}) collective-permute-start(bf16[128,512]{1,0:T(8,128)(2,1)S(1)} %get-tuple-element.225), channel_id=1, source_target_pairs={{0,16},{8,24},{16,0},{24,8},{1,17},{9,25},{17,1},{25,9},{2,18},{10... | collective-permute-start | bytes 393224 | tf_op jit(solution)/shard_map/ppermute | solution.py:371
  341.2 11.7 %collective-permute-start.83 = (bf16[128,512]{1,0:T(8,128)(2,1)S(1)}, bf16[128,512]{1,0:T(8,128)(2,1)}, u32[]{:S(2)}, u32[]{:S(2)}) collective-permute-start(bf16[128,512]{1,0:T(8,128)(2,1)S(1)} %get-tuple-element.223), channel_id=1, source_target_pairs={{0,8},{8,0},{16,24},{24,16},{1,9},{9,1},{17,25},{25,17},{2,10},{10... | collective-permute-start | bytes 393224 | tf_op jit(solution)/shard_map/ppermute | solution.py:371
  374.6 17.6 %collective-permute-start.93 = (bf16[208,512]{1,0:T(8,128)(2,1)S(1)}, bf16[208,512]{1,0:T(8,128)(2,1)S(1)}, u32[]{:S(2)}, u32[]{:S(2)}) collective-permute-start(bf16[208,512]{1,0:T(8,128)(2,1)S(1)} %get-tuple-element.238), channel_id=1, source_target_pairs={{0,2},{2,0},{4,6},{6,4},{1,3},{3,1},{5,7},{7,5},{8,10},{10,8},{12,... | collective-permute-start | bytes 638984 | tf_op jit(solution)/shard_map/ppermute | solution.py:371
  377.2 18.6 %collective-permute-start.94 = (bf16[208,512]{1,0:T(8,128)(2,1)S(1)}, bf16[208,512]{1,0:T(8,128)(2,1)}, u32[]{:S(2)}, u32[]{:S(2)}) collective-permute-start(bf16[208,512]{1,0:T(8,128)(2,1)S(1)} %get-tuple-element.239), channel_id=1, source_target_pairs={{0,4},{2,6},{4,0},{6,2},{1,5},{3,7},{5,1},{7,3},{8,12},{10,14},{12... | collective-permute-start | bytes 638984 | tf_op jit(solution)/shard_map/ppermute | solution.py:371
  378.6 17.2 %collective-permute-start.95 = (bf16[208,512]{1,0:T(8,128)(2,1)S(1)}, bf16[208,512]{1,0:T(8,128)(2,1)}, u32[]{:S(2)}, u32[]{:S(2)}) collective-permute-start(bf16[208,512]{1,0:T(8,128)(2,1)S(1)} %get-tuple-element.240), channel_id=1, source_target_pairs={{0,6},{2,4},{4,2},{6,0},{1,7},{3,5},{5,3},{7,1},{8,14},{10,12},{12... | collective-permute-start | bytes 638984 | tf_op jit(solution)/shard_map/ppermute | solution.py:371
  379.1 18.3 %collective-permute-start.100 = (bf16[576,256]{1,0:T(8,128)(2,1)}, bf16[576,256]{1,0:T(8,128)(2,1)}, u32[]{:S(2)}, u32[]{:S(2)}) collective-permute-start(bf16[576,256]{1,0:T(8,128)(2,1)} %get-tuple-element.254), channel_id=1, source_target_pairs={{0,2},{2,0},{4,6},{6,4},{1,3},{3,1},{5,7},{7,5},{8,10},{10,8},{12,... | collective-permute-start | bytes 884744 | tf_op jit(solution)/shard_map/ppermute | solution.py:371
  380.7 18.8 %collective-permute-start.101 = (bf16[576,256]{1,0:T(8,128)(2,1)}, bf16[576,256]{1,0:T(8,128)(2,1)}, u32[]{:S(2)}, u32[]{:S(2)}) collective-permute-start(bf16[576,256]{1,0:T(8,128)(2,1)} %get-tuple-element.255), channel_id=1, source_target_pairs={{0,4},{2,6},{4,0},{6,2},{1,5},{3,7},{5,1},{7,3},{8,12},{10,14},{12... | collective-permute-start | bytes 884744 | tf_op jit(solution)/shard_map/ppermute | solution.py:371
  395.8 20.1 %collective-permute-start.98 = (bf16[4,576,256]{2,1,0:T(8,128)(2,1)}, bf16[4,576,256]{2,1,0:T(8,128)(2,1)}, u32[]{:S(2)}, u32[]{:S(2)}) collective-permute-start(bf16[4,576,256]{2,1,0:T(8,128)(2,1)} %dynamic-slice_bitcast_fusion.5), channel_id=1, source_target_pairs={{0,1},{1,0},{2,3},{3,2},{4,5},{5,4},{6,7},{7,6},{8,9},{9,8},{10,11... | collective-permute-start | bytes 3538952 | tf_op jit(solution)/shard_map/ppermute | solution.py:371
  431.0 31.2 %all-to-all-start.7 = ((bf16[8,512,256]{2,1,0:T(8,128)(2,1)}), bf16[8,512,256]{2,1,0:T(8,128)(2,1)S(1)}, u32[]{:S(2)}, u32[]{:S(2)}) async-start(bf16[8,512,256]{2,1,0:T(8,128)(2,1)} %copy-done.3), calls=%async_computation.7 | async-start | bytes 4194304 | tf_op jit(solution)/shard_map/all_to_all | solution.py:919
  (172 other events, 1224.5 us)

commit v4 on v3

--- a/solution.py
+++ b/solution.py
@@ -1,4 +1,5 @@
 import functools
+import math
 
 import jax
 import jax.numpy as jnp
@@ -435,13 +436,13 @@
     part_refs = refs[2 * rows + 2 : -7]
     features = stream_ref.shape[1]
     padded = stream_ref.shape[0]
-    assemble_weights(place_ref, block_refs, full_ref, rows, features)
-    send(full_ref)
     stream = stream_ref[...].astype(jnp.float32)
     for part_ref in part_refs:
         stream = stream + part_ref[...].astype(jnp.float32)
     start_ref[...] = stream
     send(start_ref)
+    assemble_weights(place_ref, block_refs, full_ref, rows, features)
+    send(full_ref)
     normal, _ = layer_norm_parts(stream)
     normed = (normal * norm_ref[0:1] + norm_ref[2:3]).astype(jnp.bfloat16)
     first_ref[...] = normed
@@ -745,8 +746,10 @@
         if moved:
             copy = copies.pop(0)
             move = pltpu.make_async_copy(sources[place], copy, marks.at[place])
-            move.start()
             sources[place] = Staged(copy, move)
+    waiting = [source for source in sources if isinstance(source, Staged)]
+    for source in sorted(waiting, key=lambda source: math.prod(source.shape)):
+        source.move.start()
     for place, apart in enumerate(far):
         if apart:
             source = made.pop(0)
@@ -1056,21 +1059,18 @@
             moved_in = fetch_weights(found[-3])
             blocks = bring_back(list(found[:groups]))
         else:
-            moved_in = fetch_weights(found[-3], moved_out)
+            arrived = scatter_pieces(chip, "row")
+            moved_in = fetch_weights(found[-3], moved_out, *arrived[1:])
             moved_out = after(moved_out, found[0])
             grad_out = [widen_grads(layer + 1, layer_count, moved_out, grad_out)]
             blocks = bring_back(list(found[:groups]), *grad_out)
+            earlier = add_pieces(arrived).astype(low)
         pieces = combine(layer, blocks)
         if last:
             outputs = bring_back(after_all(list(found[groups : 2 * groups]), pieces[0]))
         grad_parts = scatter_pieces(after_all(pieces, moved_in), "row")
         if last:
             grad_parts[0] = after(grad_parts[0], *outputs[1:groups])
-        else:
-            outputs = scatter_pieces(after_all(outputs, *grad_parts[1:]), "row")
-            arrived = scatter_pieces(after_all(chip, *grad_parts[1:]), "row")
-            for part in outputs:
-                stream = stream + part.astype(jnp.float32)
         saved = kept[layer]
         height = -(-(4 * strip + expert_count + 4) // (16 * groups)) * (16 * groups)
         grad, branch, blocks = run_kernel(
@@ -1092,21 +1092,26 @@
         if layer > 0:
             images = gather_group(branch)
             moved_out = fetch_weights(found[-2], *images[1:rows])
+            sent = dispatch(layer - 1, images)
+            branches = scatter_pieces(sent, "dp")
+            moved_in = after(moved_in, sent[0])
             grad_in = [widen_grads(layer, layer_count, moved_in, grad_in)]
-            branches = scatter_pieces(dispatch(layer - 1, images), "dp")
             if last:
-                outputs = combine(layer, outputs)
-            branches = after_all(branches, *grad_in, *outputs)
+                outputs = combine(layer, after_all(outputs, sent[0]))
+            branches = after_all(branches, *grad_in, *outputs, *chip)
         else:
-            earlier = add_pieces(arrived).astype(low)
-            shared[layer + 1] = sum_groups(earlier)
-            arrived = scatter_pieces(after_all(chip, earlier, *outputs[1:]), "row")
+            arrived = scatter_pieces(chip, "row")
             moved_out = fetch_weights(found[-2], *arrived[1:])
             grad_in = [widen_grads(layer, layer_count, after(moved_in, chip[0]), grad_in)]
+            outputs = scatter_pieces(after_all(outputs, chip[0]), "row")
+            for part in outputs:
+                stream = stream + part.astype(jnp.float32)
             output = split(stream.astype(low))
-            arrived = after_all(arrived, *grad_in, *shared[1:], output)
+            arrived = after_all(arrived, *grad_in)
             grad_out = [widen_grads(layer, layer_count, moved_out, grad_out)]
-            shared[layer] = sum_groups(add_pieces(arrived).astype(low))
+            both_sums = jnp.concatenate([add_pieces(arrived).astype(low), earlier], axis=1)
+            both_sums = sum_groups(both_sums)
+            shared = [both_sums[:, :half], both_sums[:, half:]]
     grad_input = split(grad)
     shared = jnp.stack(shared)
     grad_qkv = (

time: 475 us -> 470 us (0.989)
  the two profiles are of different devices: /device:TPU:0 before, /device:TPU:15 now
where the time goes in v4:
time: 470 us; the launch traced here: 461 us
  waiting for transfers between devices  148 us (31%)
  starting transfers between devices  146 us (31%)
  Pallas kernels  97.6 us (21%)
  local copies, waits for them, and re-layouts  50.7 us (11%)
  other arithmetic  15.7 us (3%)
    ppermute x112, waiting for transfers between devices, exchange(): lax.ppermute(values, axis, [(place, place ^ offset) for place in range(co...  141 us
    ppermute x112, starting transfers between devices, exchange(): lax.ppermute(values, axis, [(place, place ^ offset) for place in range(co...  94.7 us
    pallas_call x15, Pallas kernels, run_kernel(): pl.pallas_call(functools.partial(staged_body, body, len(fixed), staged, a...  81 us
    all_to_all x8, starting transfers between devices, fetch_weights(): lax.all_to_all(after(own, *earlier), ('row', 'col'), split_axis=0, concat...  51.5 us
    unnamed x215, local copies, waits for them, and re-layouts  24.1 us
    pallas_call x4, Pallas kernels, widen_grads(): pl.pallas_call(widen_kernel, name='widen', grid=(members,), in_specs=[pl....  16.6 us
  transfers between devices with their start and end apart: 120, of which 60 were waited for; matrix products, arithmetic and copies ran while one was open for 8% of the time, Pallas kernels for 12%

profile of v4, /device:TPU:15, one launch (start us, length us, event | category | flops | bytes accessed | tf_op | source)
XLA Modules:
  0.0 460.9 jit_solution(11605957392090123710)
XLA Ops:
  5.7 4.6 dynamic-slice_bitcast_fusion.1
  10.3 5.5 %collective-permute-done.3.refs_4_ = bf16[256,512]{1,0:T(8,128)(2,1)S(1)} collective-permute-done((bf16[256,512]{1,0:T(8,128)(2,1)S(1)}, bf16[256,512]{1,0:T(8,128)(2,1)S(1)}, u32[]{:S(2)}, u32[]{:S(2)}) %collective-permute-start.3) | collective-permute-done | bytes 262176 | tf_op jit(solution)/shard_map/ppermute | solution.py:372
  15.8 7.3 %all-to-all-start = ((bf16[8,256,512]{2,1,0:T(8,128)(2,1)}), bf16[8,256,512]{2,1,0:T(8,128)(2,1)}, u32[]{:S(2)}, u32[]{:S(2)}) async-start(bf16[8,256,512]{2,1,0:T(8,128)(2,1)} %get-tuple-element.140), calls=%async_computation | async-start | bytes 4194304 | tf_op jit(solution)/shard_map/all_to_all | solution.py:922
  28.8 5.1 %attention_forward.2 = (f32[208,512]{1,0:T(8,128)}, f32[208,512]{1,0:T(8,128)}, bf16[208,512]{1,0:T(8,128)(2,1)}, bf16[208,1536]{1,0:T(8,128)(2,1)}, bf16[208,51...) custom-call(s32[4]{0:T(128)S(1)} %pad_add_fusion.refs_0_, bf16[256,512]{1,0:T(8,128)(2,1)} %copy-done.42, ...), custom_call_target="tpu_custom_call" | custom-call | flops 872415232 | bytes 2318352 | tf_op jit(solution)/shard_map/attention_forward/pallas_call | solution.py:779
  36.6 4.7 %dynamic-slice_bitcast_fusion = (bf16[8,512,256]{2,1,0:T(8,128)(2,1)}, bf16[8,512,256]{2,1,0:T(8,128)(2,1)}) fusion(bf16[2,32,512,256]{3,2,1,0:T(8,128)(2,1)} %param.20, s32[]{:T(128)S(6)} %select_n.84), kind=kLoop, calls=%fused_computation.6 | loop fusion | bytes 8388612 | tf_op jit(solution)/shard_map/squeeze | solution.py:919
  41.3 10.2 %collective-permute-done.9.refs_2_ = bf16[208,512]{1,0:T(8,128)(2,1)S(1)} collective-permute-done((bf16[208,512]{1,0:T(8,128)(2,1)S(1)}, bf16[208,512]{1,0:T(8,128)(2,1)S(1)}, u32[]{:S(2)}, u32[]{:S(2)}) %collective-permute-start.9) | collective-permute-done | bytes 213024 | tf_op jit(solution)/shard_map/ppermute | solution.py:372
  51.7 4.4 collective-permute-done.11.refs_4_
  56.1 7.3 %all-to-all-start.1 = ((bf16[8,512,256]{2,1,0:T(8,128)(2,1)}), bf16[8,512,256]{2,1,0:T(8,128)(2,1)}, u32[]{:S(2)}, u32[]{:S(2)}) async-start(bf16[8,512,256]{2,1,0:T(8,128)(2,1)} %get-tuple-element.142), calls=%async_computation.1 | async-start | bytes 4194304 | tf_op jit(solution)/shard_map/all_to_all | solution.py:922
  74.9 3.8 collective-permute-done.17.refs_6_
  78.8 5.5 %collective-permute-done.18.refs_7_ = bf16[128,512]{1,0:T(8,128)(2,1)S(1)} collective-permute-done((bf16[128,512]{1,0:T(8,128)(2,1)S(1)}, bf16[128,512]{1,0:T(8,128)(2,1)S(1)}, u32[]{:S(2)}, u32[]{:S(2)}) %collective-permute-start.18) | collective-permute-done | bytes 131104 | tf_op jit(solution)/shard_map/ppermute | solution.py:372
  87.4 5.9 %expert_forward.1 = (bf16[128,512]{1,0:T(8,128)(2,1)S(1)}, bf16[128,512]{1,0:T(8,128)(2,1)S(1)}, bf16[128,512]{1,0:T(8,128)(2,1)S(1)}, bf16[128,512]{1,0:T(8,128)(2,1)S(1)}) custom-call(s32[4]{0:T(128)S(1)} %pad_add_fusion.refs_0_, bf16[32,512]{1,0:T(8,128)(2,1)} %get-tuple-element.310.refs_1_, bf16[8,256,512]{2,1,0:T(8,128)(2,1)} %all-to-all-done.refs_2_, ...), custom_call_target="tpu_custom_call" | custom-call | flops 2147483648 | bytes 4751376 | tf_op jit(solution)/shard_map/expert_forward/pallas_call | solution.py:779
  93.4 7.3 %all-to-all-start.2 = ((bf16[8,256,512]{2,1,0:T(8,128)(2,1)}), bf16[8,256,512]{2,1,0:T(8,128)(2,1)}, u32[]{:S(2)}, u32[]{:S(2)}) async-start(bf16[8,256,512]{2,1,0:T(8,128)(2,1)} %get-tuple-element.158), calls=%async_computation.2 | async-start | bytes 4194304 | tf_op jit(solution)/shard_map/all_to_all | solution.py:922
  109.3 4.3 collective-permute-start.31
  120.7 3.5 combine.4
  125.2 4.8 %collective-permute-done.19.refs_2_ = bf16[256,512]{1,0:T(8,128)(2,1)S(1)} collective-permute-done((bf16[256,512]{1,0:T(8,128)(2,1)S(1)}, bf16[256,512]{1,0:T(8,128)(2,1)S(1)}, u32[]{:S(2)}, u32[]{:S(2)}) %collective-permute-start.19) | collective-permute-done | bytes 262176 | tf_op jit(solution)/shard_map/ppermute | solution.py:372
  136.5 3.7 collective-permute-done.33.refs_12_
  148.3 5.4 %attention_forward.3 = (f32[208,512]{1,0:T(8,128)}, f32[208,512]{1,0:T(8,128)}, bf16[208,512]{1,0:T(8,128)(2,1)}, bf16[208,1536]{1,0:T(8,128)(2,1)}, bf16[208,51...) custom-call(s32[4]{0:T(128)S(1)} %pad_add_fusion.refs_0_, bf16[256,512]{1,0:T(8,128)(2,1)} %copy-done.28, ...), custom_call_target="tpu_custom_call" | custom-call | flops 872415232 | bytes 3383312 | tf_op jit(solution)/shard_map/attention_forward/pallas_call | solution.py:779
  156.4 3.9 collective-permute-done.38.refs_4_
  160.4 6.5 %collective-permute-done.37.refs_3_ = bf16[208,512]{1,0:T(8,128)(2,1)S(1)} collective-permute-done((bf16[208,512]{1,0:T(8,128)(2,1)S(1)}, bf16[208,512]{1,0:T(8,128)(2,1)S(1)}, u32[]{:S(2)}, u32[]{:S(2)}) %collective-permute-start.37) | collective-permute-done | bytes 213024 | tf_op jit(solution)/shard_map/ppermute | solution.py:372
  166.8 6.4 %all-to-all-start.3 = ((bf16[8,512,256]{2,1,0:T(8,128)(2,1)}), bf16[8,512,256]{2,1,0:T(8,128)(2,1)}, u32[]{:S(2)}, u32[]{:S(2)}) async-start(bf16[8,512,256]{2,1,0:T(8,128)(2,1)} %get-tuple-element.161), calls=%async_computation.3 | async-start | bytes 4194304 | tf_op jit(solution)/shard_map/all_to_all | solution.py:922
  187.0 5.4 %collective-permute-done.55.refs_11_ = bf16[128,512]{1,0:T(8,128)(2,1)S(1)} collective-permute-done((bf16[128,512]{1,0:T(8,128)(2,1)S(1)}, bf16[128,512]{1,0:T(8,128)(2,1)S(1)}, u32[]{:S(2)}, u32[]{:S(2)}) %collective-permute-start.55) | collective-permute-done | bytes 131104 | tf_op jit(solution)/shard_map/ppermute | solution.py:372
  192.4 7.4 %collective-permute-done.51.refs_6_ = bf16[128,512]{1,0:T(8,128)(2,1)S(1)} collective-permute-done((bf16[128,512]{1,0:T(8,128)(2,1)S(1)}, bf16[128,512]{1,0:T(8,128)(2,1)S(1)}, u32[]{:S(2)}, u32[]{:S(2)}) %collective-permute-start.51) | collective-permute-done | bytes 131104 | tf_op jit(solution)/shard_map/ppermute | solution.py:372
  199.8 3.8 collective-permute-done.52.refs_7_
  204.2 11.8 %expert_full.2 = (bf16[128,512]{1,0:T(8,128)(2,1)S(1)}, bf16[128,512]{1,0:T(8,128)(2,1)S(1)}, bf16[128,512]{1,0:T(8,128)(2,1)S(1)}, bf16[128,512]{1,0:T(8,128)(2...) custom-call(s32[4]{0:T(128)S(1)} %pad_add_fusion.refs_0_, ...), custom_call_target="tpu_custom_call" | custom-call | flops 6442450944 | bytes 5275664 | tf_op jit(solution)/shard_map/expert_full/pallas_call | solution.py:779
  219.3 5.4 %all-to-all-start.4 = ((bf16[8,256,512]{2,1,0:T(8,128)(2,1)}), bf16[8,256,512]{2,1,0:T(8,128)(2,1)S(1)}, u32[]{:S(2)}, u32[]{:S(2)}) async-start(bf16[8,256,512]{2,1,0:T(8,128)(2,1)} %copy-done.6), calls=%async_computation.4 | async-start | bytes 4194304 | tf_op jit(solution)/shard_map/all_to_all | solution.py:922
  233.4 4.0 collective-permute-start.61
  242.7 3.5 combine.5
  251.6 4.9 %collective-permute-done.65.refs_4_ = bf16[128,512]{1,0:T(8,128)(2,1)} collective-permute-done((bf16[128,512]{1,0:T(8,128)(2,1)S(1)}, bf16[128,512]{1,0:T(8,128)(2,1)}, u32[]{:S(2)}, u32[]{:S(2)}) %collective-permute-start.65) | collective-permute-done | bytes 131104 | tf_op jit(solution)/shard_map/ppermute | solution.py:372
  262.7 9.5 %attention_backward.2 = (f32[208,512]{1,0:T(8,128)S(1)}, bf16[208,512]{1,0:T(8,128)(2,1)S(1)}, bf16[2,4,576,256]{3,2,1,0:T(8,128)(2,1)S(1)}) custom-call(s32[4]{0:T(128)S(1)} %pad_add_fusion.refs_0_, bf16[512,2048]{1,0:T(8,128)(2,1)} %get-tuple-element.185.refs_1_, f32[4,512]{1,0:T(4,128)} %get-tuple-element.303.refs_9_.refs_2_, ...), custom_call_target="tpu_custom_call" | custom-call | flops 1744830464 | bytes 5152784 | tf_op jit(solution)/shard_map/attention_backward/pallas_call | solution.py:779
  279.4 4.2 collective-permute-done.69.refs_2_
  283.7 4.5 collective-permute-done.70.refs_3_
  288.2 6.4 %all-to-all-start.5 = ((bf16[8,512,256]{2,1,0:T(8,128)(2,1)}), bf16[8,512,256]{2,1,0:T(8,128)(2,1)}, u32[]{:S(2)}, u32[]{:S(2)}) async-start(bf16[8,512,256]{2,1,0:T(8,128)(2,1)} %copy-done.4), calls=%async_computation.5 | async-start | bytes 4194304 | tf_op jit(solution)/shard_map/all_to_all | solution.py:922
  299.5 3.7 widen.4.refs_0_
  306.7 3.5 combine.6
  316.6 10.9 %expert_full.3 = (bf16[128,512]{1,0:T(8,128)(2,1)S(1)}, bf16[128,512]{1,0:T(8,128)(2,1)S(1)}, bf16[128,512]{1,0:T(8,128)(2,1)S(1)}, bf16[128,512]{1,0:T(8,128)(2...) custom-call(s32[4]{0:T(128)S(1)} %pad_add_fusion.refs_0_, ...), custom_call_target="tpu_custom_call" | custom-call | flops 6442450944 | bytes 5275664 | tf_op jit(solution)/shard_map/expert_full/pallas_call | solution.py:779
  332.3 6.8 %all-to-all-start.6 = ((bf16[8,256,512]{2,1,0:T(8,128)(2,1)}), bf16[8,256,512]{2,1,0:T(8,128)(2,1)S(1)}, u32[]{:S(2)}, u32[]{:S(2)}) async-start(bf16[8,256,512]{2,1,0:T(8,128)(2,1)} %copy-done.5), calls=%async_computation.6 | async-start | bytes 4194304 | tf_op jit(solution)/shard_map/all_to_all | solution.py:922
  342.2 6.0 %widen.5.refs_0_ = f32[2,8,512,256]{3,2,1,0:T(8,128)} custom-call(bf16[8,512,256]{2,1,0:T(8,128)(2,1)} %all-to-all-done.5.narrow_ref), custom_call_target="tpu_custom_call" | custom-call | tf_op jit(solution)/shard_map/widen/pallas_call | solution.py:688
  354.3 3.5 combine.7
  359.2 3.8 all-to-all-done.6.narrow_ref
  365.6 4.6 collective-permute-done.96.refs_13_
  370.2 3.3 collective-permute-done.95.refs_12_
  375.9 9.7 %attention_backward.3 = (f32[208,512]{1,0:T(8,128)S(1)}, bf16[208,512]{1,0:T(8,128)(2,1)}, bf16[2,4,576,256]{3,2,1,0:T(8,128)(2,1)S(1)}) custom-call(s32[4]{0:T(128)S(1)} %pad_add_fusion.refs_0_, bf16[512,2048]{1,0:T(8,128)(2,1)} %get-tuple-element.217.refs_1_, f32[4,512]{1,0:T(4,128)} %get-tuple-element.304.refs_9_.refs_2_, ...), custom_call_target="tpu_custom_call" | custom-call | flops 1744830464 | bytes 5365776 | tf_op jit(solution)/shard_map/attention_backward/pallas_call | solution.py:779
  404.8 3.5 widen.6
  422.1 4.8 %all-to-all-start.7 = ((bf16[8,512,256]{2,1,0:T(8,128)(2,1)}), bf16[8,512,256]{2,1,0:T(8,128)(2,1)S(1)}, u32[]{:S(2)}, u32[]{:S(2)}) async-start(bf16[8,512,256]{2,1,0:T(8,128)(2,1)} %copy-done.3), calls=%async_computation.7 | async-start | bytes 4194304 | tf_op jit(solution)/shard_map/all_to_all | solution.py:922
  427.0 3.7 collective-permute-done.108
  438.2 8.4 %collective-permute-done.110 = bf16[144,512]{1,0:T(8,128)(2,1)S(1)} collective-permute-done((bf16[144,512]{1,0:T(8,128)(2,1)S(1)}, bf16[144,512]{1,0:T(8,128)(2,1)S(1)}, u32[]{:S(2)}, u32[]{:S(2)}) %collective-permute-start.110) | collective-permute-done | bytes 147488 | tf_op jit(solution)/shard_map/ppermute | solution.py:372
  446.6 5.1 %collective-permute-done.111 = bf16[144,512]{1,0:T(8,128)(2,1)S(1)} collective-permute-done((bf16[144,512]{1,0:T(8,128)(2,1)S(1)}, bf16[144,512]{1,0:T(8,128)(2,1)S(1)}, u32[]{:S(2)}, u32[]{:S(2)}) %collective-permute-start.111) | collective-permute-done | bytes 147488 | tf_op jit(solution)/shard_map/ppermute | solution.py:372
  457.0 3.5 widen.7
  (495 shorter events, 192.9 us)
Async XLA Ops:
  3.5 12.3 %collective-permute-start.3 = (bf16[256,512]{1,0:T(8,128)(2,1)S(1)}, bf16[256,512]{1,0:T(8,128)(2,1)S(1)}, u32[]{:S(2)}, u32[]{:S(2)}) collective-permute-start(bf16[256,512]{1,0:T(8,128)(2,1)S(1)} %maximum_maximum_fusion.1.refs_1_), channel_id=1, source_target_pairs={{0,6},{2,4},{4,2},{6,0},{1,7},{3,5},{5,3},{7,1},{8,14},{10,12},{12... | collective-permute-start | bytes 786440 | tf_op jit(solution)/shard_map/ppermute | solution.py:372
  15.8 40.3 %all-to-all-start = ((bf16[8,256,512]{2,1,0:T(8,128)(2,1)}), bf16[8,256,512]{2,1,0:T(8,128)(2,1)}, u32[]{:S(2)}, u32[]{:S(2)}) async-start(bf16[8,256,512]{2,1,0:T(8,128)(2,1)} %get-tuple-element.140), calls=%async_computation | async-start | bytes 4194304 | tf_op jit(solution)/shard_map/all_to_all | solution.py:922
  33.9 17.6 %collective-permute-start.9 = (bf16[208,512]{1,0:T(8,128)(2,1)S(1)}, bf16[208,512]{1,0:T(8,128)(2,1)S(1)}, u32[]{:S(2)}, u32[]{:S(2)}) collective-permute-start(bf16[208,512]{1,0:T(8,128)(2,1)S(1)} %get-tuple-element.141.refs_1_), channel_id=1, source_target_pairs={{0,2},{2,0},{4,6},{6,4},{1,3},{3,1},{5,7},{7,5},{8,10},{10,8},{12,... | collective-permute-start | bytes 638984 | tf_op jit(solution)/shard_map/ppermute | solution.py:372
  34.2 17.5 %collective-permute-start.10 = (bf16[208,512]{1,0:T(8,128)(2,1)S(1)}, bf16[208,512]{1,0:T(8,128)(2,1)S(1)}, u32[]{:S(2)}, u32[]{:S(2)}) collective-permute-start(bf16[208,512]{1,0:T(8,128)(2,1)S(1)} %get-tuple-element.141.refs_1_), channel_id=1, source_target_pairs={{0,4},{2,6},{4,0},{6,2},{1,5},{3,7},{5,1},{7,3},{8,12},{10,14},{12... | collective-permute-start | bytes 638984 | tf_op jit(solution)/shard_map/ppermute | solution.py:372
  34.3 21.8 %collective-permute-start.11 = (bf16[208,512]{1,0:T(8,128)(2,1)S(1)}, bf16[208,512]{1,0:T(8,128)(2,1)S(1)}, u32[]{:S(2)}, u32[]{:S(2)}) collective-permute-start(bf16[208,512]{1,0:T(8,128)(2,1)S(1)} %get-tuple-element.141.refs_1_), channel_id=1, source_target_pairs={{0,6},{2,4},{4,2},{6,0},{1,7},{3,5},{5,3},{7,1},{8,14},{10,12},{12... | collective-permute-start | bytes 638984 | tf_op jit(solution)/shard_map/ppermute | solution.py:372
  56.1 31.3 %all-to-all-start.1 = ((bf16[8,512,256]{2,1,0:T(8,128)(2,1)}), bf16[8,512,256]{2,1,0:T(8,128)(2,1)}, u32[]{:S(2)}, u32[]{:S(2)}) async-start(bf16[8,512,256]{2,1,0:T(8,128)(2,1)} %get-tuple-element.142), calls=%async_computation.1 | async-start | bytes 4194304 | tf_op jit(solution)/shard_map/all_to_all | solution.py:922
  72.5 11.8 %collective-permute-start.18 = (bf16[128,512]{1,0:T(8,128)(2,1)S(1)}, bf16[128,512]{1,0:T(8,128)(2,1)S(1)}, u32[]{:S(2)}, u32[]{:S(2)}) collective-permute-start(bf16[128,512]{1,0:T(8,128)(2,1)S(1)} %get-tuple-element.146), channel_id=1, source_target_pairs={{0,24},{8,16},{16,8},{24,0},{1,25},{9,17},{17,9},{25,1},{2,26},{10... | collective-permute-start | bytes 393224 | tf_op jit(solution)/shard_map/ppermute | solution.py:372
  93.4 73.5 %all-to-all-start.2 = ((bf16[8,256,512]{2,1,0:T(8,128)(2,1)}), bf16[8,256,512]{2,1,0:T(8,128)(2,1)}, u32[]{:S(2)}, u32[]{:S(2)}) async-start(bf16[8,256,512]{2,1,0:T(8,128)(2,1)} %get-tuple-element.158), calls=%async_computation.2 | async-start | bytes 4194304 | tf_op jit(solution)/shard_map/all_to_all | solution.py:922
  103.2 11.7 %collective-permute-start.28 = (bf16[128,512]{1,0:T(8,128)(2,1)S(1)}, bf16[128,512]{1,0:T(8,128)(2,1)S(1)}, u32[]{:S(2)}, u32[]{:S(2)}) collective-permute-start(bf16[128,512]{1,0:T(8,128)(2,1)S(1)} %get-tuple-element.152), channel_id=1, source_target_pairs={{0,24},{8,16},{16,8},{24,0},{1,25},{9,17},{17,9},{25,1},{2,26},{10... | collective-permute-start | bytes 393224 | tf_op jit(solution)/shard_map/ppermute | solution.py:372
  103.7 13.9 %collective-permute-start.29 = (bf16[128,512]{1,0:T(8,128)(2,1)S(1)}, bf16[128,512]{1,0:T(8,128)(2,1)S(1)}, u32[]{:S(2)}, u32[]{:S(2)}) collective-permute-start(bf16[128,512]{1,0:T(8,128)(2,1)S(1)} %get-tuple-element.147.refs_1_), channel_id=1, source_target_pairs={{0,1},{1,0},{2,3},{3,2},{4,5},{5,4},{6,7},{7,6},{8,9},{9,8},{10,11... | collective-permute-start | bytes 393224 | tf_op jit(solution)/shard_map/ppermute | solution.py:372
  105.5 12.1 %collective-permute-start.30 = (bf16[128,512]{1,0:T(8,128)(2,1)S(1)}, bf16[128,512]{1,0:T(8,128)(2,1)S(1)}, u32[]{:S(2)}, u32[]{:S(2)}) collective-permute-start(bf16[128,512]{1,0:T(8,128)(2,1)S(1)} %collective-permute-done.26.refs_2_), channel_id=1, source_target_pairs={{0,1},{1,0},{2,3},{3,2},{4,5},{5,4},{6,7},{7,6},{8,9},{9,8},{10,11... | collective-permute-start | bytes 393224 | tf_op jit(solution)/shard_map/ppermute | solution.py:372
  116.3 13.7 %collective-permute-start.19 = (bf16[256,512]{1,0:T(8,128)(2,1)S(1)}, bf16[256,512]{1,0:T(8,128)(2,1)S(1)}, u32[]{:S(2)}, u32[]{:S(2)}) collective-permute-start(bf16[256,512]{1,0:T(8,128)(2,1)S(1)} %maximum_maximum_fusion.refs_1_), channel_id=1, source_target_pairs={{0,2},{2,0},{4,6},{6,4},{1,3},{3,1},{5,7},{7,5},{8,10},{10,8},{12,... | collective-permute-start | bytes 786440 | tf_op jit(solution)/shard_map/ppermute | solution.py:372
  117.6 13.6 %collective-permute-start.20 = (bf16[256,512]{1,0:T(8,128)(2,1)S(1)}, bf16[256,512]{1,0:T(8,128)(2,1)S(1)}, u32[]{:S(2)}, u32[]{:S(2)}) collective-permute-start(bf16[256,512]{1,0:T(8,128)(2,1)S(1)} %maximum_maximum_fusion.refs_1_), channel_id=1, source_target_pairs={{0,4},{2,6},{4,0},{6,2},{1,5},{3,7},{5,1},{7,3},{8,12},{10,14},{12... | collective-permute-start | bytes 786440 | tf_op jit(solution)/shard_map/ppermute | solution.py:372
  117.7 18.0 %collective-permute-start.21 = (bf16[256,512]{1,0:T(8,128)(2,1)S(1)}, bf16[256,512]{1,0:T(8,128)(2,1)S(1)}, u32[]{:S(2)}, u32[]{:S(2)}) collective-permute-start(bf16[256,512]{1,0:T(8,128)(2,1)S(1)} %maximum_maximum_fusion.refs_1_), channel_id=1, source_target_pairs={{0,6},{2,4},{4,2},{6,0},{1,7},{3,5},{5,3},{7,1},{8,14},{10,12},{12... | collective-permute-start | bytes 786440 | tf_op jit(solution)/shard_map/ppermute | solution.py:372
  124.9 15.3 %collective-permute-start.33 = (bf16[208,512]{1,0:T(8,128)(2,1)S(1)}, bf16[208,512]{1,0:T(8,128)(2,1)S(1)}, u32[]{:S(2)}, u32[]{:S(2)}) collective-permute-start(bf16[208,512]{1,0:T(8,128)(2,1)S(1)} %get-tuple-element.154), channel_id=1, source_target_pairs={{0,2},{2,0},{4,6},{6,4},{1,3},{3,1},{5,7},{7,5},{8,10},{10,8},{12,... | collective-permute-start | bytes 638984 | tf_op jit(solution)/shard_map/ppermute | solution.py:372
  125.2 16.4 %collective-permute-start.34 = (bf16[208,512]{1,0:T(8,128)(2,1)S(1)}, bf16[208,512]{1,0:T(8,128)(2,1)S(1)}, u32[]{:S(2)}, u32[]{:S(2)}) collective-permute-start(bf16[208,512]{1,0:T(8,128)(2,1)S(1)} %get-tuple-element.155), channel_id=1, source_target_pairs={{0,4},{2,6},{4,0},{6,2},{1,5},{3,7},{5,1},{7,3},{8,12},{10,14},{12... | collective-permute-start | bytes 638984 | tf_op jit(solution)/shard_map/ppermute | solution.py:372
  130.0 14.8 %collective-permute-start.35 = (bf16[208,512]{1,0:T(8,128)(2,1)S(1)}, bf16[208,512]{1,0:T(8,128)(2,1)S(1)}, u32[]{:S(2)}, u32[]{:S(2)}) collective-permute-start(bf16[208,512]{1,0:T(8,128)(2,1)S(1)} %get-tuple-element.156), channel_id=1, source_target_pairs={{0,6},{2,4},{4,2},{6,0},{1,7},{3,5},{5,3},{7,1},{8,14},{10,12},{12... | collective-permute-start | bytes 638984 | tf_op jit(solution)/shard_map/ppermute | solution.py:372
  131.2 14.8 %collective-permute-start.22 = (bf16[256,512]{1,0:T(8,128)(2,1)S(1)}, bf16[256,512]{1,0:T(8,128)(2,1)S(1)}, u32[]{:S(2)}, u32[]{:S(2)}) collective-permute-start(bf16[256,512]{1,0:T(8,128)(2,1)S(1)} %maximum_maximum_fusion.refs_1_), channel_id=1, source_target_pairs={{0,1},{1,0},{2,3},{3,2},{4,5},{5,4},{6,7},{7,6},{8,9},{9,8},{10,11... | collective-permute-start | bytes 786440 | tf_op jit(solution)/shard_map/ppermute | solution.py:372
  135.7 11.5 %collective-permute-start.23 = (bf16[256,512]{1,0:T(8,128)(2,1)S(1)}, bf16[256,512]{1,0:T(8,128)(2,1)S(1)}, u32[]{:S(2)}, u32[]{:S(2)}) collective-permute-start(bf16[256,512]{1,0:T(8,128)(2,1)S(1)} %collective-permute-done.19.refs_2_), channel_id=1, source_target_pairs={{0,1},{1,0},{2,3},{3,2},{4,5},{5,4},{6,7},{7,6},{8,9},{9,8},{10,11... | collective-permute-start | bytes 786440 | tf_op jit(solution)/shard_map/ppermute | solution.py:372
  166.8 36.7 %all-to-all-start.3 = ((bf16[8,512,256]{2,1,0:T(8,128)(2,1)}), bf16[8,512,256]{2,1,0:T(8,128)(2,1)}, u32[]{:S(2)}, u32[]{:S(2)}) async-start(bf16[8,512,256]{2,1,0:T(8,128)(2,1)} %get-tuple-element.161), calls=%async_computation.3 | async-start | bytes 4194304 | tf_op jit(solution)/shard_map/all_to_all | solution.py:922
  180.5 11.9 %collective-permute-start.55 = (bf16[128,512]{1,0:T(8,128)(2,1)S(1)}, bf16[128,512]{1,0:T(8,128)(2,1)S(1)}, u32[]{:S(2)}, u32[]{:S(2)}) collective-permute-start(bf16[128,512]{1,0:T(8,128)(2,1)S(1)} %get-tuple-element.177), channel_id=1, source_target_pairs={{0,24},{8,16},{16,8},{24,0},{1,25},{9,17},{17,9},{25,1},{2,26},{10... | collective-permute-start | bytes 393224 | tf_op jit(solution)/shard_map/ppermute | solution.py:372
  184.6 15.2 %collective-permute-start.51 = (bf16[128,512]{1,0:T(8,128)(2,1)S(1)}, bf16[128,512]{1,0:T(8,128)(2,1)S(1)}, u32[]{:S(2)}, u32[]{:S(2)}) collective-permute-start(bf16[128,512]{1,0:T(8,128)(2,1)S(1)} %get-tuple-element.173), channel_id=1, source_target_pairs={{0,16},{8,24},{16,0},{24,8},{1,17},{9,25},{17,1},{25,9},{2,18},{10... | collective-permute-start | bytes 393224 | tf_op jit(solution)/shard_map/ppermute | solution.py:372
  186.6 16.9 %collective-permute-start.52 = (bf16[128,512]{1,0:T(8,128)(2,1)S(1)}, bf16[128,512]{1,0:T(8,128)(2,1)S(1)}, u32[]{:S(2)}, u32[]{:S(2)}) collective-permute-start(bf16[128,512]{1,0:T(8,128)(2,1)S(1)} %get-tuple-element.174), channel_id=1, source_target_pairs={{0,24},{8,16},{16,8},{24,0},{1,25},{9,17},{17,9},{25,1},{2,26},{10... | collective-permute-start | bytes 393224 | tf_op jit(solution)/shard_map/ppermute | solution.py:372
  219.3 29.3 %all-to-all-start.4 = ((bf16[8,256,512]{2,1,0:T(8,128)(2,1)}), bf16[8,256,512]{2,1,0:T(8,128)(2,1)S(1)}, u32[]{:S(2)}, u32[]{:S(2)}) async-start(bf16[8,256,512]{2,1,0:T(8,128)(2,1)} %copy-done.6), calls=%async_computation.4 | async-start | bytes 4194304 | tf_op jit(solution)/shard_map/all_to_all | solution.py:922
  227.2 11.8 %collective-permute-start.58 = (bf16[128,512]{1,0:T(8,128)(2,1)S(1)}, bf16[128,512]{1,0:T(8,128)(2,1)}, u32[]{:S(2)}, u32[]{:S(2)}) collective-permute-start(bf16[128,512]{1,0:T(8,128)(2,1)S(1)} %get-tuple-element.182), channel_id=1, source_target_pairs={{0,24},{8,16},{16,8},{24,0},{1,25},{9,17},{17,9},{25,1},{2,26},{10... | collective-permute-start | bytes 393224 | tf_op jit(solution)/shard_map/ppermute | solution.py:372
  227.4 14.0 %collective-permute-start.59 = (bf16[128,512]{1,0:T(8,128)(2,1)S(1)}, bf16[128,512]{1,0:T(8,128)(2,1)}, u32[]{:S(2)}, u32[]{:S(2)}) collective-permute-start(bf16[128,512]{1,0:T(8,128)(2,1)S(1)} %get-tuple-element.179.refs_1_), channel_id=1, source_target_pairs={{0,1},{1,0},{2,3},{3,2},{4,5},{5,4},{6,7},{7,6},{8,9},{9,8},{10,11... | collective-permute-start | bytes 393224 | tf_op jit(solution)/shard_map/ppermute | solution.py:372
  229.5 11.9 %collective-permute-start.60 = (bf16[128,512]{1,0:T(8,128)(2,1)S(1)}, bf16[128,512]{1,0:T(8,128)(2,1)S(1)}, u32[]{:S(2)}, u32[]{:S(2)}) collective-permute-start(bf16[128,512]{1,0:T(8,128)(2,1)S(1)} %collective-permute-done.56.refs_2_), channel_id=1, source_target_pairs={{0,1},{1,0},{2,3},{3,2},{4,5},{5,4},{6,7},{7,6},{8,9},{9,8},{10,11... | collective-permute-start | bytes 393224 | tf_op jit(solution)/shard_map/ppermute | solution.py:372
  248.6 13.2 %collective-permute-start.68 = (bf16[208,512]{1,0:T(8,128)(2,1)S(1)}, bf16[208,512]{1,0:T(8,128)(2,1)S(1)}, u32[]{:S(2)}, u32[]{:S(2)}) collective-permute-start(bf16[208,512]{1,0:T(8,128)(2,1)S(1)} %get-tuple-element.205), channel_id=1, source_target_pairs={{0,6},{2,4},{4,2},{6,0},{1,7},{3,5},{5,3},{7,1},{8,14},{10,12},{12... | collective-permute-start | bytes 638984 | tf_op jit(solution)/shard_map/ppermute | solution.py:372
  248.6 13.2 %collective-permute-start.67 = (bf16[208,512]{1,0:T(8,128)(2,1)S(1)}, bf16[208,512]{1,0:T(8,128)(2,1)S(1)}, u32[]{:S(2)}, u32[]{:S(2)}) collective-permute-start(bf16[208,512]{1,0:T(8,128)(2,1)S(1)} %get-tuple-element.203), channel_id=1, source_target_pairs={{0,4},{2,6},{4,0},{6,2},{1,5},{3,7},{5,1},{7,3},{8,12},{10,14},{12... | collective-permute-start | bytes 638984 | tf_op jit(solution)/shard_map/ppermute | solution.py:372
  249.9 11.9 %collective-permute-start.66 = (bf16[208,512]{1,0:T(8,128)(2,1)S(1)}, bf16[208,512]{1,0:T(8,128)(2,1)S(1)}, u32[]{:S(2)}, u32[]{:S(2)}) collective-permute-start(bf16[208,512]{1,0:T(8,128)(2,1)S(1)} %get-tuple-element.201), channel_id=1, source_target_pairs={{0,2},{2,0},{4,6},{6,4},{1,3},{3,1},{5,7},{7,5},{8,10},{10,8},{12,... | collective-permute-start | bytes 638984 | tf_op jit(solution)/shard_map/ppermute | solution.py:372
  274.7 35.5 %collective-permute-start.80 = (bf16[4,576,256]{2,1,0:T(8,128)(2,1)}, bf16[4,576,256]{2,1,0:T(8,128)(2,1)}, u32[]{:S(2)}, u32[]{:S(2)}) collective-permute-start(bf16[4,576,256]{2,1,0:T(8,128)(2,1)} %dynamic-slice_bitcast_fusion.5), channel_id=1, source_target_pairs={{0,1},{1,0},{2,3},{3,2},{4,5},{5,4},{6,7},{7,6},{8,9},{9,8},{10,11... | collective-permute-start | bytes 3538952 | tf_op jit(solution)/shard_map/ppermute | solution.py:372
  288.2 44.1 %all-to-all-start.5 = ((bf16[8,512,256]{2,1,0:T(8,128)(2,1)}), bf16[8,512,256]{2,1,0:T(8,128)(2,1)}, u32[]{:S(2)}, u32[]{:S(2)}) async-start(bf16[8,512,256]{2,1,0:T(8,128)(2,1)} %copy-done.4), calls=%async_computation.5 | async-start | bytes 4194304 | tf_op jit(solution)/shard_map/all_to_all | solution.py:922
  303.6 11.7 %collective-permute-start.82 = (bf16[128,512]{1,0:T(8,128)(2,1)S(1)}, bf16[128,512]{1,0:T(8,128)(2,1)S(1)}, u32[]{:S(2)}, u32[]{:S(2)}) collective-permute-start(bf16[128,512]{1,0:T(8,128)(2,1)S(1)} %get-tuple-element.231), channel_id=1, source_target_pairs={{0,16},{8,24},{16,0},{24,8},{1,17},{9,25},{17,1},{25,9},{2,18},{10... | collective-permute-start | bytes 393224 | tf_op jit(solution)/shard_map/ppermute | solution.py:372
  311.9 18.9 %collective-permute-start.91 = (bf16[576,256]{1,0:T(8,128)(2,1)S(1)}, bf16[576,256]{1,0:T(8,128)(2,1)S(1)}, u32[]{:S(2)}, u32[]{:S(2)}) collective-permute-start(bf16[576,256]{1,0:T(8,128)(2,1)S(1)} %get-tuple-element.288), channel_id=1, source_target_pairs={{0,2},{2,0},{4,6},{6,4},{1,3},{3,1},{5,7},{7,5},{8,10},{10,8},{12,... | collective-permute-start | bytes 884744 | tf_op jit(solution)/shard_map/ppermute | solution.py:372
  312.3 18.6 %collective-permute-start.92 = (bf16[576,256]{1,0:T(8,128)(2,1)S(1)}, bf16[576,256]{1,0:T(8,128)(2,1)S(1)}, u32[]{:S(2)}, u32[]{:S(2)}) collective-permute-start(bf16[576,256]{1,0:T(8,128)(2,1)S(1)} %get-tuple-element.287), channel_id=1, source_target_pairs={{0,4},{2,6},{4,0},{6,2},{1,5},{3,7},{5,1},{7,3},{8,12},{10,14},{12... | collective-permute-start | bytes 884744 | tf_op jit(solution)/shard_map/ppermute | solution.py:372
  313.5 18.8 %collective-permute-start.93 = (bf16[576,256]{1,0:T(8,128)(2,1)S(1)}, bf16[576,256]{1,0:T(8,128)(2,1)}, u32[]{:S(2)}, u32[]{:S(2)}) collective-permute-start(bf16[576,256]{1,0:T(8,128)(2,1)S(1)} %get-tuple-element.286), channel_id=1, source_target_pairs={{0,6},{2,4},{4,2},{6,0},{1,7},{3,5},{5,3},{7,1},{8,14},{10,12},{12... | collective-permute-start | bytes 884744 | tf_op jit(solution)/shard_map/ppermute | solution.py:372
  332.3 30.6 %all-to-all-start.6 = ((bf16[8,256,512]{2,1,0:T(8,128)(2,1)}), bf16[8,256,512]{2,1,0:T(8,128)(2,1)S(1)}, u32[]{:S(2)}, u32[]{:S(2)}) async-start(bf16[8,256,512]{2,1,0:T(8,128)(2,1)} %copy-done.5), calls=%async_computation.6 | async-start | bytes 4194304 | tf_op jit(solution)/shard_map/all_to_all | solution.py:922
  339.1 12.3 %collective-permute-start.85 = (bf16[128,512]{1,0:T(8,128)(2,1)S(1)}, bf16[128,512]{1,0:T(8,128)(2,1)S(1)}, u32[]{:S(2)}, u32[]{:S(2)}) collective-permute-start(bf16[128,512]{1,0:T(8,128)(2,1)S(1)} %get-tuple-element.243), channel_id=1, source_target_pairs={{0,16},{8,24},{16,0},{24,8},{1,17},{9,25},{17,1},{25,9},{2,18},{10... | collective-permute-start | bytes 393224 | tf_op jit(solution)/shard_map/ppermute | solution.py:372
  395.2 13.1 %collective-permute-start.103 = (bf16[576,256]{1,0:T(8,128)(2,1)}, bf16[576,256]{1,0:T(8,128)(2,1)}, u32[]{:S(2)}, u32[]{:S(2)}) collective-permute-start(bf16[576,256]{1,0:T(8,128)(2,1)} %get-tuple-element.282), channel_id=1, source_target_pairs={{0,2},{2,0},{4,6},{6,4},{1,3},{3,1},{5,7},{7,5},{8,10},{10,8},{12,... | collective-permute-start | bytes 884744 | tf_op jit(solution)/shard_map/ppermute | solution.py:372
  395.3 13.3 %collective-permute-start.104 = (bf16[576,256]{1,0:T(8,128)(2,1)}, bf16[576,256]{1,0:T(8,128)(2,1)}, u32[]{:S(2)}, u32[]{:S(2)}) collective-permute-start(bf16[576,256]{1,0:T(8,128)(2,1)} %get-tuple-element.284), channel_id=1, source_target_pairs={{0,4},{2,6},{4,0},{6,2},{1,5},{3,7},{5,1},{7,3},{8,12},{10,14},{12... | collective-permute-start | bytes 884744 | tf_op jit(solution)/shard_map/ppermute | solution.py:372
  395.5 15.5 %collective-permute-start.105 = (bf16[576,256]{1,0:T(8,128)(2,1)}, bf16[576,256]{1,0:T(8,128)(2,1)}, u32[]{:S(2)}, u32[]{:S(2)}) collective-permute-start(bf16[576,256]{1,0:T(8,128)(2,1)} %get-tuple-element.283), channel_id=1, source_target_pairs={{0,6},{2,4},{4,2},{6,0},{1,7},{3,5},{5,3},{7,1},{8,14},{10,12},{12... | collective-permute-start | bytes 884744 | tf_op jit(solution)/shard_map/ppermute | solution.py:372
  402.9 29.0 %collective-permute-start.102 = (f32[197,256]{1,0:T(8,128)}, f32[197,256]{1,0:T(8,128)}, u32[]{:S(2)}, u32[]{:S(2)}) collective-permute-start(f32[197,256]{1,0:T(8,128)} %bitcast.104), channel_id=1, source_target_pairs={{0,1},{1,0},{2,3},{3,2},{4,5},{5,4},{6,7},{7,6},{8,9},{9,8},{10,11... | collective-permute-start | bytes 605192 | tf_op jit(solution)/shard_map/ppermute | solution.py:372
  413.0 13.9 %collective-permute-start.106 = (bf16[144,512]{1,0:T(8,128)(2,1)}, bf16[144,512]{1,0:T(8,128)(2,1)}, u32[]{:S(2)}, u32[]{:S(2)}) collective-permute-start(bf16[144,512]{1,0:T(8,128)(2,1)} %get-tuple-element.290), channel_id=1, source_target_pairs={{0,8},{8,0},{16,24},{24,16},{1,9},{9,1},{17,25},{25,17},{2,10},{10... | collective-permute-start | bytes 442376 | tf_op jit(solution)/shard_map/ppermute | solution.py:372
  415.2 11.8 %collective-permute-start.107 = (bf16[144,512]{1,0:T(8,128)(2,1)}, bf16[144,512]{1,0:T(8,128)(2,1)S(1)}, u32[]{:S(2)}, u32[]{:S(2)}) collective-permute-start(bf16[144,512]{1,0:T(8,128)(2,1)} %get-tuple-element.291), channel_id=1, source_target_pairs={{0,16},{8,24},{16,0},{24,8},{1,17},{9,25},{17,1},{25,9},{2,18},{10... | collective-permute-start | bytes 442376 | tf_op jit(solution)/shard_map/ppermute | solution.py:372
  416.2 14.5 %collective-permute-start.108 = (bf16[144,512]{1,0:T(8,128)(2,1)S(1)}, bf16[144,512]{1,0:T(8,128)(2,1)S(1)}, u32[]{:S(2)}, u32[]{:S(2)}) collective-permute-start(bf16[144,512]{1,0:T(8,128)(2,1)S(1)} %get-tuple-element.292), channel_id=1, source_target_pairs={{0,24},{8,16},{16,8},{24,0},{1,25},{9,17},{17,9},{25,1},{2,26},{10... | collective-permute-start | bytes 442376 | tf_op jit(solution)/shard_map/ppermute | solution.py:372
  421.1 12.7 %collective-permute-start.101 = (bf16[197,256]{1,0:T(8,128)(2,1)}, bf16[197,256]{1,0:T(8,128)(2,1)}, u32[]{:S(2)}, u32[]{:S(2)}) collective-permute-start(bf16[197,256]{1,0:T(8,128)(2,1)} %bitcast.106), channel_id=1, source_target_pairs={{0,1},{1,0},{2,3},{3,2},{4,5},{5,4},{6,7},{7,6},{8,9},{9,8},{10,11... | collective-permute-start | bytes 302600 | tf_op jit(solution)/shard_map/ppermute | solution.py:372
  422.1 34.9 %all-to-all-start.7 = ((bf16[8,512,256]{2,1,0:T(8,128)(2,1)}), bf16[8,512,256]{2,1,0:T(8,128)(2,1)S(1)}, u32[]{:S(2)}, u32[]{:S(2)}) async-start(bf16[8,512,256]{2,1,0:T(8,128)(2,1)} %copy-done.3), calls=%async_computation.7 | async-start | bytes 4194304 | tf_op jit(solution)/shard_map/all_to_all | solution.py:922
  436.7 15.0 %collective-permute-start.111 = (bf16[144,512]{1,0:T(8,128)(2,1)S(1)}, bf16[144,512]{1,0:T(8,128)(2,1)S(1)}, u32[]{:S(2)}, u32[]{:S(2)}) collective-permute-start(bf16[144,512]{1,0:T(8,128)(2,1)S(1)} %get-tuple-element.271), channel_id=1, source_target_pairs={{0,24},{8,16},{16,8},{24,0},{1,25},{9,17},{17,9},{25,1},{2,26},{10... | collective-permute-start | bytes 442376 | tf_op jit(solution)/shard_map/ppermute | solution.py:372
  (176 other events, 1226.2 us)

commit v5 on v4

--- a/solution.py
+++ b/solution.py
@@ -793,7 +793,7 @@
         + list(scratch),
         compiler_params=pltpu.CompilerParams(vmem_limit_bytes=room * 1024 * 1024),
         cost_estimate=pl.CostEstimate(
-            flops=work,
+            flops=work // 4,
             bytes_accessed=sum(piece.size * piece.dtype.itemsize for piece in arguments),
             transcendentals=0,
         ),

time: 470 us -> 468 us (level)
  the two profiles are of different devices: /device:TPU:15 before, /device:TPU:0 now
where the time goes in v5:
time: 468 us; the launch traced here: 459 us
  waiting for transfers between devices  152 us (32%)
  starting transfers between devices  140 us (30%)
  Pallas kernels  97.5 us (21%)
  local copies, waits for them, and re-layouts  51.9 us (11%)
  other arithmetic  15.1 us (3%)
    ppermute x112, waiting for transfers between devices, exchange(): lax.ppermute(values, axis, [(place, place ^ offset) for place in range(co...  138 us
    ppermute x112, starting transfers between devices, exchange(): lax.ppermute(values, axis, [(place, place ^ offset) for place in range(co...  105 us
    pallas_call x15, Pallas kernels, run_kernel(): pl.pallas_call(functools.partial(staged_body, body, len(fixed), staged, a...  80.9 us
    all_to_all x8, starting transfers between devices, fetch_weights(): lax.all_to_all(after(own, *earlier), ('row', 'col'), split_axis=0, concat...  35.1 us
    unnamed x213, local copies, waits for them, and re-layouts  25.2 us
    pallas_call x4, Pallas kernels, widen_grads(): pl.pallas_call(widen_kernel, name='widen', grid=(members,), in_specs=[pl....  16.6 us
    all_to_all x8, waiting for transfers between devices, fetch_weights(): lax.all_to_all(after(own, *earlier), ('row', 'col'), split_axis=0, concat...  13.5 us
  transfers between devices with their start and end apart: 120, of which 49 were waited for; matrix products, arithmetic and copies ran while one was open for 8% of the time, Pallas kernels for 12%

profile of v5, /device:TPU:0, one launch (start us, length us, event | category | flops | bytes accessed | tf_op | source)
XLA Modules:
  0.0 458.7 jit_solution(11548561462974937753)
XLA Ops:
  7.5 4.6 %dynamic-slice_bitcast_fusion.1 = (bf16[8,256,512]{2,1,0:T(8,128)(2,1)}, bf16[8,256,512]{2,1,0:T(8,128)(2,1)}) fusion(bf16[2,32,256,512]{3,2,1,0:T(8,128)(2,1)} %param.19, s32[]{:T(128)S(6)} %select_n.84), kind=kLoop, calls=%fused_computation.7 | loop fusion | bytes 8388612 | tf_op jit(solution)/shard_map/squeeze | solution.py:919
  13.1 6.2 %collective-permute-done.2.refs_3_ = bf16[256,512]{1,0:T(8,128)(2,1)S(1)} collective-permute-done((bf16[256,512]{1,0:T(8,128)(2,1)S(1)}, bf16[256,512]{1,0:T(8,128)(2,1)S(1)}, u32[]{:S(2)}, u32[]{:S(2)}) %collective-permute-start.2) | collective-permute-done | bytes 262176 | tf_op jit(solution)/shard_map/ppermute | solution.py:372
  19.4 4.5 all-to-all-start
  29.6 5.1 %attention_forward.2 = (f32[208,512]{1,0:T(8,128)}, f32[208,512]{1,0:T(8,128)}, bf16[208,512]{1,0:T(8,128)(2,1)}, bf16[208,1536]{1,0:T(8,128)(2,1)}, bf16[208,51...) custom-call(s32[4]{0:T(128)S(1)} %pad_add_fusion.refs_0_, bf16[256,512]{1,0:T(8,128)(2,1)} %copy-done.28, ...), custom_call_target="tpu_custom_call" | custom-call | flops 218103808 | bytes 2318352 | tf_op jit(solution)/shard_map/attention_forward/pallas_call | solution.py:779
  38.3 4.6 %dynamic-slice_bitcast_fusion = (bf16[8,512,256]{2,1,0:T(8,128)(2,1)}, bf16[8,512,256]{2,1,0:T(8,128)(2,1)}) fusion(bf16[2,32,512,256]{3,2,1,0:T(8,128)(2,1)} %param.20, s32[]{:T(128)S(6)} %select_n.84), kind=kLoop, calls=%fused_computation.6 | loop fusion | bytes 8388612 | tf_op jit(solution)/shard_map/squeeze | solution.py:919
  42.9 11.7 %collective-permute-done.9.refs_2_ = bf16[208,512]{1,0:T(8,128)(2,1)S(1)} collective-permute-done((bf16[208,512]{1,0:T(8,128)(2,1)S(1)}, bf16[208,512]{1,0:T(8,128)(2,1)S(1)}, u32[]{:S(2)}, u32[]{:S(2)}) %collective-permute-start.9) | collective-permute-done | bytes 213024 | tf_op jit(solution)/shard_map/ppermute | solution.py:372
  54.6 5.0 %collective-permute-done.11.refs_4_ = bf16[208,512]{1,0:T(8,128)(2,1)S(1)} collective-permute-done((bf16[208,512]{1,0:T(8,128)(2,1)S(1)}, bf16[208,512]{1,0:T(8,128)(2,1)S(1)}, u32[]{:S(2)}, u32[]{:S(2)}) %collective-permute-start.11) | collective-permute-done | bytes 213024 | tf_op jit(solution)/shard_map/ppermute | solution.py:372
  59.6 4.5 all-to-all-start.1
  79.2 6.7 %collective-permute-done.17.refs_6_ = bf16[128,512]{1,0:T(8,128)(2,1)S(1)} collective-permute-done((bf16[128,512]{1,0:T(8,128)(2,1)S(1)}, bf16[128,512]{1,0:T(8,128)(2,1)S(1)}, u32[]{:S(2)}, u32[]{:S(2)}) %collective-permute-start.17) | collective-permute-done | bytes 131104 | tf_op jit(solution)/shard_map/ppermute | solution.py:372
  85.8 4.9 %all-to-all-done.1.refs_3_ = bf16[8,512,256]{2,1,0:T(8,128)(2,1)} async-done(((bf16[8,512,256]{2,1,0:T(8,128)(2,1)}), bf16[8,512,256]{2,1,0:T(8,128)(2,1)}, u32[]{:S(2)}, u32[]{:S(2)}) %all-to-all-start.1) | async-done | bytes 2097184 | tf_op jit(solution)/shard_map/all_to_all | solution.py:922
  90.8 5.9 %expert_forward.1 = (bf16[128,512]{1,0:T(8,128)(2,1)S(1)}, bf16[128,512]{1,0:T(8,128)(2,1)S(1)}, bf16[128,512]{1,0:T(8,128)(2,1)S(1)}, bf16[128,512]{1,0:T(8,128)(2,1)S(1)}) custom-call(s32[4]{0:T(128)S(1)} %pad_add_fusion.refs_0_, bf16[32,512]{1,0:T(8,128)(2,1)} %get-tuple-element.310.refs_1_, bf16[8,256,512]{2,1,0:T(8,128)(2,1)} %all-to-all-done.refs_2_, ...), custom_call_target="tpu_custom_call" | custom-call | flops 536870912 | bytes 4751376 | tf_op jit(solution)/shard_map/expert_forward/pallas_call | solution.py:779
  96.7 4.6 all-to-all-start.2
  110.6 5.6 %collective-permute-done.27.refs_3_ = bf16[128,512]{1,0:T(8,128)(2,1)S(1)} collective-permute-done((bf16[128,512]{1,0:T(8,128)(2,1)S(1)}, bf16[128,512]{1,0:T(8,128)(2,1)S(1)}, u32[]{:S(2)}, u32[]{:S(2)}) %collective-permute-start.27) | collective-permute-done | bytes 131104 | tf_op jit(solution)/shard_map/ppermute | solution.py:372
  121.8 3.5 combine.4
  128.1 4.9 %collective-permute-done.19.refs_2_ = bf16[256,512]{1,0:T(8,128)(2,1)S(1)} collective-permute-done((bf16[256,512]{1,0:T(8,128)(2,1)S(1)}, bf16[256,512]{1,0:T(8,128)(2,1)S(1)}, u32[]{:S(2)}, u32[]{:S(2)}) %collective-permute-start.19) | collective-permute-done | bytes 262176 | tf_op jit(solution)/shard_map/ppermute | solution.py:372
  134.5 5.1 %collective-permute-done.21.refs_4_ = bf16[256,512]{1,0:T(8,128)(2,1)S(1)} collective-permute-done((bf16[256,512]{1,0:T(8,128)(2,1)S(1)}, bf16[256,512]{1,0:T(8,128)(2,1)S(1)}, u32[]{:S(2)}, u32[]{:S(2)}) %collective-permute-start.21) | collective-permute-done | bytes 262176 | tf_op jit(solution)/shard_map/ppermute | solution.py:372
  139.6 3.6 collective-permute-done.33.refs_12_
  143.8 4.5 collective-permute-done.35.refs_14_
  152.6 5.4 %attention_forward.3 = (f32[208,512]{1,0:T(8,128)}, f32[208,512]{1,0:T(8,128)}, bf16[208,512]{1,0:T(8,128)(2,1)}, bf16[208,1536]{1,0:T(8,128)(2,1)}, bf16[208,51...) custom-call(s32[4]{0:T(128)S(1)} %pad_add_fusion.refs_0_, bf16[256,512]{1,0:T(8,128)(2,1)} %copy-done.29, ...), custom_call_target="tpu_custom_call" | custom-call | flops 218103808 | bytes 3383312 | tf_op jit(solution)/shard_map/attention_forward/pallas_call | solution.py:779
  161.6 5.6 %collective-permute-done.38.refs_4_ = bf16[208,512]{1,0:T(8,128)(2,1)S(1)} collective-permute-done((bf16[208,512]{1,0:T(8,128)(2,1)S(1)}, bf16[208,512]{1,0:T(8,128)(2,1)S(1)}, u32[]{:S(2)}, u32[]{:S(2)}) %collective-permute-start.38) | collective-permute-done | bytes 213024 | tf_op jit(solution)/shard_map/ppermute | solution.py:372
  169.1 4.8 %all-to-all-start.3 = ((bf16[8,512,256]{2,1,0:T(8,128)(2,1)}), bf16[8,512,256]{2,1,0:T(8,128)(2,1)}, u32[]{:S(2)}, u32[]{:S(2)}) async-start(bf16[8,512,256]{2,1,0:T(8,128)(2,1)} %get-tuple-element.161), calls=%async_computation.3 | async-start | bytes 4194304 | tf_op jit(solution)/shard_map/all_to_all | solution.py:922
  186.6 3.5 collective-permute-start.51
  194.2 10.3 %collective-permute-done.51.refs_6_ = bf16[128,512]{1,0:T(8,128)(2,1)S(1)} collective-permute-done((bf16[128,512]{1,0:T(8,128)(2,1)S(1)}, bf16[128,512]{1,0:T(8,128)(2,1)S(1)}, u32[]{:S(2)}, u32[]{:S(2)}) %collective-permute-start.51) | collective-permute-done | bytes 131104 | tf_op jit(solution)/shard_map/ppermute | solution.py:372
  205.2 11.8 %expert_full.2 = (bf16[128,512]{1,0:T(8,128)(2,1)S(1)}, bf16[128,512]{1,0:T(8,128)(2,1)S(1)}, bf16[128,512]{1,0:T(8,128)(2,1)S(1)}, bf16[128,512]{1,0:T(8,128)(2...) custom-call(s32[4]{0:T(128)S(1)} %pad_add_fusion.refs_0_, ...), custom_call_target="tpu_custom_call" | custom-call | flops 1610612736 | bytes 5275664 | tf_op jit(solution)/shard_map/expert_full/pallas_call | solution.py:779
  220.3 4.2 all-to-all-start.4
  229.4 4.0 collective-permute-done.56.refs_2_
  233.4 6.6 %collective-permute-done.57.refs_3_ = bf16[128,512]{1,0:T(8,128)(2,1)} collective-permute-done((bf16[128,512]{1,0:T(8,128)(2,1)S(1)}, bf16[128,512]{1,0:T(8,128)(2,1)}, u32[]{:S(2)}, u32[]{:S(2)}) %collective-permute-start.57) | collective-permute-done | bytes 131104 | tf_op jit(solution)/shard_map/ppermute | solution.py:372
  242.8 3.5 combine.5
  254.6 3.4 collective-permute-start.64
  258.0 4.0 collective-permute-done.64.refs_3_
  264.4 9.5 %attention_backward.2 = (f32[208,512]{1,0:T(8,128)S(1)}, bf16[208,512]{1,0:T(8,128)(2,1)S(1)}, bf16[2,4,576,256]{3,2,1,0:T(8,128)(2,1)S(1)}) custom-call(s32[4]{0:T(128)S(1)} %pad_add_fusion.refs_0_, bf16[512,2048]{1,0:T(8,128)(2,1)} %get-tuple-element.185.refs_1_, f32[4,512]{1,0:T(4,128)} %get-tuple-element.303.refs_9_.refs_2_, ...), custom_call_target="tpu_custom_call" | custom-call | flops 436207616 | bytes 5152784 | tf_op jit(solution)/shard_map/attention_backward/pallas_call | solution.py:779
  280.8 8.0 %collective-permute-done.70.refs_3_ = bf16[208,512]{1,0:T(8,128)(2,1)S(1)} collective-permute-done((bf16[208,512]{1,0:T(8,128)(2,1)S(1)}, bf16[208,512]{1,0:T(8,128)(2,1)S(1)}, u32[]{:S(2)}, u32[]{:S(2)}) %collective-permute-start.70) | collective-permute-done | bytes 213024 | tf_op jit(solution)/shard_map/ppermute | solution.py:372
  288.8 4.5 all-to-all-start.5
  308.9 3.7 widen.4.refs_0_
  312.7 3.5 combine.6
  317.5 10.9 %expert_full.3 = (bf16[128,512]{1,0:T(8,128)(2,1)S(1)}, bf16[128,512]{1,0:T(8,128)(2,1)S(1)}, bf16[128,512]{1,0:T(8,128)(2,1)S(1)}, bf16[128,512]{1,0:T(8,128)(2...) custom-call(s32[4]{0:T(128)S(1)} %pad_add_fusion.refs_0_, ...), custom_call_target="tpu_custom_call" | custom-call | flops 1610612736 | bytes 5275664 | tf_op jit(solution)/shard_map/expert_full/pallas_call | solution.py:779
  333.2 4.3 all-to-all-start.6
  342.0 6.0 %widen.5.refs_0_ = f32[2,8,512,256]{3,2,1,0:T(8,128)} custom-call(bf16[8,512,256]{2,1,0:T(8,128)(2,1)} %all-to-all-done.5.narrow_ref), custom_call_target="tpu_custom_call" | custom-call | tf_op jit(solution)/shard_map/widen/pallas_call | solution.py:688
  348.0 3.9 collective-permute-done.85.refs_3_
  354.7 3.5 combine.7
  359.6 4.6 all-to-all-done.6.narrow_ref
  367.6 5.0 %collective-permute-done.96.refs_13_ = bf16[208,512]{1,0:T(8,128)(2,1)S(1)} collective-permute-done((bf16[208,512]{1,0:T(8,128)(2,1)}, bf16[208,512]{1,0:T(8,128)(2,1)S(1)}, u32[]{:S(2)}, u32[]{:S(2)}) %collective-permute-start.96) | collective-permute-done | bytes 213024 | tf_op jit(solution)/shard_map/ppermute | solution.py:372
  375.5 9.7 %attention_backward.3 = (f32[208,512]{1,0:T(8,128)S(1)}, bf16[208,512]{1,0:T(8,128)(2,1)}, bf16[2,4,576,256]{3,2,1,0:T(8,128)(2,1)S(1)}) custom-call(s32[4]{0:T(128)S(1)} %pad_add_fusion.refs_0_, bf16[512,2048]{1,0:T(8,128)(2,1)} %get-tuple-element.217.refs_1_, f32[4,512]{1,0:T(4,128)} %get-tuple-element.304.refs_9_.refs_2_, ...), custom_call_target="tpu_custom_call" | custom-call | flops 436207616 | bytes 5365776 | tf_op jit(solution)/shard_map/attention_backward/pallas_call | solution.py:779
  387.7 3.2 collective-permute-done.97
  403.1 3.5 widen.6
  424.4 3.7 all-to-all-start.7
  437.2 9.8 %collective-permute-done.110 = bf16[144,512]{1,0:T(8,128)(2,1)S(1)} collective-permute-done((bf16[144,512]{1,0:T(8,128)(2,1)S(1)}, bf16[144,512]{1,0:T(8,128)(2,1)S(1)}, u32[]{:S(2)}, u32[]{:S(2)}) %collective-permute-start.110) | collective-permute-done | bytes 147488 | tf_op jit(solution)/shard_map/ppermute | solution.py:372
  454.8 3.5 widen.7
  (493 shorter events, 192.8 us)
Async XLA Ops:
  6.0 13.4 %collective-permute-start.2 = (bf16[256,512]{1,0:T(8,128)(2,1)S(1)}, bf16[256,512]{1,0:T(8,128)(2,1)S(1)}, u32[]{:S(2)}, u32[]{:S(2)}) collective-permute-start(bf16[256,512]{1,0:T(8,128)(2,1)S(1)} %maximum_maximum_fusion.1.refs_1_), channel_id=1, source_target_pairs={{0,4},{2,6},{4,0},{6,2},{1,5},{3,7},{5,1},{7,3},{8,12},{10,14},{12... | collective-permute-start | bytes 786440 | tf_op jit(solution)/shard_map/ppermute | solution.py:372
  7.5 11.9 %collective-permute-start.3 = (bf16[256,512]{1,0:T(8,128)(2,1)S(1)}, bf16[256,512]{1,0:T(8,128)(2,1)S(1)}, u32[]{:S(2)}, u32[]{:S(2)}) collective-permute-start(bf16[256,512]{1,0:T(8,128)(2,1)S(1)} %maximum_maximum_fusion.1.refs_1_), channel_id=1, source_target_pairs={{0,6},{2,4},{4,2},{6,0},{1,7},{3,5},{5,3},{7,1},{8,14},{10,12},{12... | collective-permute-start | bytes 786440 | tf_op jit(solution)/shard_map/ppermute | solution.py:372
  19.4 40.2 %all-to-all-start = ((bf16[8,256,512]{2,1,0:T(8,128)(2,1)}), bf16[8,256,512]{2,1,0:T(8,128)(2,1)}, u32[]{:S(2)}, u32[]{:S(2)}) async-start(bf16[8,256,512]{2,1,0:T(8,128)(2,1)} %get-tuple-element.140), calls=%async_computation | async-start | bytes 4194304 | tf_op jit(solution)/shard_map/all_to_all | solution.py:922
  34.7 19.9 %collective-permute-start.9 = (bf16[208,512]{1,0:T(8,128)(2,1)S(1)}, bf16[208,512]{1,0:T(8,128)(2,1)S(1)}, u32[]{:S(2)}, u32[]{:S(2)}) collective-permute-start(bf16[208,512]{1,0:T(8,128)(2,1)S(1)} %get-tuple-element.141.refs_1_), channel_id=1, source_target_pairs={{0,2},{2,0},{4,6},{6,4},{1,3},{3,1},{5,7},{7,5},{8,10},{10,8},{12,... | collective-permute-start | bytes 638984 | tf_op jit(solution)/shard_map/ppermute | solution.py:372
  36.5 18.1 %collective-permute-start.10 = (bf16[208,512]{1,0:T(8,128)(2,1)S(1)}, bf16[208,512]{1,0:T(8,128)(2,1)S(1)}, u32[]{:S(2)}, u32[]{:S(2)}) collective-permute-start(bf16[208,512]{1,0:T(8,128)(2,1)S(1)} %get-tuple-element.141.refs_1_), channel_id=1, source_target_pairs={{0,4},{2,6},{4,0},{6,2},{1,5},{3,7},{5,1},{7,3},{8,12},{10,14},{12... | collective-permute-start | bytes 638984 | tf_op jit(solution)/shard_map/ppermute | solution.py:372
  38.0 21.6 %collective-permute-start.11 = (bf16[208,512]{1,0:T(8,128)(2,1)S(1)}, bf16[208,512]{1,0:T(8,128)(2,1)S(1)}, u32[]{:S(2)}, u32[]{:S(2)}) collective-permute-start(bf16[208,512]{1,0:T(8,128)(2,1)S(1)} %get-tuple-element.141.refs_1_), channel_id=1, source_target_pairs={{0,6},{2,4},{4,2},{6,0},{1,7},{3,5},{5,3},{7,1},{8,14},{10,12},{12... | collective-permute-start | bytes 638984 | tf_op jit(solution)/shard_map/ppermute | solution.py:372
  59.6 31.2 %all-to-all-start.1 = ((bf16[8,512,256]{2,1,0:T(8,128)(2,1)}), bf16[8,512,256]{2,1,0:T(8,128)(2,1)}, u32[]{:S(2)}, u32[]{:S(2)}) async-start(bf16[8,512,256]{2,1,0:T(8,128)(2,1)} %get-tuple-element.142), calls=%async_computation.1 | async-start | bytes 4194304 | tf_op jit(solution)/shard_map/all_to_all | solution.py:922
  72.9 12.9 %collective-permute-start.17 = (bf16[128,512]{1,0:T(8,128)(2,1)S(1)}, bf16[128,512]{1,0:T(8,128)(2,1)S(1)}, u32[]{:S(2)}, u32[]{:S(2)}) collective-permute-start(bf16[128,512]{1,0:T(8,128)(2,1)S(1)} %get-tuple-element.145), channel_id=1, source_target_pairs={{0,16},{8,24},{16,0},{24,8},{1,17},{9,25},{17,1},{25,9},{2,18},{10... | collective-permute-start | bytes 393224 | tf_op jit(solution)/shard_map/ppermute | solution.py:372
  96.7 72.4 %all-to-all-start.2 = ((bf16[8,256,512]{2,1,0:T(8,128)(2,1)}), bf16[8,256,512]{2,1,0:T(8,128)(2,1)}, u32[]{:S(2)}, u32[]{:S(2)}) async-start(bf16[8,256,512]{2,1,0:T(8,128)(2,1)} %get-tuple-element.158), calls=%async_computation.2 | async-start | bytes 4194304 | tf_op jit(solution)/shard_map/all_to_all | solution.py:922
  103.3 13.0 %collective-permute-start.27 = (bf16[128,512]{1,0:T(8,128)(2,1)S(1)}, bf16[128,512]{1,0:T(8,128)(2,1)S(1)}, u32[]{:S(2)}, u32[]{:S(2)}) collective-permute-start(bf16[128,512]{1,0:T(8,128)(2,1)S(1)} %get-tuple-element.151), channel_id=1, source_target_pairs={{0,16},{8,24},{16,0},{24,8},{1,17},{9,25},{17,1},{25,9},{2,18},{10... | collective-permute-start | bytes 393224 | tf_op jit(solution)/shard_map/ppermute | solution.py:372
  109.2 23.8 %collective-permute-start.19 = (bf16[256,512]{1,0:T(8,128)(2,1)S(1)}, bf16[256,512]{1,0:T(8,128)(2,1)S(1)}, u32[]{:S(2)}, u32[]{:S(2)}) collective-permute-start(bf16[256,512]{1,0:T(8,128)(2,1)S(1)} %maximum_maximum_fusion.refs_1_), channel_id=1, source_target_pairs={{0,2},{2,0},{4,6},{6,4},{1,3},{3,1},{5,7},{7,5},{8,10},{10,8},{12,... | collective-permute-start | bytes 786440 | tf_op jit(solution)/shard_map/ppermute | solution.py:372
  116.8 17.8 %collective-permute-start.20 = (bf16[256,512]{1,0:T(8,128)(2,1)S(1)}, bf16[256,512]{1,0:T(8,128)(2,1)S(1)}, u32[]{:S(2)}, u32[]{:S(2)}) collective-permute-start(bf16[256,512]{1,0:T(8,128)(2,1)S(1)} %maximum_maximum_fusion.refs_1_), channel_id=1, source_target_pairs={{0,4},{2,6},{4,0},{6,2},{1,5},{3,7},{5,1},{7,3},{8,12},{10,14},{12... | collective-permute-start | bytes 786440 | tf_op jit(solution)/shard_map/ppermute | solution.py:372
  118.7 20.9 %collective-permute-start.21 = (bf16[256,512]{1,0:T(8,128)(2,1)S(1)}, bf16[256,512]{1,0:T(8,128)(2,1)S(1)}, u32[]{:S(2)}, u32[]{:S(2)}) collective-permute-start(bf16[256,512]{1,0:T(8,128)(2,1)S(1)} %maximum_maximum_fusion.refs_1_), channel_id=1, source_target_pairs={{0,6},{2,4},{4,2},{6,0},{1,7},{3,5},{5,3},{7,1},{8,14},{10,12},{12... | collective-permute-start | bytes 786440 | tf_op jit(solution)/shard_map/ppermute | solution.py:372
  126.1 17.2 %collective-permute-start.33 = (bf16[208,512]{1,0:T(8,128)(2,1)S(1)}, bf16[208,512]{1,0:T(8,128)(2,1)S(1)}, u32[]{:S(2)}, u32[]{:S(2)}) collective-permute-start(bf16[208,512]{1,0:T(8,128)(2,1)S(1)} %get-tuple-element.154), channel_id=1, source_target_pairs={{0,2},{2,0},{4,6},{6,4},{1,3},{3,1},{5,7},{7,5},{8,10},{10,8},{12,... | collective-permute-start | bytes 638984 | tf_op jit(solution)/shard_map/ppermute | solution.py:372
  126.2 17.1 %collective-permute-start.34 = (bf16[208,512]{1,0:T(8,128)(2,1)S(1)}, bf16[208,512]{1,0:T(8,128)(2,1)S(1)}, u32[]{:S(2)}, u32[]{:S(2)}) collective-permute-start(bf16[208,512]{1,0:T(8,128)(2,1)S(1)} %get-tuple-element.155), channel_id=1, source_target_pairs={{0,4},{2,6},{4,0},{6,2},{1,5},{3,7},{5,1},{7,3},{8,12},{10,14},{12... | collective-permute-start | bytes 638984 | tf_op jit(solution)/shard_map/ppermute | solution.py:372
  133.0 15.3 %collective-permute-start.35 = (bf16[208,512]{1,0:T(8,128)(2,1)S(1)}, bf16[208,512]{1,0:T(8,128)(2,1)S(1)}, u32[]{:S(2)}, u32[]{:S(2)}) collective-permute-start(bf16[208,512]{1,0:T(8,128)(2,1)S(1)} %get-tuple-element.156), channel_id=1, source_target_pairs={{0,6},{2,4},{4,2},{6,0},{1,7},{3,5},{5,3},{7,1},{8,14},{10,12},{12... | collective-permute-start | bytes 638984 | tf_op jit(solution)/shard_map/ppermute | solution.py:372
  134.5 14.3 %collective-permute-start.22 = (bf16[256,512]{1,0:T(8,128)(2,1)S(1)}, bf16[256,512]{1,0:T(8,128)(2,1)S(1)}, u32[]{:S(2)}, u32[]{:S(2)}) collective-permute-start(bf16[256,512]{1,0:T(8,128)(2,1)S(1)} %maximum_maximum_fusion.refs_1_), channel_id=1, source_target_pairs={{0,1},{1,0},{2,3},{3,2},{4,5},{5,4},{6,7},{7,6},{8,9},{9,8},{10,11... | collective-permute-start | bytes 786440 | tf_op jit(solution)/shard_map/ppermute | solution.py:372
  148.3 11.8 %collective-permute-start.39 = (bf16[208,512]{1,0:T(8,128)(2,1)S(1)}, bf16[208,512]{1,0:T(8,128)(2,1)S(1)}, u32[]{:S(2)}, u32[]{:S(2)}) collective-permute-start(bf16[208,512]{1,0:T(8,128)(2,1)S(1)} %get-tuple-element.160.refs_1_.refs_8_), channel_id=1, source_target_pairs={{0,2},{2,0},{4,6},{6,4},{1,3},{3,1},{5,7},{7,5},{8,10},{10,8},{12,... | collective-permute-start | bytes 638984 | tf_op jit(solution)/shard_map/ppermute | solution.py:372
  148.9 12.8 %collective-permute-start.40 = (bf16[208,512]{1,0:T(8,128)(2,1)S(1)}, bf16[208,512]{1,0:T(8,128)(2,1)S(1)}, u32[]{:S(2)}, u32[]{:S(2)}) collective-permute-start(bf16[208,512]{1,0:T(8,128)(2,1)S(1)} %get-tuple-element.160.refs_1_.refs_8_), channel_id=1, source_target_pairs={{0,4},{2,6},{4,0},{6,2},{1,5},{3,7},{5,1},{7,3},{8,12},{10,14},{12... | collective-permute-start | bytes 638984 | tf_op jit(solution)/shard_map/ppermute | solution.py:372
  149.2 12.4 %collective-permute-start.41 = (bf16[208,512]{1,0:T(8,128)(2,1)S(1)}, bf16[208,512]{1,0:T(8,128)(2,1)S(1)}, u32[]{:S(2)}, u32[]{:S(2)}) collective-permute-start(bf16[208,512]{1,0:T(8,128)(2,1)S(1)} %get-tuple-element.160.refs_1_.refs_8_), channel_id=1, source_target_pairs={{0,6},{2,4},{4,2},{6,0},{1,7},{3,5},{5,3},{7,1},{8,14},{10,12},{12... | collective-permute-start | bytes 638984 | tf_op jit(solution)/shard_map/ppermute | solution.py:372
  169.1 35.4 %all-to-all-start.3 = ((bf16[8,512,256]{2,1,0:T(8,128)(2,1)}), bf16[8,512,256]{2,1,0:T(8,128)(2,1)}, u32[]{:S(2)}, u32[]{:S(2)}) async-start(bf16[8,512,256]{2,1,0:T(8,128)(2,1)} %get-tuple-element.161), calls=%async_computation.3 | async-start | bytes 4194304 | tf_op jit(solution)/shard_map/all_to_all | solution.py:922
  180.3 13.0 %collective-permute-start.54 = (bf16[128,512]{1,0:T(8,128)(2,1)S(1)}, bf16[128,512]{1,0:T(8,128)(2,1)S(1)}, u32[]{:S(2)}, u32[]{:S(2)}) collective-permute-start(bf16[128,512]{1,0:T(8,128)(2,1)S(1)} %get-tuple-element.176), channel_id=1, source_target_pairs={{0,16},{8,24},{16,0},{24,8},{1,17},{9,25},{17,1},{25,9},{2,18},{10... | collective-permute-start | bytes 393224 | tf_op jit(solution)/shard_map/ppermute | solution.py:372
  186.6 17.9 %collective-permute-start.51 = (bf16[128,512]{1,0:T(8,128)(2,1)S(1)}, bf16[128,512]{1,0:T(8,128)(2,1)S(1)}, u32[]{:S(2)}, u32[]{:S(2)}) collective-permute-start(bf16[128,512]{1,0:T(8,128)(2,1)S(1)} %get-tuple-element.173), channel_id=1, source_target_pairs={{0,16},{8,24},{16,0},{24,8},{1,17},{9,25},{17,1},{25,9},{2,18},{10... | collective-permute-start | bytes 393224 | tf_op jit(solution)/shard_map/ppermute | solution.py:372
  190.1 14.4 %collective-permute-start.52 = (bf16[128,512]{1,0:T(8,128)(2,1)S(1)}, bf16[128,512]{1,0:T(8,128)(2,1)S(1)}, u32[]{:S(2)}, u32[]{:S(2)}) collective-permute-start(bf16[128,512]{1,0:T(8,128)(2,1)S(1)} %get-tuple-element.174), channel_id=1, source_target_pairs={{0,24},{8,16},{16,8},{24,0},{1,25},{9,17},{17,9},{25,1},{2,26},{10... | collective-permute-start | bytes 393224 | tf_op jit(solution)/shard_map/ppermute | solution.py:372
  220.3 30.8 %all-to-all-start.4 = ((bf16[8,256,512]{2,1,0:T(8,128)(2,1)}), bf16[8,256,512]{2,1,0:T(8,128)(2,1)S(1)}, u32[]{:S(2)}, u32[]{:S(2)}) async-start(bf16[8,256,512]{2,1,0:T(8,128)(2,1)} %copy-done.5), calls=%async_computation.4 | async-start | bytes 4194304 | tf_op jit(solution)/shard_map/all_to_all | solution.py:922
  226.9 13.0 %collective-permute-start.57 = (bf16[128,512]{1,0:T(8,128)(2,1)S(1)}, bf16[128,512]{1,0:T(8,128)(2,1)}, u32[]{:S(2)}, u32[]{:S(2)}) collective-permute-start(bf16[128,512]{1,0:T(8,128)(2,1)S(1)} %get-tuple-element.181), channel_id=1, source_target_pairs={{0,16},{8,24},{16,0},{24,8},{1,17},{9,25},{17,1},{25,9},{2,18},{10... | collective-permute-start | bytes 393224 | tf_op jit(solution)/shard_map/ppermute | solution.py:372
  228.0 11.9 %collective-permute-start.58 = (bf16[128,512]{1,0:T(8,128)(2,1)S(1)}, bf16[128,512]{1,0:T(8,128)(2,1)}, u32[]{:S(2)}, u32[]{:S(2)}) collective-permute-start(bf16[128,512]{1,0:T(8,128)(2,1)S(1)} %get-tuple-element.182), channel_id=1, source_target_pairs={{0,24},{8,16},{16,8},{24,0},{1,25},{9,17},{17,9},{25,1},{2,26},{10... | collective-permute-start | bytes 393224 | tf_op jit(solution)/shard_map/ppermute | solution.py:372
  229.4 12.0 %collective-permute-start.59 = (bf16[128,512]{1,0:T(8,128)(2,1)S(1)}, bf16[128,512]{1,0:T(8,128)(2,1)}, u32[]{:S(2)}, u32[]{:S(2)}) collective-permute-start(bf16[128,512]{1,0:T(8,128)(2,1)S(1)} %get-tuple-element.179.refs_1_), channel_id=1, source_target_pairs={{0,1},{1,0},{2,3},{3,2},{4,5},{5,4},{6,7},{7,6},{8,9},{9,8},{10,11... | collective-permute-start | bytes 393224 | tf_op jit(solution)/shard_map/ppermute | solution.py:372
  251.1 12.5 %collective-permute-start.68 = (bf16[208,512]{1,0:T(8,128)(2,1)S(1)}, bf16[208,512]{1,0:T(8,128)(2,1)S(1)}, u32[]{:S(2)}, u32[]{:S(2)}) collective-permute-start(bf16[208,512]{1,0:T(8,128)(2,1)S(1)} %get-tuple-element.205), channel_id=1, source_target_pairs={{0,6},{2,4},{4,2},{6,0},{1,7},{3,5},{5,3},{7,1},{8,14},{10,12},{12... | collective-permute-start | bytes 638984 | tf_op jit(solution)/shard_map/ppermute | solution.py:372
  276.5 12.4 %collective-permute-start.70 = (bf16[208,512]{1,0:T(8,128)(2,1)S(1)}, bf16[208,512]{1,0:T(8,128)(2,1)S(1)}, u32[]{:S(2)}, u32[]{:S(2)}) collective-permute-start(bf16[208,512]{1,0:T(8,128)(2,1)S(1)} %get-tuple-element.206.refs_1_), channel_id=1, source_target_pairs={{0,4},{2,6},{4,0},{6,2},{1,5},{3,7},{5,1},{7,3},{8,12},{10,14},{12... | collective-permute-start | bytes 638984 | tf_op jit(solution)/shard_map/ppermute | solution.py:372
  280.7 18.2 %collective-permute-start.80 = (bf16[4,576,256]{2,1,0:T(8,128)(2,1)}, bf16[4,576,256]{2,1,0:T(8,128)(2,1)}, u32[]{:S(2)}, u32[]{:S(2)}) collective-permute-start(bf16[4,576,256]{2,1,0:T(8,128)(2,1)} %dynamic-slice_bitcast_fusion.5), channel_id=1, source_target_pairs={{0,1},{1,0},{2,3},{3,2},{4,5},{5,4},{6,7},{7,6},{8,9},{9,8},{10,11... | collective-permute-start | bytes 3538952 | tf_op jit(solution)/shard_map/ppermute | solution.py:372
  288.8 44.4 %all-to-all-start.5 = ((bf16[8,512,256]{2,1,0:T(8,128)(2,1)}), bf16[8,512,256]{2,1,0:T(8,128)(2,1)}, u32[]{:S(2)}, u32[]{:S(2)}) async-start(bf16[8,512,256]{2,1,0:T(8,128)(2,1)} %copy-done.3), calls=%async_computation.5 | async-start | bytes 4194304 | tf_op jit(solution)/shard_map/all_to_all | solution.py:922
  303.7 28.1 %collective-permute-start.91 = (bf16[576,256]{1,0:T(8,128)(2,1)S(1)}, bf16[576,256]{1,0:T(8,128)(2,1)S(1)}, u32[]{:S(2)}, u32[]{:S(2)}) collective-permute-start(bf16[576,256]{1,0:T(8,128)(2,1)S(1)} %get-tuple-element.288), channel_id=1, source_target_pairs={{0,2},{2,0},{4,6},{6,4},{1,3},{3,1},{5,7},{7,5},{8,10},{10,8},{12,... | collective-permute-start | bytes 884744 | tf_op jit(solution)/shard_map/ppermute | solution.py:372
  305.6 26.2 %collective-permute-start.92 = (bf16[576,256]{1,0:T(8,128)(2,1)S(1)}, bf16[576,256]{1,0:T(8,128)(2,1)S(1)}, u32[]{:S(2)}, u32[]{:S(2)}) collective-permute-start(bf16[576,256]{1,0:T(8,128)(2,1)S(1)} %get-tuple-element.287), channel_id=1, source_target_pairs={{0,4},{2,6},{4,0},{6,2},{1,5},{3,7},{5,1},{7,3},{8,12},{10,14},{12... | collective-permute-start | bytes 884744 | tf_op jit(solution)/shard_map/ppermute | solution.py:372
  307.1 26.1 %collective-permute-start.93 = (bf16[576,256]{1,0:T(8,128)(2,1)S(1)}, bf16[576,256]{1,0:T(8,128)(2,1)}, u32[]{:S(2)}, u32[]{:S(2)}) collective-permute-start(bf16[576,256]{1,0:T(8,128)(2,1)S(1)} %get-tuple-element.286), channel_id=1, source_target_pairs={{0,6},{2,4},{4,2},{6,0},{1,7},{3,5},{5,3},{7,1},{8,14},{10,12},{12... | collective-permute-start | bytes 884744 | tf_op jit(solution)/shard_map/ppermute | solution.py:372
  333.2 30.9 %all-to-all-start.6 = ((bf16[8,256,512]{2,1,0:T(8,128)(2,1)}), bf16[8,256,512]{2,1,0:T(8,128)(2,1)S(1)}, u32[]{:S(2)}, u32[]{:S(2)}) async-start(bf16[8,256,512]{2,1,0:T(8,128)(2,1)} %copy-done.4), calls=%async_computation.6 | async-start | bytes 4194304 | tf_op jit(solution)/shard_map/all_to_all | solution.py:922
  340.4 11.5 %collective-permute-start.84 = (bf16[128,512]{1,0:T(8,128)(2,1)S(1)}, bf16[128,512]{1,0:T(8,128)(2,1)S(1)}, u32[]{:S(2)}, u32[]{:S(2)}) collective-permute-start(bf16[128,512]{1,0:T(8,128)(2,1)S(1)} %get-tuple-element.241), channel_id=1, source_target_pairs={{0,8},{8,0},{16,24},{24,16},{1,9},{9,1},{17,25},{25,17},{2,10},{10... | collective-permute-start | bytes 393224 | tf_op jit(solution)/shard_map/ppermute | solution.py:372
  393.9 14.4 %collective-permute-start.103 = (bf16[576,256]{1,0:T(8,128)(2,1)}, bf16[576,256]{1,0:T(8,128)(2,1)}, u32[]{:S(2)}, u32[]{:S(2)}) collective-permute-start(bf16[576,256]{1,0:T(8,128)(2,1)} %get-tuple-element.282), channel_id=1, source_target_pairs={{0,2},{2,0},{4,6},{6,4},{1,3},{3,1},{5,7},{7,5},{8,10},{10,8},{12,... | collective-permute-start | bytes 884744 | tf_op jit(solution)/shard_map/ppermute | solution.py:372
  395.5 15.4 %collective-permute-start.104 = (bf16[576,256]{1,0:T(8,128)(2,1)}, bf16[576,256]{1,0:T(8,128)(2,1)}, u32[]{:S(2)}, u32[]{:S(2)}) collective-permute-start(bf16[576,256]{1,0:T(8,128)(2,1)} %get-tuple-element.284), channel_id=1, source_target_pairs={{0,4},{2,6},{4,0},{6,2},{1,5},{3,7},{5,1},{7,3},{8,12},{10,14},{12... | collective-permute-start | bytes 884744 | tf_op jit(solution)/shard_map/ppermute | solution.py:372
  397.1 15.2 %collective-permute-start.105 = (bf16[576,256]{1,0:T(8,128)(2,1)}, bf16[576,256]{1,0:T(8,128)(2,1)}, u32[]{:S(2)}, u32[]{:S(2)}) collective-permute-start(bf16[576,256]{1,0:T(8,128)(2,1)} %get-tuple-element.283), channel_id=1, source_target_pairs={{0,6},{2,4},{4,2},{6,0},{1,7},{3,5},{5,3},{7,1},{8,14},{10,12},{12... | collective-permute-start | bytes 884744 | tf_op jit(solution)/shard_map/ppermute | solution.py:372
  402.4 29.8 %collective-permute-start.102 = (f32[197,256]{1,0:T(8,128)}, f32[197,256]{1,0:T(8,128)}, u32[]{:S(2)}, u32[]{:S(2)}) collective-permute-start(f32[197,256]{1,0:T(8,128)} %bitcast.104), channel_id=1, source_target_pairs={{0,1},{1,0},{2,3},{3,2},{4,5},{5,4},{6,7},{7,6},{8,9},{9,8},{10,11... | collective-permute-start | bytes 605192 | tf_op jit(solution)/shard_map/ppermute | solution.py:372
  408.2 11.9 %collective-permute-start.99 = (bf16[208,512]{1,0:T(8,128)(2,1)S(1)}, bf16[208,512]{1,0:T(8,128)(2,1)S(1)}, u32[]{:S(2)}, u32[]{:S(2)}) collective-permute-start(bf16[208,512]{1,0:T(8,128)(2,1)S(1)} %get-tuple-element.260), channel_id=1, source_target_pairs={{0,4},{2,6},{4,0},{6,2},{1,5},{3,7},{5,1},{7,3},{8,12},{10,14},{12... | collective-permute-start | bytes 638984 | tf_op jit(solution)/shard_map/ppermute | solution.py:372
  410.9 12.0 %collective-permute-start.100 = (bf16[208,512]{1,0:T(8,128)(2,1)S(1)}, bf16[208,512]{1,0:T(8,128)(2,1)S(1)}, u32[]{:S(2)}, u32[]{:S(2)}) collective-permute-start(bf16[208,512]{1,0:T(8,128)(2,1)S(1)} %get-tuple-element.261), channel_id=1, source_target_pairs={{0,6},{2,4},{4,2},{6,0},{1,7},{3,5},{5,3},{7,1},{8,14},{10,12},{12... | collective-permute-start | bytes 638984 | tf_op jit(solution)/shard_map/ppermute | solution.py:372
  414.5 13.7 %collective-permute-start.106 = (bf16[144,512]{1,0:T(8,128)(2,1)}, bf16[144,512]{1,0:T(8,128)(2,1)}, u32[]{:S(2)}, u32[]{:S(2)}) collective-permute-start(bf16[144,512]{1,0:T(8,128)(2,1)} %get-tuple-element.290), channel_id=1, source_target_pairs={{0,8},{8,0},{16,24},{24,16},{1,9},{9,1},{17,25},{25,17},{2,10},{10... | collective-permute-start | bytes 442376 | tf_op jit(solution)/shard_map/ppermute | solution.py:372
  414.9 13.3 %collective-permute-start.107 = (bf16[144,512]{1,0:T(8,128)(2,1)}, bf16[144,512]{1,0:T(8,128)(2,1)S(1)}, u32[]{:S(2)}, u32[]{:S(2)}) collective-permute-start(bf16[144,512]{1,0:T(8,128)(2,1)} %get-tuple-element.291), channel_id=1, source_target_pairs={{0,16},{8,24},{16,0},{24,8},{1,17},{9,25},{17,1},{25,9},{2,18},{10... | collective-permute-start | bytes 442376 | tf_op jit(solution)/shard_map/ppermute | solution.py:372
  424.4 30.3 %all-to-all-start.7 = ((bf16[8,512,256]{2,1,0:T(8,128)(2,1)}), bf16[8,512,256]{2,1,0:T(8,128)(2,1)S(1)}, u32[]{:S(2)}, u32[]{:S(2)}) async-start(bf16[8,512,256]{2,1,0:T(8,128)(2,1)} %copy-done.2), calls=%async_computation.7 | async-start | bytes 4194304 | tf_op jit(solution)/shard_map/all_to_all | solution.py:922
  434.8 12.2 %collective-permute-start.110 = (bf16[144,512]{1,0:T(8,128)(2,1)S(1)}, bf16[144,512]{1,0:T(8,128)(2,1)S(1)}, u32[]{:S(2)}, u32[]{:S(2)}) collective-permute-start(bf16[144,512]{1,0:T(8,128)(2,1)S(1)} %get-tuple-element.271), channel_id=1, source_target_pairs={{0,16},{8,24},{16,0},{24,8},{1,17},{9,25},{17,1},{25,9},{2,18},{10... | collective-permute-start | bytes 442376 | tf_op jit(solution)/shard_map/ppermute | solution.py:372
  435.5 11.5 %collective-permute-start.111 = (bf16[144,512]{1,0:T(8,128)(2,1)S(1)}, bf16[144,512]{1,0:T(8,128)(2,1)S(1)}, u32[]{:S(2)}, u32[]{:S(2)}) collective-permute-start(bf16[144,512]{1,0:T(8,128)(2,1)S(1)} %get-tuple-element.271), channel_id=1, source_target_pairs={{0,24},{8,16},{16,8},{24,0},{1,25},{9,17},{17,9},{25,1},{2,26},{10... | collective-permute-start | bytes 442376 | tf_op jit(solution)/shard_map/ppermute | solution.py:372
  (175 other events, 1278.4 us)
